TPU v7x, 256 devices: a whole 4x4x8 slice. The times are simulated.
256 devices in a mesh: seq: 64 (over y_lo, x, z), head: 4 (over y_hi, core).
Axes of the slice: x: 4, y: 4 (y_hi: 2, y_lo: 2; y = y_hi * 2 + y_lo), z: 8, core: 2. Of those that a mesh axis runs over, the one named last changes fastest.
Arguments:
- queries: bfloat16 [8192, 1536], P('seq', 'head'), may hold values from -45 to 45
- keys: bfloat16 [8192, 1536], P('seq', 'head'), may hold values from -4 to 4
- values: bfloat16 [8192, 1536], P('seq', 'head'), may hold values from -6 to 6
- grad_y: bfloat16 [8192, 1536], P('seq', 'head'), may hold values from -384 to 384
- out_weight: bfloat16 [768, 768], P('head'), may hold values from -0.21875 to 0.21875
- counts: int32 [64], replicated, may hold values from 64 to 256, as said below
- offsets: int32 [2, 16], replicated, may hold values from 0 to 15, as said below
Outputs:
- grad_queries: bfloat16 [8192, 1536], P('seq', 'head')
- grad_keys: bfloat16 [8192, 1536], P('seq', 'head')
- grad_values: bfloat16 [8192, 1536], P('seq', 'head')
Inputs may be any that keep to these rules, and one draw needn't show every extreme that they name: The first counts[s] rows of sequence shard s hold tissue, the rest are empty; some shard is full. `offsets`: row 0 lies below 4, row 1 below 16.
All inputs are finite; a program needn't handle non-finite values.
Results may differ from a plain program's by a relative error of at most 0.006.
Values may be sent and summed in bfloat16 or wider, within the bound.
No kernel may reach another device: no remote copies, remote signals or barrier semaphores. Data moves between devices by JAX's collectives and lax.ppermute only.
A program may use at most 64 MiB of HBM per device.

v0:
```python
import jax
import jax.numpy as jnp
from jax import lax
from jax.sharding import PartitionSpec as P

HEAD_SIZE = 48
MID_BITS = 3
MIDDLE_DILATION = 4
TOP_DILATION = 16


def partner(block, axis, distance):
    count = lax.axis_size(axis)
    route = []
    for low in range(count):
        high = low | 1 << distance
        if high != low and high < count:
            route += [(low, high), (high, low)]
    return lax.ppermute(block, axis, route)


def to_tokens(paired):
    half_rows, width = paired.shape
    head_tally = width // (2 * HEAD_SIZE)
    return (
        paired.reshape(half_rows, head_tally, 2, HEAD_SIZE)
        .transpose(0, 2, 1, 3)
        .reshape(2 * half_rows, head_tally * HEAD_SIZE)
    )


def to_pairs(flat):
    row_tally, width = flat.shape
    head_tally = width // HEAD_SIZE
    return (
        flat.reshape(row_tally // 2, 2, head_tally, HEAD_SIZE)
        .transpose(0, 2, 1, 3)
        .reshape(row_tally // 2, 2 * width)
    )


def choose_rows(source_shard, dilation_rate, head_shifts):
    sparse_rows = source_shard.shape[0] // dilation_rate
    reshaped_rows = source_shard.reshape((sparse_rows, dilation_rate) + source_shard.shape[1:])
    pattern = jnp.arange(dilation_rate)[:, None] == head_shifts[None, :]
    pattern = pattern.reshape(
        (1, dilation_rate, head_shifts.shape[0]) + (1,) * (source_shard.ndim - 2)
    )
    return jnp.sum(jnp.where(pattern, reshaped_rows, jnp.zeros((), source_shard.dtype)), axis=1)


def position_rows(compress_rows, dilation_rate, head_shifts, filler):
    sparse_rows = compress_rows.shape[0]
    pattern = jnp.arange(dilation_rate)[:, None] == head_shifts[None, :]
    pattern = pattern.reshape(
        (1, dilation_rate, head_shifts.shape[0]) + (1,) * (compress_rows.ndim - 2)
    )
    expand_rows = jnp.where(
        pattern, compress_rows[:, None], jnp.asarray(filler, compress_rows.dtype)
    )
    return expand_rows.reshape((sparse_rows * dilation_rate,) + compress_rows.shape[1:])


def key_valid(group_tallies, dilation_rate, head_shifts, sparse_rows):
    tile_positions = jnp.arange(sparse_rows)[None, :] * dilation_rate + head_shifts[:, None]
    return (tile_positions[:, None, :] < group_tallies[None, :, None]).reshape(
        head_shifts.shape[0], -1
    )


def to_heads(flat, head_tally):
    return flat.reshape(flat.shape[0], head_tally, HEAD_SIZE).transpose(1, 0, 2)


def attention_forward(sparse_query, key_per_head, value_per_head, valid_keys):
    head_tally, query_tally = (sparse_query.shape[0], sparse_query.shape[1])
    score_scale = HEAD_SIZE ** (-0.5)
    query_stride = min(query_tally, 512)
    head_step = max(1, min(head_tally, 512 // query_tally))
    row_maxima, exponent_sums, level_outputs = ([], [], [])
    for head_begin in range(0, head_tally, head_step):
        head_finish = head_begin + head_step
        key_block = key_per_head[head_begin:head_finish]
        value_block = value_per_head[head_begin:head_finish]
        live_block = valid_keys[head_begin:head_finish]
        part_tops, part_sums, part_outs = ([], [], [])
        query_tile_block = sparse_query[head_begin:head_finish, 0:query_stride]
        logit_scores = (
            jnp.einsum(
                "hqd,hkd->hqk", query_tile_block, key_block, preferred_element_type=jnp.float32
            )
            * score_scale
        )
        logit_scores = jnp.where(live_block[:, None, :], logit_scores, -jnp.inf)
        row_maximum = jnp.max(logit_scores, axis=-1)
        expo_vals = jnp.exp(logit_scores - row_maximum[..., None])
        part_tops.append(row_maximum)
        part_sums.append(jnp.sum(expo_vals, axis=-1))
        part_outs.append(
            jnp.einsum(
                "hqk,hkd->hqd",
                expo_vals.astype(jnp.bfloat16),
                value_block,
                preferred_element_type=jnp.float32,
            )
        )
        row_maxima.append(part_tops[0])
        exponent_sums.append(part_sums[0])
        level_outputs.append(part_outs[0])
    return (
        jnp.concatenate(row_maxima, axis=0),
        jnp.concatenate(exponent_sums, axis=0),
        jnp.concatenate(level_outputs, axis=0),
    )


def attention_backward(
    sparse_query,
    sparse_gradient,
    sparse_logsum,
    sparse_product,
    key_per_head,
    value_per_head,
    valid_keys,
):
    head_tally, query_tally = (sparse_query.shape[0], sparse_query.shape[1])
    key_count = key_per_head.shape[1]
    score_scale = HEAD_SIZE ** (-0.5)
    query_stride = min(query_tally, 512)
    head_step = max(1, min(head_tally, 512 // query_tally))
    query_parts, key_parts, value_parts = ([], [], [])
    for head_begin in range(0, head_tally, head_step):
        head_finish = head_begin + head_step
        key_block = key_per_head[head_begin:head_finish]
        value_block = value_per_head[head_begin:head_finish]
        live_block = valid_keys[head_begin:head_finish]
        query_tile_block = sparse_query[head_begin:head_finish, 0:query_stride]
        block_gradient = sparse_gradient[head_begin:head_finish, 0:query_stride]
        logit_scores = (
            jnp.einsum(
                "hqd,hkd->hqk", query_tile_block, key_block, preferred_element_type=jnp.float32
            )
            * score_scale
        )
        attention_weight = jnp.where(
            live_block[:, None, :],
            jnp.exp(logit_scores - sparse_logsum[head_begin:head_finish, 0:query_stride, None]),
            0.0,
        )
        weight_gradient = jnp.einsum(
            "hqd,hkd->hqk", block_gradient, value_block, preferred_element_type=jnp.float32
        )
        grad_score = (
            attention_weight
            * (weight_gradient - sparse_product[head_begin:head_finish, 0:query_stride, None])
        ).astype(jnp.bfloat16)
        query_lines = (
            jnp.einsum("hqk,hkd->hqd", grad_score, key_block, preferred_element_type=jnp.float32)
            * score_scale
        )
        key_sum = jnp.einsum(
            "hqk,hqd->khd", grad_score, query_tile_block, preferred_element_type=jnp.float32
        )
        value_sum = jnp.einsum(
            "hqk,hqd->khd",
            attention_weight.astype(jnp.bfloat16),
            block_gradient,
            preferred_element_type=jnp.float32,
        )
        query_parts.append(query_lines)
        key_parts.append(key_sum * score_scale)
        value_parts.append(value_sum)
    query_gradient = jnp.concatenate(query_parts, axis=0)
    key_gradient = jnp.concatenate(key_parts, axis=1).reshape(key_count, head_tally * HEAD_SIZE)
    value_gradient = jnp.concatenate(value_parts, axis=1).reshape(key_count, head_tally * HEAD_SIZE)
    return (query_gradient, jnp.stack([key_gradient, value_gradient]))


def collect_group(local_pair, sequence_index):
    gathered = local_pair
    for bit_pos in range(MID_BITS):
        peer_shard = partner(gathered, "seq", bit_pos)
        is_upper = sequence_index // 2**bit_pos % 2 == 1
        gathered = jnp.where(
            is_upper,
            jnp.concatenate([peer_shard, gathered], axis=1),
            jnp.concatenate([gathered, peer_shard], axis=1),
        )
    return gathered


def reduce_group(key_parts, sequence_index):
    for bit_pos in reversed(range(MID_BITS)):
        half_rows = key_parts.shape[1] // 2
        is_upper = sequence_index // 2**bit_pos % 2 == 1
        kept_half = jnp.where(is_upper, key_parts[:, half_rows:], key_parts[:, :half_rows])
        sent_half = jnp.where(is_upper, key_parts[:, :half_rows], key_parts[:, half_rows:])
        key_parts = kept_half + partner(sent_half.astype(jnp.bfloat16), "seq", bit_pos).astype(
            sent_half.dtype
        )
    return key_parts


def reduce_pair(key_parts, is_upper):
    half_rows = key_parts.shape[1] // 2
    kept_half = jnp.where(is_upper, key_parts[:, half_rows:], key_parts[:, :half_rows])
    sent_half = jnp.where(is_upper, key_parts[:, :half_rows], key_parts[:, half_rows:])
    return kept_half + partner(sent_half, "seq", 0)


def per_device(queries, keys, values, grad_y, out_weight, counts, offsets):
    row_tally = 2 * queries.shape[0]
    column_total = queries.shape[1] // 2
    head_tally = column_total // HEAD_SIZE
    sequence_index = lax.axis_index("seq")
    head_index = lax.axis_index("head")
    level_shifts = lax.dynamic_slice(offsets, (0, head_index * head_tally), (2, head_tally))
    zero_shifts = jnp.zeros((head_tally,), jnp.int32)
    my_count = lax.dynamic_index_in_dim(counts, sequence_index, 0, keepdims=False)
    tissue = jnp.arange(row_tally) < my_count
    pair_bit = sequence_index % 2
    pair_counts = lax.dynamic_slice(counts, (sequence_index - pair_bit,), (2,))
    mid_group = 2**MID_BITS
    middle_tallies = lax.dynamic_slice(
        counts, (sequence_index - sequence_index % mid_group,), (mid_group,)
    )
    level_list = (
        (1, zero_shifts),
        (MIDDLE_DILATION, level_shifts[0]),
        (TOP_DILATION, level_shifts[1]),
    )
    query_lines = to_tokens(queries).reshape(row_tally, head_tally, HEAD_SIZE)
    key_lines = to_tokens(keys).reshape(row_tally, head_tally, HEAD_SIZE)
    value_lines = to_tokens(values).reshape(row_tally, head_tally, HEAD_SIZE)
    sparse_query_rows = []
    sparse_pairings = []
    for dilation_rate, head_shifts in level_list:
        sparse_rows = row_tally // dilation_rate
        sparse_query_rows.append(choose_rows(query_lines, dilation_rate, head_shifts))
        sparse_pairings.append(
            jnp.stack(
                [
                    choose_rows(key_lines, dilation_rate, head_shifts).reshape(
                        sparse_rows, column_total
                    ),
                    choose_rows(value_lines, dilation_rate, head_shifts).reshape(
                        sparse_rows, column_total
                    ),
                ]
            )
        )
    peer_shard = partner(sparse_pairings[0], "seq", 0)
    pair_whole = jnp.where(
        pair_bit == 1,
        jnp.concatenate([peer_shard, sparse_pairings[0]], axis=1),
        jnp.concatenate([sparse_pairings[0], peer_shard], axis=1),
    )
    middle_entire = collect_group(sparse_pairings[1], sequence_index)
    top_entire = lax.all_gather(sparse_pairings[2], "seq", axis=1, tiled=True)
    groups = (pair_whole, middle_entire, top_entire)
    lives = (
        key_valid(pair_counts, 1, zero_shifts, row_tally),
        key_valid(middle_tallies, MIDDLE_DILATION, level_shifts[0], row_tally // MIDDLE_DILATION),
        key_valid(counts, TOP_DILATION, level_shifts[1], row_tally // TOP_DILATION),
    )
    key_per_head = [to_heads(group[0], head_tally) for group in groups]
    value_per_head = [to_heads(group[1], head_tally) for group in groups]
    row_maxima, exponent_sums, level_outputs = ([], [], [])
    for level_number in range(3):
        dilation_rate, head_shifts = level_list[level_number]
        row_maximum, exponent_sum, level_output = attention_forward(
            sparse_query_rows[level_number].transpose(1, 0, 2),
            key_per_head[level_number],
            value_per_head[level_number],
            lives[level_number],
        )
        row_maxima.append(position_rows(row_maximum.T, dilation_rate, head_shifts, -jnp.inf))
        exponent_sums.append(position_rows(exponent_sum.T, dilation_rate, head_shifts, 0.0))
        level_outputs.append(
            position_rows(level_output.transpose(1, 0, 2), dilation_rate, head_shifts, 0.0)
        )
    greatest = jnp.maximum(jnp.maximum(row_maxima[0], row_maxima[1]), row_maxima[2])
    scales = [jnp.exp(row_maximum - greatest) for row_maximum in row_maxima]
    norm_sum = (
        exponent_sums[0] * scales[0] + exponent_sums[1] * scales[1] + exponent_sums[2] * scales[2]
    )
    attended = (
        level_outputs[0] * scales[0][..., None]
        + level_outputs[1] * scales[1][..., None]
        + level_outputs[2] * scales[2][..., None]
    ) / norm_sum[..., None]
    logsum_total = greatest + jnp.log(norm_sum)
    model_width = out_weight.shape[1]
    all_heads = model_width // HEAD_SIZE
    weight_grid = out_weight.T.reshape(all_heads, HEAD_SIZE, head_tally, HEAD_SIZE)
    pair_eye = jnp.eye(2, dtype=out_weight.dtype)
    pair_weight = jnp.einsum("adbe,tu->atdbue", weight_grid, pair_eye).reshape(
        2 * model_width, 2 * column_total
    )
    paired_grad = jnp.dot(
        lax.all_gather(grad_y, "head", axis=1, tiled=True),
        pair_weight,
        preferred_element_type=jnp.float32,
    )
    attend_grad = to_tokens(paired_grad)
    row_gradient = attend_grad.astype(jnp.bfloat16) * tissue[:, None].astype(jnp.bfloat16)
    row_gradient = row_gradient.reshape(row_tally, head_tally, HEAD_SIZE)
    product_gradient = jnp.sum(row_gradient.astype(jnp.float32) * attended, axis=-1)
    query_gradient = jnp.zeros((row_tally, head_tally, HEAD_SIZE), jnp.float32)
    key_gradient = jnp.zeros((row_tally, head_tally, HEAD_SIZE), jnp.float32)
    value_gradient = jnp.zeros((row_tally, head_tally, HEAD_SIZE), jnp.float32)
    for level_number in range(3):
        dilation_rate, head_shifts = level_list[level_number]
        sparse_rows = row_tally // dilation_rate
        sparse_gradient = choose_rows(row_gradient, dilation_rate, head_shifts)
        sparse_logsum = choose_rows(logsum_total, dilation_rate, head_shifts)
        sparse_product = choose_rows(product_gradient, dilation_rate, head_shifts)
        if level_number < 2:
            query_part, key_parts = attention_backward(
                sparse_query_rows[level_number].transpose(1, 0, 2),
                sparse_gradient.transpose(1, 0, 2),
                sparse_logsum.T,
                sparse_product.T,
                key_per_head[level_number],
                value_per_head[level_number],
                lives[level_number],
            )
            if level_number == 0:
                local_pieces = reduce_pair(key_parts, pair_bit == 1)
            else:
                local_pieces = reduce_group(key_parts, sequence_index)
        else:
            query_part, key_parts = attention_backward(
                sparse_query_rows[level_number].transpose(1, 0, 2),
                sparse_gradient.transpose(1, 0, 2),
                sparse_logsum.T,
                sparse_product.T,
                key_per_head[level_number],
                value_per_head[level_number],
                lives[level_number],
            )
            local_pieces = lax.psum_scatter(key_parts, "seq", scatter_dimension=1, tiled=True)
        query_gradient = query_gradient + position_rows(
            query_part.transpose(1, 0, 2), dilation_rate, head_shifts, 0.0
        )
        reshaped_rows = local_pieces.reshape(2, sparse_rows, head_tally, HEAD_SIZE)
        key_gradient = key_gradient + position_rows(
            reshaped_rows[0], dilation_rate, head_shifts, 0.0
        )
        value_gradient = value_gradient + position_rows(
            reshaped_rows[1], dilation_rate, head_shifts, 0.0
        )
    return (
        to_pairs(query_gradient.reshape(row_tally, column_total).astype(jnp.bfloat16)),
        to_pairs(key_gradient.reshape(row_tally, column_total).astype(jnp.bfloat16)),
        to_pairs(value_gradient.reshape(row_tally, column_total).astype(jnp.bfloat16)),
    )


def solution(mesh):
    return jax.shard_map(
        per_device,
        mesh=mesh,
        in_specs=(
            P("seq", "head"),
            P("seq", "head"),
            P("seq", "head"),
            P("seq", "head"),
            P("head", None),
            P(),
            P(),
        ),
        out_specs=(P("seq", "head"), P("seq", "head"), P("seq", "head")),
        check_vma=False,
    )
```

profile of v0, /device:TPU:2, one launch (start us, length us, event | category | flops | bytes accessed | tf_op | source)
XLA Modules:
  0.0 906.6 jit_solution(6668647098596701567)
XLA Ops:
  7.2 1.1 copy.321
  9.4 1.0 copy.323
  11.4 1.9 collective-permute-start
  15.0 0.9 reshape.679
  16.0 1.5 copy.344
  17.5 3.9 multiply_bitcast_fusion
  21.4 3.0 reshape.680
  24.4 8.3 all_gather.7
  32.7 1.3 dynamic_slice.16
  34.7 1.8 convolution_convert_fusion
  36.5 0.8 select_reduce_fusion.5
  40.6 148.5 %all_gather.6 = bf16[2,1024,192]{2,0,1:T(2,128)(2,1)S(1)} all-gather(bf16[2,16,192]{2,0,1:T(2,128)(2,1)S(1)} %copy.342), channel_id=1, replica_groups=mesh['seq'=64,'head'=4] {'seq'}, dimensions={1}, use_global_device_ids=true | all-gather | bytes 798720 | tf_op jit(solution)/shard_map/all_gather | solution.py:259
  189.1 1.5 fusion.107
  199.7 1.0 reduce_sum.300
  202.1 1.1 maximum_select_fusion.3
  203.3 1.3 compare_convert_fusion.1
  204.6 5.7 collective-permute-done.2
  210.5 1.4 maximum_select_fusion
  212.7 1.3 bitcast_reduce_fusion.1
  214.0 1.3 fusion.15
  215.3 0.8 reshape.684
  218.3 0.8 reshape.683
  220.4 1.1 copy.350
  221.5 0.9 copy.353
  222.4 1.2 maximum_select_fusion.1
  224.9 2.2 fusion.57
  227.0 1.0 select_n.445
  228.0 1.6 select_n.427
  229.6 1.0 select_n.444
  230.6 1.6 select_n.419
  232.3 2.1 select_reduce_fusion.8
  234.3 0.8 select_n.429
  235.2 0.8 select_n.425
  236.0 1.3 add_bitcast_fusion
  238.1 1.6 copy.363
  240.5 1.6 copy.361
  242.8 1.6 copy.357
  244.4 1.6 convolution_bitcast_fusion.2
  246.0 1.6 copy.354
  247.6 1.0 broadcast_in_dim.499
  249.6 1.2 multiply_reduce_fusion
  251.0 1.3 select_reduce_fusion.10
  252.3 1.4 reduce_sum.309
  253.7 1.9 fusion.58
  255.6 1.4 reduce_sum.310
  257.1 0.9 fusion.7
  258.0 1.2 convolution_multiply_fusion.2
  259.2 1.9 fusion.11
  262.6 1.0 convolution_bitcast_fusion
  263.6 1.4 fusion.2
  265.3 0.8 convolution_multiply_fusion.9
  267.3 0.8 convolution_multiply_fusion.10
  268.6 0.9 broadcast_select_fusion
  269.5 2.4 copy.397
  271.9 1.9 copy.396
  273.8 5.0 pad_maximum_fusion
  280.7 6.0 collective-permute-start.5
  286.9 3.5 collective-permute-done.5
  290.8 5.5 collective-permute-done.6
  296.4 3.2 collective-permute-start.7
  300.5 1.8 collective-permute-done.7
  303.1 1.2 select_add_fusion
  305.3 590.6 %all-reduce.3.cloned.1.call-done = f32[2,1024,192]{2,0,1:T(2,128)} async-done(((f32[2,1024,192]{2,0,1:T(2,128)}), f32[2,1024,192]{2,0,1:T(2,128)}) %all-reduce.3.cloned.1.call-update) | async-done | bytes 1572880
  895.9 0.9 dynamic-slice_reduce_fusion
  (294 shorter events, 37.7 us)
Async XLA Ops:
  7.2 6.3 copy-start
  7.2 6.2 copy-start.33
  7.2 7.8 copy-start.22
  7.2 888.7 %all-reduce.3.cloned.1.call-start = ((), (), s32[]{:S(2)}) async-start(), calls=%async_computation | async-start | bytes 4194304
  11.4 199.0 %collective-permute-start = (bf16[2,256,192]{2,1,0:T(8,128)(2,1)}, bf16[2,256,192]{2,1,0:T(8,128)(2,1)}, u32[]{:S(2)}, u32[]{:S(2)}) collective-permute-start(bf16[2,256,192]{2,1,0:T(8,128)(2,1)} %constant_dynamic-update-slice_fusion), channel_id=1, source_target_pairs={{0,4},{4,0},{8,12},{12,8},{16,20},{20,16},{24,28},{28,24},{32,36},... | collective-permute-start | bytes 589832 | tf_op jit(solution)/shard_map/ppermute | solution.py:19
  13.6 1.1 copy-start.55
  14.4 22.1 %copy-start.37 = (pred[128,2,4]{0,1,2:T(4,128)(4,1)}, pred[128,2,4]{0,1,2:T(4,128)(4,1)S(1)}, u32[]{:S(2)}) copy-start(pred[128,2,4]{0,1,2:T(4,128)(4,1)S(1)} %copy.329) | copy-start | bytes 3076
  15.0 21.5 %copy-start.39 = (pred[128,2,4]{0,1,2:T(4,128)(4,1)}, pred[128,2,4]{0,1,2:T(4,128)(4,1)S(1)}, u32[]{:S(2)}) copy-start(pred[128,2,4]{0,1,2:T(4,128)(4,1)S(1)} %copy.336) | copy-start | bytes 3076
  21.4 3.0 copy-start.34
  24.4 15.0 %copy-start.60 = (s32[64]{0:T(128)S(1)}, s32[64]{0:T(128)}, u32[]{:S(2)}) copy-start(s32[64]{0:T(128)} %param.12) | copy-start | bytes 772
  24.4 15.1 %copy-start.57 = (s32[4]{0:T(128)S(1)}, s32[4]{0:T(128)}, u32[]{:S(2)}) copy-start(s32[4]{0:T(128)} %copy-done.56) | copy-start | bytes 52
  34.7 5.3 copy-start.58
  36.5 161.4 %copy-start.7 = (bf16[384,128]{1,0:T(8,128)(2,1)}, bf16[384,128]{1,0:T(8,128)(2,1)S(1)}, u32[]{:S(2)}) copy-start(bf16[384,128]{1,0:T(8,128)(2,1)S(1)} %convolution_convert_fusion) | copy-start | bytes 294916
  39.2 162.8 %collective-permute-start.1 = (bf16[2,64,192]{1,2,0:T(8,128)(2,1)}, bf16[2,64,192]{1,2,0:T(8,128)(2,1)}, u32[]{:S(2)}, u32[]{:S(2)}) collective-permute-start(bf16[2,64,192]{1,2,0:T(8,128)(2,1)} %pad_maximum_fusion.5), channel_id=1, source_target_pairs={{0,4},{4,0},{8,12},{12,8},{16,20},{20,16},{24,28},{28,24},{32,36},... | collective-permute-start | bytes 147464 | tf_op jit(solution)/shard_map/ppermute | solution.py:19
  191.2 3.1 copy-start.1
  191.2 2.1 copy-start.27
  191.5 3.6 copy-start.29
  191.5 2.9 copy-start.36
  191.9 5.5 copy-start.26
  192.8 6.8 copy-start.25
  193.0 4.5 copy-start.42
  193.0 7.7 copy-start.61
  195.1 16.9 %copy-start.46 = (pred[1,2,2,256]{3,1,2,0:T(4,128)(4,1)}, pred[1,2,2,256]{3,1,2,0:T(4,128)(4,1)S(1)}, u32[]{:S(2)}) copy-start(pred[1,2,2,256]{3,1,2,0:T(4,128)(4,1)S(1)} %copy.425) | copy-start | bytes 3076
  195.2 16.8 %copy-start.17 = (bf16[256,4,48]{0,2,1:T(8,128)(2,1)}, bf16[256,4,48]{0,2,1:T(8,128)(2,1)S(1)}, u32[]{:S(2)}) copy-start(bf16[256,4,48]{0,2,1:T(8,128)(2,1)S(1)} %copy.328) | copy-start | bytes 294916
  197.9 25.8 %copy-start.11 = (bf16[64,4,48]{2,0,1:T(8,128)(2,1)}, bf16[64,4,48]{2,0,1:T(8,128)(2,1)S(1)}, u32[]{:S(2)}) copy-start(bf16[64,4,48]{2,0,1:T(8,128)(2,1)S(1)} %reduce_sum.275) | copy-start | bytes 73732
  203.2 7.1 collective-permute-start.2
  210.3 12.1 %collective-permute-start.3 = (bf16[2,256,192]{1,2,0:T(8,128)(2,1)S(1)}, bf16[2,256,192]{1,2,0:T(8,128)(2,1)}, u32[]{:S(2)}, u32[]{:S(2)}) collective-permute-start(bf16[2,256,192]{1,2,0:T(8,128)(2,1)S(1)} %maximum_select_fusion.2), channel_id=1, source_target_pairs={{0,16},{16,0},{4,20},{20,4},{8,24},{24,8},{12,28},{28,12},{32,48},... | collective-permute-start | bytes 589832 | tf_op jit(solution)/shard_map/ppermute | solution.py:19
  212.7 5.6 copy-start.49
  212.7 4.3 copy-start.47
  214.0 4.3 copy-start.50
  214.0 3.6 copy-start.44
  215.3 4.4 copy-start.51
  215.3 4.4 copy-start.52
  216.9 2.8 copy-start.23
  222.4 2.4 copy-start.14
  222.4 2.4 copy-start.15
  222.4 2.4 copy-start.32
  223.6 22.4 %copy-start.3 = (bf16[1,512,192]{1,2,0:T(8,128)(2,1)}, bf16[1,512,192]{1,2,0:T(8,128)(2,1)S(1)}, u32[]{:S(2)}) copy-start(bf16[1,512,192]{1,2,0:T(8,128)(2,1)S(1)} %get-tuple-element.47) | copy-start | bytes 589828
  224.6 2.4 copy-start.41
  249.4 7.7 copy-start.28
  249.4 8.6 copy-start.30
  251.0 11.6 %copy-start.8 = (bf16[256,4,48]{0,2,1:T(8,128)(2,1)S(1)}, bf16[256,4,48]{0,2,1:T(8,128)(2,1)}, u32[]{:S(2)}) copy-start(bf16[256,4,48]{0,2,1:T(8,128)(2,1)} %copy.346) | copy-start | bytes 294916
  252.3 10.2 %copy-start.48 = (pred[1,2,2,256]{3,1,2,0:T(4,128)(4,1)S(1)}, pred[1,2,2,256]{3,1,2,0:T(4,128)(4,1)}, u32[]{:S(2)}) copy-start(pred[1,2,2,256]{3,1,2,0:T(4,128)(4,1)} %copy-done.46) | copy-start | bytes 3076
  258.0 5.6 copy-start.54
  259.2 5.8 copy-start.18
  262.5 2.8 copy-start.10
  262.6 3.6 copy-start.45
  263.6 2.9 copy-start.16
  265.0 1.6 copy-start.24
  265.3 1.7 copy-start.19
  268.4 3.5 copy-start.2
  269.5 33.6 %collective-permute-start.4 = (f32[2,256,192]{2,1,0:T(8,128)}, f32[2,256,192]{2,1,0:T(8,128)}, u32[]{:S(2)}, u32[]{:S(2)}) collective-permute-start(f32[2,256,192]{2,1,0:T(8,128)} %broadcast_select_fusion), channel_id=1, source_target_pairs={{0,4},{4,0},{8,12},{12,8},{16,20},{20,16},{24,28},{28,24},{32,36},... | collective-permute-start | bytes 1179656 | tf_op jit(solution)/shard_map/ppermute | solution.py:19
  278.8 0.9 copy-start.43
  278.9 1.2 copy-start.4
  278.9 1.5 copy-start.12
  278.9 7.8 copy-start.6
  280.4 10.4 %copy-start.31 = (f32[16,4,48]{2,0,1:T(8,128)S(1)}, f32[16,4,48]{2,0,1:T(8,128)}, u32[]{:S(2)}) copy-start(f32[16,4,48]{2,0,1:T(8,128)} %fusion.11) | copy-start | bytes 36868
  280.6 19.1 %copy-start.20 = (f32[2,256,48]{1,2,0:T(8,128)S(1)}, f32[2,256,48]{1,2,0:T(8,128)}, u32[]{:S(2)}) copy-start(f32[2,256,48]{1,2,0:T(8,128)} %convolution_multiply_fusion.9) | copy-start | bytes 294916
  280.6 19.1 %copy-start.21 = (f32[2,256,48]{1,2,0:T(8,128)S(1)}, f32[2,256,48]{1,2,0:T(8,128)}, u32[]{:S(2)}) copy-start(f32[2,256,48]{1,2,0:T(8,128)} %convolution_multiply_fusion.10) | copy-start | bytes 294916
  280.7 9.7 %collective-permute-start.5 = (bf16[2,256,192]{1,2,0:T(8,128)(2,1)S(1)}, bf16[2,256,192]{1,2,0:T(8,128)(2,1)S(1)}, u32[]{:S(2)}, u32[]{:S(2)}) collective-permute-start(bf16[2,256,192]{1,2,0:T(8,128)(2,1)S(1)} %select_convert_fusion), channel_id=1, source_target_pairs={{0,16},{16,0},{4,20},{20,4},{8,24},{24,8},{12,28},{28,12},{32,48},... | collective-permute-start | bytes 589832 | tf_op jit(solution)/shard_map/ppermute | solution.py:19
  290.5 5.8 collective-permute-start.6
  296.4 5.8 collective-permute-start.7
  304.6 592.7 %copy-start.38 = (pred[128,2,4]{0,1,2:T(4,128)(4,1)S(1)}, pred[128,2,4]{0,1,2:T(4,128)(4,1)}, u32[]{:S(2)}) copy-start(pred[128,2,4]{0,1,2:T(4,128)(4,1)} %copy-done.37) | copy-start | bytes 3076
  304.6 592.7 %copy-start.40 = (pred[128,2,4]{0,1,2:T(4,128)(4,1)S(1)}, pred[128,2,4]{0,1,2:T(4,128)(4,1)}, u32[]{:S(2)}) copy-start(pred[128,2,4]{0,1,2:T(4,128)(4,1)} %copy-done.39) | copy-start | bytes 3076
  (7 other events, 4.8 us)
Sparse Core Ops, SparseCore 0:
  279.0 616.8 all-reduce.2
where the time goes:
time: 917 us; the launch traced here: 907 us
  waiting for transfers between devices  607 us (66%)
  blocking collectives  157 us (17%)
  local copies, waits for them, and re-layouts  61.3 us (7%)
  other arithmetic  34.2 us (4%)
  matrix products  19.3 us (2%)
  between operations  16.1 us (2%)
  starting transfers between devices  11.8 us (1%)
    unnamed x2, waiting for transfers between devices  591 us
    all_gather x1, blocking collectives, per_device(): top_entire = lax.all_gather(sparse_pairings[2], 'seq', axis=1, tiled=True)  149 us
  transfers between devices with their start and end apart: 9, of which 5 were waited for; matrix products, arithmetic and copies ran while one was open for 6% of the time, Pallas kernels for 0%

commit v1 on v0

v1 whole, which is shorter than its diff:
```python
import math

import jax
import jax.numpy as jnp
from jax import lax
from jax.experimental import pallas as pl
from jax.experimental.pallas import tpu as pltpu
from jax.sharding import PartitionSpec as P

HEAD = 48
HEADS = 4
TOKENS = 256
HALF = TOKENS // 2
FEAT = HEADS * HEAD
LANES = 256
MID = 4
TOP = 16
GROUP = 8
ROWS1 = TOKENS // MID
ROWS2 = TOKENS // TOP
SCALE = HEAD**-0.5
ROOT = math.sqrt(HEAD)
EXP2 = SCALE * math.log2(math.e)
BIG = 1e30
BF = jnp.bfloat16
F32 = jnp.float32

VMEM = pl.BlockSpec(memory_space=pltpu.VMEM)
SMEM = pl.BlockSpec(memory_space=pltpu.SMEM)


def iota(shape, dim):
    return lax.broadcasted_iota(jnp.int32, shape, dim)


def nt(a, b):
    return lax.dot_general(a, b, (((1,), (1,)), ((), ())), preferred_element_type=F32)


def nn(a, b):
    return jnp.dot(a, b, preferred_element_type=F32)


def head_mask(h, shape):
    lane = iota(shape, 1)
    return ((lane >= HEAD * h) & (lane < HEAD * (h + 1))) | ((lane >= FEAT + 8 * h) & (lane < FEAT + 8 * h + 8))


def helper_lane(shape):
    lane = iota(shape, 1)
    return jnp.where((lane >= FEAT) & (lane < FEAT + 8 * HEADS), (lane - FEAT) & 7, 8)


def pair_matrix():
    row = iota((2 * FEAT, 2 * LANES), 0)
    col = iota((2 * FEAT, 2 * LANES), 1)
    parity = (col >= LANES).astype(jnp.int32)
    at = col - LANES * parity
    h = (at >= HEAD).astype(jnp.int32) + (at >= 2 * HEAD).astype(jnp.int32) + (at >= 3 * HEAD).astype(jnp.int32)
    hit = (row == at + HEAD * (h + parity)) & (at < FEAT)
    return jnp.where(hit, 1.0, 0.0).astype(BF)


def unpair_matrix():
    row = iota((2 * LANES, 2 * FEAT), 0)
    col = iota((2 * LANES, 2 * FEAT), 1)
    parity = (row >= LANES).astype(jnp.int32)
    at = row - LANES * parity
    h = (at >= HEAD).astype(jnp.int32) + (at >= 2 * HEAD).astype(jnp.int32) + (at >= 3 * HEAD).astype(jnp.int32)
    hit = (col == at + HEAD * (h + parity)) & (at < FEAT)
    return jnp.where(hit, 1.0, 0.0).astype(BF)


def by_parity(paired, matrix):
    both = nn(paired, matrix)
    return jnp.concatenate([both[:, :LANES], both[:, LANES:]], axis=0)


def to_paired(flat, matrix):
    wide = jnp.concatenate([flat[:HALF], flat[HALF:]], axis=1)
    return nn(wide, matrix).astype(BF)


def chosen(offsets, level, h, shape, dim):
    rate = MID if level == 0 else TOP
    place = rate * iota(shape, dim) + offsets[level, h]
    return ((place >> 1) + (place & 1) * HALF) == iota(shape, 1 - dim)


def select_stack(offsets, level):
    rows = ROWS1 if level == 0 else ROWS2
    return jnp.concatenate(
        [jnp.where(chosen(offsets, level, h, (rows, TOKENS), 0), 1.0, 0.0) for h in range(HEADS)], axis=0
    ).astype(BF)


def masked_stack(stack, rows):
    return jnp.concatenate(
        [jnp.where(head_mask(h, (rows, LANES)), stack[h * rows : (h + 1) * rows], 0.0) for h in range(HEADS)], axis=0
    )


def folded(stack, rows):
    total = stack[:rows]
    for h in range(1, HEADS):
        total = total + stack[h * rows : (h + 1) * rows]
    return total


def split3(x):
    high = x.astype(BF)
    rest = x - high.astype(F32)
    mid = rest.astype(BF)
    low = (rest - mid.astype(F32)).astype(BF)
    return high, mid, low


def prep_kernel(offsets, count, q, k, v, qt, kt, vt, s1, s2):
    matrix = pair_matrix()
    tile = (TOKENS, LANES)
    row = iota(tile, 0)
    place = jnp.where(row < HALF, 2 * row, 2 * (row - HALF) + 1)
    helper = helper_lane(tile)
    key_mask = jnp.where(place < count[0], 0.0, -BIG)
    q_aux = jnp.where(helper == 3, 1.0, 0.0)
    k_aux = jnp.where(helper < 3, -1.0, jnp.where(helper == 3, key_mask, 0.0))
    v_aux = jnp.where((helper >= 4) & (helper < 7), -1.0, 0.0)
    first = select_stack(offsets, 0)
    second = select_stack(offsets, 1)
    for n, (src, aux, dst) in enumerate(((q, q_aux, qt), (k, k_aux, kt), (v, v_aux, vt))):
        flat = (by_parity(src[...], matrix) + aux).astype(BF)
        dst[...] = flat
        cols = slice(n * LANES, (n + 1) * LANES)
        s1[:, cols] = folded(masked_stack(nn(first, flat), ROWS1), ROWS1).astype(BF)
        s2[:, cols] = folded(masked_stack(nn(second, flat), ROWS2), ROWS2).astype(BF)


def proj_kernel(count, gy, w, g):
    matrix = pair_matrix()
    total = jnp.zeros((TOKENS, FEAT), F32)
    for i in range(4):
        flat = by_parity(gy[i], matrix).astype(BF)
        total = total + nt(flat[:, :FEAT], w[:, i * FEAT : (i + 1) * FEAT])
    row = iota((TOKENS, FEAT), 0)
    place = jnp.where(row < HALF, 2 * row, 2 * (row - HALF) + 1)
    total = jnp.where(place < count[0], total, 0.0)
    g[...] = jnp.concatenate([total, jnp.zeros((TOKENS, LANES - FEAT), F32)], axis=1).astype(BF)


def level_stats(key_parts, value_parts, queries, grads):
    scores = [nt(k, queries) for k in key_parts]
    top = scores[0].max(axis=0, keepdims=True)
    for s in scores[1:]:
        top = jnp.maximum(top, s.max(axis=0, keepdims=True))
    mass = dot = None
    for s, v in zip(scores, value_parts):
        e = jnp.exp2((s - top) * EXP2)
        part = e.sum(axis=0, keepdims=True)
        part_dot = (e * nt(v, grads)).sum(axis=0, keepdims=True)
        mass = part if mass is None else mass + part
        dot = part_dot if dot is None else dot + part_dot
    return top, mass, dot


def spread(stats, stack, rows):
    top, mass, dot = stats
    width = top.shape[1]
    lane = iota((HEADS, width), 1)
    own = (lane >= rows * iota((HEADS, width), 0)) & (lane < rows * (iota((HEADS, width), 0) + 1))
    placed = [jnp.where(own, x, 0.0) for x in (top, mass, dot, jnp.ones_like(top))]
    placed = jnp.concatenate(placed, axis=0)
    out = sum(nn(term, stack) for term in split3(placed))
    there = out[12:16] > 0.5
    return jnp.where(there, out[0:4], -BIG), out[4:8], out[8:12]


def forward_kernel(offsets, q, g, k, v, kp, vp, kv1, kv2, gt, g1, g2):
    first = select_stack(offsets, 0)
    second = jnp.concatenate([select_stack(offsets, 1), jnp.zeros((128 - HEADS * ROWS2, TOKENS), BF)], axis=0)
    queries, grads = q[...], g[...]
    tops, masses, dots = [], [], []
    for h in range(HEADS):
        mask = head_mask(h, (1, LANES)).astype(BF)
        top, mass, dot = level_stats((k[...], kp[...]), (v[...], vp[...]), queries * mask, grads * mask)
        tops.append(top)
        masses.append(mass)
        dots.append(dot)
    top0, mass0, dot0 = (jnp.concatenate(x, axis=0) for x in (tops, masses, dots))

    def stack_of(select, x, rows):
        full = nn(select, x)
        parts = [masked_stack(full[: HEADS * rows], rows)]
        if full.shape[0] > HEADS * rows:
            parts.append(full[HEADS * rows :])
        return jnp.concatenate(parts, axis=0).astype(BF)

    stats1 = level_stats(
        (kv1[:, :LANES],), (kv1[:, LANES:],), stack_of(first, queries, ROWS1), stack_of(first, grads, ROWS1)
    )
    stats2 = level_stats(
        (kv2[:, :LANES],), (kv2[:, LANES:],), stack_of(second, queries, ROWS2), stack_of(second, grads, ROWS2)
    )
    top1, mass1, dot1 = spread(stats1, first, ROWS1)
    top2, mass2, dot2 = spread(stats2, second, ROWS2)
    top = jnp.maximum(jnp.maximum(top0, top1), top2)
    f0, f1, f2 = (jnp.exp2((x - top) * EXP2) for x in (top0, top1, top2))
    total = mass0 * f0 + mass1 * f1 + mass2 * f2
    grad_dot = (dot0 * f0 + dot1 * f1 + dot2 * f2) / total
    log_total = top + jnp.log(total) * ROOT
    rows = jnp.concatenate(
        [x.astype(F32) for x in (*split3(log_total), *split3(grad_dot))]
        + [jnp.ones((HEADS, TOKENS), F32), jnp.zeros((HEADS, TOKENS), F32)],
        axis=0,
    )
    at = iota((8 * HEADS, LANES), 0)
    s, h = at >> 2, at & 3
    slot = jnp.where(s < 3, s, jnp.where(s < 6, s + 1, jnp.where(s == 6, 3, 7)))
    place = jnp.where(iota((8 * HEADS, LANES), 1) == FEAT + 8 * h + slot, 1.0, 0.0).astype(BF)
    full = grads.astype(F32) + nn(rows.T.astype(BF), place)
    full = full.astype(BF)
    gt[...] = full
    g1[...] = folded(masked_stack(nn(first, full), ROWS1), ROWS1).astype(BF)
    g2[...] = folded(masked_stack(nn(second, full)[: HEADS * ROWS2], ROWS2), ROWS2).astype(BF)


def with_helpers(x, helpers):
    return jnp.where(iota(x.shape, 1) < FEAT, x, helpers)


def feature_mask(h, shape):
    lane = iota(shape, 1)
    return (lane >= HEAD * h) & (lane < HEAD * (h + 1))


def scatter_rows(offsets, parts1, parts2):
    total = None
    for level, part, rows in ((0, parts1, ROWS1), (1, parts2, ROWS2)):
        place = jnp.concatenate(
            [jnp.where(chosen(offsets, level, h, (TOKENS, rows), 1), 1.0, 0.0) for h in range(HEADS)], axis=1
        ).astype(BF)
        part = jnp.concatenate(
            [jnp.where(feature_mask(h, (rows, LANES)), part[h * rows : (h + 1) * rows], 0.0) for h in range(HEADS)],
            axis=0,
        )
        high = part.astype(BF)
        low = (part - high.astype(F32)).astype(BF)
        got = nn(place, high) + nn(place, low)
        total = got if total is None else total + got
    return total


def grad_query_kernel(offsets, q, gt, k, v, kp, vp, kv1, kv2, dq):
    first, second = select_stack(offsets, 0), select_stack(offsets, 1)
    grads = gt[...]
    queries = with_helpers(q[...], grads)

    def back(queries, grads, keys, values):
        total = None
        for kk, vv in zip(keys, values):
            weight = jnp.exp2(nt(queries, kk) * EXP2)
            score = (weight * nt(grads, vv)).astype(BF)
            part = nn(score, kk)
            total = part if total is None else total + part
        return total

    total = jnp.zeros((TOKENS, LANES), F32)
    for h in range(HEADS):
        mask = head_mask(h, (1, LANES)).astype(BF)
        part = back(queries * mask, grads * mask, (k[...], kp[...]), (v[...], vp[...]))
        total = jnp.where(feature_mask(h, (TOKENS, LANES)), part, total)
    q1 = masked_stack(nn(first, queries), ROWS1).astype(BF)
    g1 = masked_stack(nn(first, grads), ROWS1).astype(BF)
    q2 = masked_stack(nn(second, queries), ROWS2).astype(BF)
    g2 = masked_stack(nn(second, grads), ROWS2).astype(BF)
    part1 = back(q1, g1, (kv1[:, :LANES],), (kv1[:, LANES:],))
    part2 = back(q2, g2, (kv2[:, :LANES],), (kv2[:, LANES:],))
    total = (total + scatter_rows(offsets, part1, part2)) * SCALE
    dq[...] = to_paired(total.astype(BF), unpair_matrix())


def grad_key_kernel(offsets, k, v, q, gt, qp, gp, q1, g1, q2, g2, dk, dv):
    first, second = select_stack(offsets, 0), select_stack(offsets, 1)
    keys, values = k[...], v[...]

    def back(keys, values, queries, grads):
        total_k = total_v = None
        for qq, gg in zip(queries, grads):
            qq = with_helpers(qq, gg)
            weight = jnp.exp2(nt(keys, qq) * EXP2)
            score = (weight * nt(values, gg)).astype(BF)
            part_k = nn(score, qq)
            part_v = nn(weight.astype(BF), gg)
            total_k = part_k if total_k is None else total_k + part_k
            total_v = part_v if total_v is None else total_v + part_v
        return total_k, total_v

    total_k = jnp.zeros((TOKENS, LANES), F32)
    total_v = jnp.zeros((TOKENS, LANES), F32)
    for h in range(HEADS):
        mask = head_mask(h, (1, LANES)).astype(BF)
        part_k, part_v = back(keys * mask, values * mask, (q[...], qp[...]), (gt[...], gp[...]))
        features = feature_mask(h, (TOKENS, LANES))
        total_k = jnp.where(features, part_k, total_k)
        total_v = jnp.where(features, part_v, total_v)
    k1 = masked_stack(nn(first, keys), ROWS1).astype(BF)
    v1 = masked_stack(nn(first, values), ROWS1).astype(BF)
    k2 = masked_stack(nn(second, keys), ROWS2).astype(BF)
    v2 = masked_stack(nn(second, values), ROWS2).astype(BF)
    k1_part, v1_part = back(k1, v1, (q1[...],), (g1[...],))
    k2_part, v2_part = back(k2, v2, (q2[...],), (g2[...],))
    total_k = (total_k + scatter_rows(offsets, k1_part, k2_part)) * SCALE
    total_v = total_v + scatter_rows(offsets, v1_part, v2_part)
    matrix = unpair_matrix()
    dk[...] = to_paired(total_k.astype(BF), matrix)
    dv[...] = to_paired(total_v.astype(BF), matrix)


def call(kernel, outs, n_smem, *args):
    return pl.pallas_call(
        kernel,
        out_shape=[jax.ShapeDtypeStruct(s, BF) for s in outs],
        in_specs=[SMEM] * n_smem + [VMEM] * (len(args) - n_smem),
        out_specs=[VMEM] * len(outs),
        compiler_params=pltpu.CompilerParams(vmem_limit_bytes=48 * 1024 * 1024),
    )(*args)


def per_device(queries, keys, values, grad_y, out_weight, counts, offsets):
    seq = lax.axis_index("seq")
    head = lax.axis_index("head")
    my_offsets = lax.dynamic_slice(offsets, (0, head * HEADS), (2, HEADS))
    my_count = lax.dynamic_slice(counts, (seq,), (1,))
    n_seq = lax.axis_size("seq")
    swap = [(i, i ^ 1) for i in range(n_seq)]
    rings = [[GROUP * b + i for i in range(GROUP)] for b in range(n_seq // GROUP)]
    planes = [[GROUP * b + i for b in range(n_seq // GROUP)] for i in range(GROUP)]

    def pair(x):
        return lax.ppermute(x, "seq", swap)

    def ring(x):
        copies = jnp.broadcast_to(x[None], (GROUP,) + x.shape)
        return lax.all_to_all(copies, "seq", 0, 0, axis_index_groups=rings).reshape((-1,) + x.shape[1:])

    def across(x):
        copies = jnp.broadcast_to(x[None], (GROUP,) + x.shape)
        return lax.all_to_all(copies, "seq", 0, 0, axis_index_groups=planes).reshape((-1,) + x.shape[1:])

    def gather_levels(rows1, rows2):
        both = ring(jnp.concatenate([rows1, rows2], axis=0)).reshape(GROUP, ROWS1 + ROWS2, -1)
        level1 = both[:, :ROWS1].reshape(GROUP * ROWS1, -1)
        level2 = across(both[:, ROWS1:].reshape(GROUP * ROWS2, -1))
        return level1, level2

    gy = lax.all_gather(grad_y, "head", axis=0)
    flat = (TOKENS, LANES)
    q, k, v, s1, s2 = call(
        prep_kernel, [flat, flat, flat, (ROWS1, 3 * LANES), (ROWS2, 3 * LANES)], 2, my_offsets, my_count, queries, keys, values
    )
    kvq1, kvq2 = gather_levels(s1, s2)
    q1, kv1 = kvq1[:, :LANES], kvq1[:, LANES:]
    q2, kv2 = kvq2[:, :LANES], kvq2[:, LANES:]
    kp, vp, qp = pair(k), pair(v), pair(q)
    (g,) = call(proj_kernel, [flat], 1, my_count, gy, out_weight)
    gt, g1, g2 = call(
        forward_kernel, [flat, (ROWS1, LANES), (ROWS2, LANES)], 1, my_offsets, q, g, k, v, kp, vp, kv1, kv2
    )
    gp = pair(gt)
    g1, g2 = gather_levels(g1, g2)
    paired = (HALF, 2 * FEAT)
    (dq,) = call(grad_query_kernel, [paired], 1, my_offsets, q, gt, k, v, kp, vp, kv1, kv2)
    dk, dv = call(grad_key_kernel, [paired, paired], 1, my_offsets, k, v, q, gt, qp, gp, q1, g1, q2, g2)
    return dq, dk, dv


def solution(mesh):
    split = P("seq", "head")
    return jax.shard_map(
        per_device,
        mesh=mesh,
        in_specs=(split, split, split, split, P("head", None), P(), P()),
        out_specs=(split, split, split),
        check_vma=False,
    )
```

time: 917 us -> 119 us (0.13); the launches traced: 907 us -> 118 us
  waiting for transfers between devices: 607 us -> 0.02 us
  blocking collectives: 157 us -> 72.1 us
  local copies, waits for them, and re-layouts: 61.3 us -> 14.4 us
  other arithmetic: 34.2 us -> 0.01 us
  matrix products: 19.3 us -> 0 us
  Pallas kernels: 0 us -> 16.2 us
  between operations: 16.1 us -> 0.78 us
    unnamed x2 -> x0, waiting for transfers between devices: 591 us -> none
    all_gather x2 -> x1, blocking collectives: 157 us -> 20.1 us  [per_device(): gy = lax.all_gather(grad_y, 'head', axis=0)]
    all_to_all x0 -> x2, blocking collectives: none -> 52 us  [ring(): lax.all_to_all(copies, 'seq', 0, 0, axis_index_groups=rings)]
    dot_general x25 -> x0, matrix products: 19.3 us -> none  [the longest x4 3.76 us: attention_backward(): jnp.einsum('hqk,hkd->hqd', grad_score, key_block, preferred_element_type=...]
    ppermute x8 -> x4, waiting for transfers between devices: 16.4 us -> 0.01 us  [pair(): return lax.ppermute(x, 'seq', swap)]
    pallas_call x0 -> x5, Pallas kernels: none -> 16.2 us  [call(): pl.pallas_call(kernel, out_shape=[jax.ShapeDtypeStruct(s, BF) for s in ou...]
    reduce_sum x18 -> x0, other arithmetic: 13.9 us -> none  [the longest x14 11 us: choose_rows(): jnp.sum(jnp.where(pattern, reshaped_rows, jnp.zeros((), source_shard.dtyp...]
    all_to_all x0 -> x2, starting transfers between devices: none -> 10.5 us  [across(): lax.all_to_all(copies, 'seq', 0, 0, axis_index_groups=planes)]
  transfers between devices with their start and end apart: 9 -> 6, of which waited for: 5 -> 0; matrix products, arithmetic and copies ran while one was open for 6% -> 3% of each run, Pallas kernels for 0% -> 5%
where the time goes in v1:
time: 119 us; the launch traced here: 118 us
  blocking collectives  72.1 us (61%)
  Pallas kernels  16.2 us (14%)
  starting transfers between devices  14.6 us (12%)
  local copies, waits for them, and re-layouts  14.4 us (12%)
    all_to_all x2, blocking collectives, ring(): lax.all_to_all(copies, 'seq', 0, 0, axis_index_groups=rings)  52 us
    all_gather x1, blocking collectives, per_device(): gy = lax.all_gather(grad_y, 'head', axis=0)  20.1 us
    pallas_call x5, Pallas kernels, call(): pl.pallas_call(kernel, out_shape=[jax.ShapeDtypeStruct(s, BF) for s in ou...  16.2 us
    all_to_all x2, starting transfers between devices, across(): lax.all_to_all(copies, 'seq', 0, 0, axis_index_groups=planes)  10.5 us
    unnamed x26, local copies, waits for them, and re-layouts  7.39 us
    ppermute x4, starting transfers between devices, pair(): return lax.ppermute(x, 'seq', swap)  4.05 us
    slice x2, local copies, waits for them, and re-layouts, per_device(): q2, kv2 = (kvq2[:, :LANES], kvq2[:, LANES:])  2.42 us
  transfers between devices with their start and end apart: 6, of which 0 were waited for; matrix products, arithmetic and copies ran while one was open for 3% of the time, Pallas kernels for 5%

profile of v1, /device:TPU:2, one launch (start us, length us, event | category | flops | bytes accessed | tf_op | source)
XLA Modules:
  0.0 118.1 jit_solution(11707959813036579994)
XLA Ops:
  0.6 0.0 copy-start
  0.7 1.2 %dynamic_slice.7.count = s32[1]{0:T(128)} dynamic-slice(s32[64]{0:T(128)} %param.12, s32[]{:T(128)S(6)} %select_n.7), dynamic_slice_sizes={1} | dynamic-slice | bytes 12 | tf_op jit(solution)/shard_map/dynamic_slice | solution.py:332
  1.9 0.0 copy-done
  1.9 0.1 constant_dynamic-slice_fusion.offsets
  2.0 0.0 copy-start.6
  2.0 0.9 copy-done.6
  2.9 0.0 copy-start.7
  2.9 0.9 copy-done.7
  3.8 0.0 copy-start.8
  3.8 0.9 copy-done.8
  4.6 2.2 %shard_map.94 = (bf16[256,256]{1,0:T(8,128)(2,1)S(1)}, bf16[256,256]{1,0:T(8,128)(2,1)S(1)}, bf16[256,256]{1,0:T(8,128)(2,1)S(1)}, bf16[64,768]{1,0:T(8,128)(2,1)S(1)}, bf16[16,768]{1,0:T(8,128)(2,1)S(1)}) custom-call(s32[2,4]{1,0:T(2,128)S(1)} %constant_dynamic-slice_fusion.offsets, s32[1]{0:T(128)} %dynamic_slice.7.count, bf16[128,384]{1,0:T(8,128)(2,1)S(1)} %copy-done.6, ...), custom_call_target="tpu_custom_call" | custom-call | tf_op jit(solution)/shard_map/pallas_call | solution.py:319
  6.9 0.1 broadcast_in_dim.12
  6.9 35.6 %all_to_all.20 = bf16[8,80,768]{2,1,0:T(8,128)(2,1)S(1)} all-to-all(bf16[8,80,768]{2,1,0:T(8,128)(2,1)S(1)} %broadcast_in_dim.12), channel_id=1, replica_groups={{0,4,8,12,16,20,24,28},{32,36,40,44,48,52,56,60},{64,68,72,76,80,84,88,..., dimensions={0} | all-to-all | bytes 1966080 | tf_op jit(solution)/shard_map/all_to_all | solution.py:343
  42.5 1.2 %broadcast_in_dim.28 = bf16[8,128,768]{2,1,0:T(8,128)(2,1)} broadcast(bf16[128,768]{1,0:T(8,128)(2,1)S(1)} %bitcast.12), dimensions={1,2} | broadcast | bytes 1769472 | tf_op jit(solution)/shard_map/broadcast_in_dim | solution.py:346
  43.8 0.0 copy-start.12
  43.8 0.0 copy-start.1
  43.8 6.0 %all-to-all-start.1 = ((bf16[8,128,768]{2,1,0:T(8,128)(2,1)}), bf16[8,128,768]{2,1,0:T(8,128)(2,1)}, u32[]{:S(2)}, u32[]{:S(2)}) async-start(bf16[8,128,768]{2,1,0:T(8,128)(2,1)} %broadcast_in_dim.28), calls=%async_computation.1 | async-start | bytes 3145728 | tf_op jit(solution)/shard_map/all_to_all | solution.py:347
  49.8 0.6 collective-permute-start
  50.3 1.5 %collective-permute-start.1 = (bf16[256,256]{1,0:T(8,128)(2,1)S(1)}, bf16[256,256]{1,0:T(8,128)(2,1)S(1)}, u32[]{:S(2)}, u32[]{:S(2)}) collective-permute-start(bf16[256,256]{1,0:T(8,128)(2,1)S(1)} %get-tuple-element.15.v), channel_id=1, source_target_pairs={{0,4},{4,0},{8,12},{12,8},{16,20},{20,16},{24,28},{28,24},{32,36},... | collective-permute-start | bytes 393224 | tf_op jit(solution)/shard_map/ppermute | solution.py:339
  51.8 0.0 copy-done.12
  51.8 20.1 %all-gather = bf16[512,384]{1,0:T(8,128)(2,1)S(1)} all-gather(bf16[128,384]{1,0:T(8,128)(2,1)S(1)} %copy-done.12), channel_id=2, replica_groups=mesh['seq'=64,'head'=4] {'head'}, dimensions={0}, use_global_device_ids=true | all-gather | bytes 491520 | tf_op jit(solution)/shard_map/all_gather | solution.py:355
  71.9 0.0 copy-done.1
  71.9 1.4 %shard_map.95.g = bf16[256,256]{1,0:T(8,128)(2,1)S(1)} custom-call(s32[1]{0:T(128)} %dynamic_slice.7.count, bf16[4,128,384]{2,1,0:T(8,128)(2,1)S(1)} %bitcast.8, bf16[192,768]{1,0:T(8,128)(2,1)S(1)} %copy-done.1), custom_call_target="tpu_custom_call" | custom-call | tf_op jit(solution)/shard_map/pallas_call | solution.py:319
  73.2 0.1 slice.32
  73.3 0.0 copy-start.9
  73.3 0.9 copy-done.9
  74.2 0.0 all-to-all-done.1
  74.2 1.3 %slice.35.kv2 = bf16[1024,512]{1,0:T(8,128)(2,1)S(1)} slice(bf16[1024,768]{1,0:T(8,128)(2,1)} %bitcast.3), slice={[0:1024], [256:768]} | slice | bytes 2097152 | tf_op jit(solution)/shard_map/slice | solution.py:362
  75.5 0.0 collective-permute-done.kp
  75.6 0.0 collective-permute-done.1.vp
  75.6 3.9 %shard_map.96 = (bf16[256,256]{1,0:T(8,128)(2,1)}, bf16[64,256]{1,0:T(8,128)(2,1)S(1)}, bf16[16,256]{1,0:T(8,128)(2,1)S(1)}) custom-call(s32[2,4]{1,0:T(2,128)S(1)} %constant_dynamic-slice_fusion.offsets, bf16[256,256]{1,0:T(8,128)(2,1)S(1)} %get-tuple-element.13.q, bf16[256,256]{1,0:T(8,128)(2,1)S(1)} %shard_map.95.g, ...), custom_call_target="tpu_custom_call" | custom-call | tf_op jit(solution)/shard_map/pallas_call | solution.py:319
  79.4 16.4 %all_to_all.21 = bf16[8,80,256]{2,1,0:T(8,128)(2,1)S(1)} all-to-all(bf16[8,80,256]{2,1,0:T(8,128)(2,1)S(1)} %broadcast_in_dim.29), channel_id=1, replica_groups={{0,4,8,12,16,20,24,28},{32,36,40,44,48,52,56,60},{64,68,72,76,80,84,88,..., dimensions={0} | all-to-all | bytes 655360 | tf_op jit(solution)/shard_map/all_to_all | solution.py:343
  95.9 0.0 copy-start.10
  95.9 0.7 copy-done.10
  96.6 0.8 broadcast_in_dim.31
  97.5 4.6 %all-to-all-start.3 = ((bf16[8,128,256]{2,1,0:T(8,128)(2,1)}), bf16[8,128,256]{2,1,0:T(8,128)(2,1)S(1)}, u32[]{:S(2)}, u32[]{:S(2)}) async-start(bf16[8,128,256]{2,1,0:T(8,128)(2,1)} %broadcast_in_dim.31), calls=%async_computation.3 | async-start | bytes 1048576 | tf_op jit(solution)/shard_map/all_to_all | solution.py:347
  102.0 0.6 collective-permute-start.2
  102.6 1.5 %collective-permute-start.3 = (bf16[256,256]{1,0:T(8,128)(2,1)}, bf16[256,256]{1,0:T(8,128)(2,1)S(1)}, u32[]{:S(2)}, u32[]{:S(2)}) collective-permute-start(bf16[256,256]{1,0:T(8,128)(2,1)} %get-tuple-element.18.gt), channel_id=1, source_target_pairs={{0,4},{4,0},{8,12},{12,8},{16,20},{20,16},{24,28},{28,24},{32,36},... | collective-permute-start | bytes 393224 | tf_op jit(solution)/shard_map/ppermute | solution.py:339
  104.1 1.0 slice.36.q1
  105.0 0.0 copy-start.11
  105.0 1.1 slice.38.q2
  106.2 4.1 %shard_map.97 = bf16[128,384]{1,0:T(8,128)(2,1)} custom-call(s32[2,4]{1,0:T(2,128)S(1)} %constant_dynamic-slice_fusion.offsets, bf16[256,256]{1,0:T(8,128)(2,1)S(1)} %get-tuple-element.13.q, bf16[256,256]{1,0:T(8,128)(2,1)} %get-tuple-element.18.gt, bf16[256,256]{1,0:T(8,128)(2,1)S(1)} %get-tuple-element.14.k, bf16[256,256]{1,0:T(8,128)(2,1)S(1)} %get-tuple-element.15.v, ...), custom_call_target="tpu_custom_call" | custom-call | tf_op jit(solution)/shard_map/pallas_call | solution.py:319
  110.3 0.0 copy-done.11
  110.3 0.0 collective-permute-done.2.qp
  110.3 0.0 copy-start.2
  110.3 0.6 copy-done.2
  111.0 0.0 collective-permute-done.3.gp
  111.0 0.0 copy-start.4
  111.0 0.6 copy-done.4
  111.6 0.0 all-to-all-done.3
  111.6 0.0 copy-start.3
  111.6 0.9 copy-done.3
  112.5 0.0 copy-start.5
  112.5 0.9 copy-done.5
  113.4 4.6 %shard_map.98 = (bf16[128,384]{1,0:T(8,128)(2,1)}, bf16[128,384]{1,0:T(8,128)(2,1)}) custom-call(s32[2,4]{1,0:T(2,128)S(1)} %constant_dynamic-slice_fusion.offsets, bf16[256,256]{1,0:T(8,128)(2,1)S(1)} %get-tuple-element.14.k, bf16[256,256]{1,0:T(8,128)(2,1)S(1)} %get-tuple-element.15.v, bf16[256,256]{1,0:T(8,128)(2,1)S(1)} %get-tuple-element.13.q, ...), custom_call_target="tpu_custom_call" | custom-call | tf_op jit(solution)/shard_map/pallas_call | solution.py:319
  (7 shorter events, 0.1 us)
Async XLA Ops:
  0.6 1.3 %copy-start = (s32[2,16]{1,0:T(2,128)S(1)}, s32[2,16]{1,0:T(2,128)}, u32[]{:S(2)}) copy-start(s32[2,16]{1,0:T(2,128)} %param.13) | copy-start | bytes 388
  2.0 0.9 copy-start.6
  2.9 0.9 copy-start.7
  3.8 0.9 copy-start.8
  43.8 8.0 %copy-start.12 = (bf16[128,384]{1,0:T(8,128)(2,1)S(1)}, bf16[128,384]{1,0:T(8,128)(2,1)}, u32[]{:S(2)}) copy-start(bf16[128,384]{1,0:T(8,128)(2,1)} %param.10) | copy-start | bytes 294916
  43.8 28.1 %copy-start.1 = (bf16[192,768]{1,0:T(8,128)(2,1)S(1)}, bf16[192,768]{1,0:T(8,128)(2,1)}, u32[]{:S(2)}) copy-start(bf16[192,768]{1,0:T(8,128)(2,1)} %w.1) | copy-start | bytes 884740
  43.8 30.4 %all-to-all-start.1 = ((bf16[8,128,768]{2,1,0:T(8,128)(2,1)}), bf16[8,128,768]{2,1,0:T(8,128)(2,1)}, u32[]{:S(2)}, u32[]{:S(2)}) async-start(bf16[8,128,768]{2,1,0:T(8,128)(2,1)} %broadcast_in_dim.28), calls=%async_computation.1 | async-start | bytes 3145728 | tf_op jit(solution)/shard_map/all_to_all | solution.py:347
  49.8 25.8 %collective-permute-start = (bf16[256,256]{1,0:T(8,128)(2,1)S(1)}, bf16[256,256]{1,0:T(8,128)(2,1)S(1)}, u32[]{:S(2)}, u32[]{:S(2)}) collective-permute-start(bf16[256,256]{1,0:T(8,128)(2,1)S(1)} %get-tuple-element.14.k), channel_id=1, source_target_pairs={{0,4},{4,0},{8,12},{12,8},{16,20},{20,16},{24,28},{28,24},{32,36},... | collective-permute-start | bytes 393224 | tf_op jit(solution)/shard_map/ppermute | solution.py:339
  50.3 25.2 %collective-permute-start.1 = (bf16[256,256]{1,0:T(8,128)(2,1)S(1)}, bf16[256,256]{1,0:T(8,128)(2,1)S(1)}, u32[]{:S(2)}, u32[]{:S(2)}) collective-permute-start(bf16[256,256]{1,0:T(8,128)(2,1)S(1)} %get-tuple-element.15.v), channel_id=1, source_target_pairs={{0,4},{4,0},{8,12},{12,8},{16,20},{20,16},{24,28},{28,24},{32,36},... | collective-permute-start | bytes 393224 | tf_op jit(solution)/shard_map/ppermute | solution.py:339
  73.3 0.9 copy-start.9
  95.9 0.7 copy-start.10
  97.5 14.1 %all-to-all-start.3 = ((bf16[8,128,256]{2,1,0:T(8,128)(2,1)}), bf16[8,128,256]{2,1,0:T(8,128)(2,1)S(1)}, u32[]{:S(2)}, u32[]{:S(2)}) async-start(bf16[8,128,256]{2,1,0:T(8,128)(2,1)} %broadcast_in_dim.31), calls=%async_computation.3 | async-start | bytes 1048576 | tf_op jit(solution)/shard_map/all_to_all | solution.py:347
  102.0 8.3 %collective-permute-start.2 = (bf16[256,256]{1,0:T(8,128)(2,1)S(1)}, bf16[256,256]{1,0:T(8,128)(2,1)S(1)}, u32[]{:S(2)}, u32[]{:S(2)}) collective-permute-start(bf16[256,256]{1,0:T(8,128)(2,1)S(1)} %get-tuple-element.13.q), channel_id=1, source_target_pairs={{0,4},{4,0},{8,12},{12,8},{16,20},{20,16},{24,28},{28,24},{32,36},... | collective-permute-start | bytes 393224 | tf_op jit(solution)/shard_map/ppermute | solution.py:339
  102.6 8.4 %collective-permute-start.3 = (bf16[256,256]{1,0:T(8,128)(2,1)}, bf16[256,256]{1,0:T(8,128)(2,1)S(1)}, u32[]{:S(2)}, u32[]{:S(2)}) collective-permute-start(bf16[256,256]{1,0:T(8,128)(2,1)} %get-tuple-element.18.gt), channel_id=1, source_target_pairs={{0,4},{4,0},{8,12},{12,8},{16,20},{20,16},{24,28},{28,24},{32,36},... | collective-permute-start | bytes 393224 | tf_op jit(solution)/shard_map/ppermute | solution.py:339
  105.0 5.3 %copy-start.11 = (bf16[8,80,256]{2,1,0:T(8,128)(2,1)S(1)}, bf16[8,80,256]{2,1,0:T(8,128)(2,1)}, u32[]{:S(2)}) copy-start(bf16[8,80,256]{2,1,0:T(8,128)(2,1)} %copy-done.10) | copy-start | bytes 983044
  110.3 0.7 copy-start.2
  111.0 0.6 copy-start.4
  111.6 0.9 copy-start.3
  112.5 0.9 copy-start.5

commit v2 on v1

v2 whole, which is shorter than its diff:
```python
import math

import jax
import jax.numpy as jnp
from jax import lax
from jax.experimental import pallas as pl
from jax.experimental.pallas import tpu as pltpu
from jax.sharding import PartitionSpec as P

HEAD = 48
HEADS = 4
TOKENS = 256
HALF = TOKENS // 2
FEAT = HEADS * HEAD
PAIR = 2 * FEAT
LANES = 256
SIDE = 128
MID = 4
TOP = 16
GROUP = 8
ROWS1 = TOKENS // MID
ROWS2 = TOKENS // TOP
ROWS = ROWS1 + ROWS2
OWN = GROUP * ROWS1
TAIL = 2 * ROWS2 + 48
SCALE = HEAD**-0.5
ROOT = math.sqrt(HEAD)
EXP2 = SCALE * math.log2(math.e)
BIG = 1e30
VMEM_BYTES = 20 * 1024 * 1024
BF = jnp.bfloat16
F32 = jnp.float32

VMEM = pl.BlockSpec(memory_space=pltpu.VMEM)
SMEM = pl.BlockSpec(memory_space=pltpu.SMEM)


def iota(shape, dim):
    return lax.broadcasted_iota(jnp.int32, shape, dim)


def nt(a, b):
    return lax.dot_general(a, b, (((1,), (1,)), ((), ())), preferred_element_type=F32)


def nn(a, b):
    return jnp.dot(a, b, preferred_element_type=F32)


def first_mask(h, shape):
    lane = iota(shape, 1)
    return ((lane >= HEAD * h) & (lane < HEAD * (h + 1))) | ((lane >= FEAT + 8 * h) & (lane < FEAT + 8 * h + 8))


def second_mask(h, shape):
    lane = iota(shape, 1)
    at = lane - (LANES - FEAT)
    return ((at >= HEAD * h) & (at < HEAD * (h + 1))) | ((lane >= 8 * h) & (lane < 8 * h + 8))


def helper_mask(h, shape):
    lane = iota(shape, 1) & 63
    return (lane >= 8 * h) & (lane < 8 * h + 8)


def first_view(pair, helpers):
    left, right = pair[:, :SIDE], pair[:, SIDE:LANES]
    return jnp.concatenate([left, jnp.where(iota(right.shape, 1) < 64, right, helpers)], axis=1)


def second_view(pair, helpers):
    left, right = pair[:, SIDE:LANES], pair[:, LANES:]
    return jnp.concatenate([jnp.where(iota(left.shape, 1) < 64, helpers, left), right], axis=1)


def query_helpers(rows):
    lane = iota((rows, SIDE), 1)
    return jnp.where((lane >= 64) & (lane < 96) & ((lane & 7) == 3), 1.0, 0.0).astype(BF)


def key_helpers(mask):
    lane = iota(mask.shape, 1)
    slot = lane & 7
    used = (lane & 63) < 32
    value = jnp.where(slot < 3, -1.0, jnp.where(slot == 3, mask, jnp.where(slot < 7, -1.0, 0.0)))
    value = jnp.where((lane < 64) & (slot < 4), 0.0, value)
    value = jnp.where((lane >= 64) & (slot >= 4), 0.0, value)
    return jnp.where(used, value, 0.0).astype(BF)


def lane_offsets(offsets, level, shape):
    h = (iota(shape, 1) >> 3) & 3
    base = lax.axis_index("head") * HEADS
    at = [offsets[level, base + i] for i in range(HEADS)]
    return jnp.where(h == 0, at[0], jnp.where(h == 1, at[1], jnp.where(h == 2, at[2], at[3])))


def dilated_mask(offsets, level, count):
    rows, rate = (ROWS1, MID) if level == 0 else (ROWS2, TOP)
    shape = (rows, SIDE)
    return jnp.where(rate * iota(shape, 0) + lane_offsets(offsets, level, shape) < count, 0.0, -BIG)


def positions(shape):
    row = iota(shape, 0)
    return jnp.where(row < HALF, 2 * row, 2 * (row - HALF) + 1)


def full_mask(count):
    return jnp.where(positions((TOKENS, SIDE)) < count, 0.0, -BIG)


def by_parity(paired):
    halves = [
        jnp.concatenate([paired[:, (2 * h + t) * HEAD : (2 * h + t + 1) * HEAD] for h in range(HEADS)], axis=1)
        for t in range(2)
    ]
    return jnp.concatenate(halves, axis=0)


def to_paired(flat):
    pieces = []
    for h in range(HEADS):
        for t in range(2):
            pieces.append(flat[t * HALF : (t + 1) * HALF, h * HEAD : (h + 1) * HEAD])
    return jnp.concatenate(pieces, axis=1).astype(BF)


def place_of(offsets, level, h, shape, dim):
    rate = MID if level == 0 else TOP
    return rate * iota(shape, dim) + offsets[level, lax.axis_index("head") * HEADS + h]


def chosen(offsets, level, h, shape, dim):
    place = place_of(offsets, level, h, shape, dim)
    return ((place >> 1) + (place & 1) * HALF) == iota(shape, 1 - dim)


def select_stack(offsets, level):
    rows = ROWS1 if level == 0 else ROWS2
    return jnp.concatenate(
        [jnp.where(chosen(offsets, level, h, (rows, TOKENS), 0), 1.0, 0.0) for h in range(HEADS)], axis=0
    ).astype(BF)


def folded(stack, rows, mask):
    total = None
    for h in range(HEADS):
        part = jnp.where(mask(h, (rows, stack.shape[1])), stack[h * rows : (h + 1) * rows], 0.0)
        total = part if total is None else total + part
    return total


def head_stack(rows, mask):
    return jnp.concatenate([rows * mask(h, (1, rows.shape[1])).astype(BF) for h in range(HEADS)], axis=0)


def feature_mask(h, shape):
    lane = iota(shape, 1)
    return (lane >= HEAD * h) & (lane < HEAD * (h + 1))


def split3(x):
    high = x.astype(BF)
    rest = x - high.astype(F32)
    mid = rest.astype(BF)
    low = (rest - mid.astype(F32)).astype(BF)
    return high, mid, low


def paired_rows(offsets, source):
    parts = []
    for level, rows in ((0, ROWS1), (1, ROWS2)):
        total = None
        for h in range(HEADS):
            row = place_of(offsets, level, h, (rows, HALF), 0) >> 1
            pick = jnp.where(row == iota((rows, HALF), 1), 1.0, 0.0).astype(BF)
            both = nn(pick, source[:, 2 * HEAD * h : 2 * HEAD * (h + 1)])
            odd = (place_of(offsets, level, h, (rows, HEAD), 0) & 1) == 1
            part = jnp.where(odd, both[:, HEAD:], both[:, :HEAD])
            total = [part] if total is None else total + [part]
        parts.append(jnp.concatenate(total, axis=1))
    return jnp.concatenate(parts, axis=0)


def rows_kernel(offsets, k, v, copies):
    both = jnp.concatenate([paired_rows(offsets, k), paired_rows(offsets, v)], axis=1).astype(BF)
    for i in range(GROUP):
        copies[i] = both


def pairs_kernel(k, v, k_next, v_next, kv, kv_next):
    for a, b, out in ((k, v, kv), (k_next, v_next, kv_next)):
        out[...] = jnp.concatenate([by_parity(a[...].astype(F32)), by_parity(b[...].astype(F32))], axis=1).astype(BF)


def repeat_kernel(rows, out):
    block = rows[:, ROWS1:].reshape(GROUP * ROWS2, PAIR)
    for i in range(GROUP):
        out[i] = block


def proj_kernel(offsets, counts, gy, w, q, qg, qg_top):
    total = jnp.zeros((TOKENS, FEAT), F32)
    for i in range(4):
        flat = by_parity(gy[i].astype(F32)).astype(BF)
        total = total + nt(flat, w[:, i * FEAT : (i + 1) * FEAT])
    total = jnp.where(positions((TOKENS, FEAT)) < counts[lax.axis_index("seq")], total, 0.0)
    flat = jnp.concatenate([by_parity(q[...].astype(F32)), total], axis=1).astype(BF)
    qg[:TOKENS] = flat

    def mask(h, shape):
        return feature_mask(h, shape) | feature_mask(h + HEADS, shape)

    qg[TOKENS : TOKENS + ROWS1] = folded(nn(select_stack(offsets, 0), flat), ROWS1, mask).astype(BF)
    qg_top[...] = folded(nn(select_stack(offsets, 1), flat), ROWS2, mask).astype(BF)


def level_stats(keys, values, queries, grads):
    scores = [nt(k, queries) for k in keys]
    top = scores[0].max(axis=0, keepdims=True)
    for s in scores[1:]:
        top = jnp.maximum(top, s.max(axis=0, keepdims=True))
    mass = dot = None
    for s, v in zip(scores, values):
        e = jnp.exp2((s - top) * EXP2)
        part = e.sum(axis=0, keepdims=True)
        part_dot = (e * nt(v, grads)).sum(axis=0, keepdims=True)
        mass = part if mass is None else mass + part
        dot = part_dot if dot is None else dot + part_dot
    return top, mass, dot


def spread(stats, stack, rows):
    top, mass, dot = stats
    width = top.shape[1]
    lane = iota((HEADS, width), 1)
    row = iota((HEADS, width), 0)
    own = (lane >= rows * row) & (lane < rows * (row + 1))
    placed = [jnp.where(own, x, 0.0) for x in (top, mass, dot, jnp.ones_like(top))]
    placed = jnp.concatenate(placed, axis=0)
    out = sum(nn(term, stack) for term in split3(placed))
    there = out[12:16] > 0.5
    return jnp.where(there, out[0:4], -BIG), out[4:8], out[8:12]


def merged(parts):
    top = parts[0][0]
    for p in parts[1:]:
        top = jnp.maximum(top, p[0])
    mass = dot = 0.0
    for p in parts:
        f = jnp.exp2((p[0] - top) * EXP2)
        mass = mass + p[1] * f
        dot = dot + p[2] * f
    return top, mass, dot


def fill_level1(offsets, counts, rows, kv1):
    seq = lax.axis_index("seq")
    base = seq - (seq & (GROUP - 1))
    for s in range(GROUP):
        helpers = key_helpers(dilated_mask(offsets, 0, counts[base + s]))
        block = rows[s, :ROWS1]
        kv1[0, s * ROWS1 : (s + 1) * ROWS1] = first_view(block, helpers)
        kv1[1, s * ROWS1 : (s + 1) * ROWS1] = second_view(block, helpers)


def forward_kernel(offsets, counts, qg, qg_top, kv, kvp, rows, tail, kv1):
    seq = lax.axis_index("seq")
    fill_level1(offsets, counts, rows, kv1)
    flat = qg[:TOKENS]
    queries = first_view(flat, query_helpers(TOKENS))
    grads = second_view(flat, jnp.zeros((TOKENS, SIDE), BF))
    own = key_helpers(full_mask(counts[seq]))
    other = key_helpers(full_mask(counts[seq ^ 1]))
    keys = (first_view(kv[...], own), first_view(kvp[...], other))
    values = (second_view(kv[...], own), second_view(kvp[...], other))
    parts = []
    for h in range(HEADS):
        q_mask = first_mask(h, (1, LANES)).astype(BF)
        g_mask = second_mask(h, (1, LANES)).astype(BF)
        parts.append(level_stats(keys, values, queries * q_mask, grads * g_mask))
    level0 = [jnp.concatenate([p[i] for p in parts], axis=0) for i in range(3)]
    block = qg[TOKENS : TOKENS + ROWS1]
    q1 = head_stack(first_view(block, query_helpers(ROWS1)), first_mask)
    g1 = head_stack(second_view(block, jnp.zeros((ROWS1, SIDE), BF)), second_mask)
    select1, select2 = select_stack(offsets, 0), select_stack(offsets, 1)
    level1 = spread(level_stats((kv1[0],), (kv1[1],), q1, g1), select1, ROWS1)
    terms = split3(jnp.concatenate(merged((level0, level1)), axis=0))
    own_head = [(iota((3 * HEADS, 1), 0) & 3) == h for h in range(HEADS)]
    empty = jnp.zeros((3 * HEADS, SIDE - ROWS), F32)
    chosen_terms = []
    for term in terms:
        one, two = nt(term, select1), nt(term, select2)
        row1 = row2 = 0.0
        for h in range(HEADS):
            row1 = row1 + jnp.where(own_head[h], one[:, h * ROWS1 : (h + 1) * ROWS1], 0.0)
            row2 = row2 + jnp.where(own_head[h], two[:, h * ROWS2 : (h + 1) * ROWS2], 0.0)
        chosen_terms.append(jnp.concatenate([row1, row2, empty], axis=1))
    pad = jnp.zeros((16 - 3 * HEADS, PAIR), F32)
    tail[:ROWS2] = qg_top[...]
    tail[ROWS2 : 2 * ROWS2] = jnp.concatenate([jnp.concatenate(chosen_terms, axis=1), pad], axis=0).astype(BF)
    for i, term in enumerate(terms):
        wide = jnp.concatenate([term.astype(F32), jnp.zeros((3 * HEADS, PAIR - LANES), F32)], axis=1)
        tail[16 * (i + 2) : 16 * (i + 3)] = jnp.concatenate([wide, pad], axis=0).astype(BF)


def fill_level2(offsets, counts, rows, keys, values):
    for a in range(GROUP):
        for s in range(GROUP):
            helpers = key_helpers(dilated_mask(offsets, 1, counts[a * GROUP + s]))
            block = rows[a, s * ROWS2 : (s + 1) * ROWS2]
            at = (a * GROUP + s) * ROWS2
            keys[at : at + ROWS2] = first_view(block, helpers)
            values[at : at + ROWS2] = second_view(block, helpers)


def summed_terms(ref, at):
    wide = ref[at : at + 16].astype(F32)
    return wide[:, :SIDE] + wide[:, SIDE : 2 * SIDE] + wide[:, 2 * SIDE :]


def finish_kernel(offsets, counts, tails, rows, st, packed, keys, values):
    fill_level2(offsets, counts, rows, keys, values)
    starts = [0, TAIL] + [2 * TAIL + 2 * ROWS2 * i for i in range(GROUP - 2)]
    block = jnp.concatenate([tails[at : at + ROWS2] for at in starts], axis=0)
    width = GROUP * ROWS2
    q2 = head_stack(first_view(block, query_helpers(width)), first_mask)
    g2 = head_stack(second_view(block, jnp.zeros((width, SIDE), BF)), second_mask)
    flat = level_stats((keys[...],), (values[...],), q2, g2)
    level2 = [jnp.concatenate([x[:, h * width : (h + 1) * width] for h in range(HEADS)], axis=0) for x in flat]
    small = [summed_terms(tails, at + ROWS2) for at in starts]
    early1 = jnp.concatenate([x[:, :ROWS1] for x in small], axis=1)
    early2 = jnp.concatenate([x[:, ROWS1:ROWS] for x in small], axis=1)
    early0 = [
        sum(tails[at + 16 * i : at + 16 * (i + 1), :LANES].astype(F32) for i in range(2, 5)) for at in (0, TAIL)
    ]
    early = jnp.concatenate([early1, *early0], axis=1)
    total_rows = GROUP * ROWS1 + 2 * TOKENS
    shape = (width, total_rows)
    lane = iota(shape, 1)
    row = iota(shape, 0)
    ring = lane < GROUP * ROWS1
    inside = (lane - GROUP * ROWS1) & (TOKENS - 1)
    where0 = jnp.where(inside < HALF, 2 * inside, 2 * (inside - HALF) + 1)
    shard = jnp.where(ring, lane >> 6, (lane - GROUP * ROWS1) >> 8)
    same = shard == (row >> 4)
    head = lax.axis_index("head") * HEADS
    spread2 = []
    for h in range(HEADS):
        place = jnp.where(ring, MID * (lane & (ROWS1 - 1)) + offsets[0, head + h], where0)
        hit = same & (place == TOP * (row & (ROWS2 - 1)) + offsets[1, head + h])
        one_hot = jnp.where(hit, 1.0, 0.0).astype(BF)
        values_h = jnp.concatenate([x[h : h + 1] for x in level2] + [jnp.ones((1, width), F32)], axis=0)
        spread2.append(sum(nn(term, one_hot) for term in split3(values_h)))
    late = [jnp.concatenate([x[i : i + 1] for x in spread2], axis=0) for i in range(4)]
    late[0] = jnp.where(late[3] > 0.5, late[0], -BIG)
    first = merged(((early[0:4], early[4:8], early[8:12]), late[:3]))
    second = merged(((early2[0:4], early2[4:8], early2[8:12]), level2))
    top, total, dot = (jnp.concatenate([x, y], axis=1) for x, y in zip(first, second))
    grad_dot = dot / total
    log_total = top + jnp.log(total) * ROOT
    count = total_rows + width
    columns = jnp.concatenate(
        [x.astype(F32) for x in (*split3(log_total), *split3(grad_dot))]
        + [jnp.ones((HEADS, count), F32), jnp.zeros((HEADS, count), F32)],
        axis=0,
    )
    at = iota((8 * HEADS, SIDE), 0)
    s, h = at >> 2, at & 3
    slot = jnp.where(s < 3, s, jnp.where(s < 6, s + 1, jnp.where(s == 6, 3, 7)))
    place = jnp.where((iota((8 * HEADS, SIDE), 1) & 63) == 8 * h + slot, 1.0, 0.0).astype(BF)
    full = nn(columns.T.astype(BF), place).astype(BF)
    st[...] = full
    wide = jnp.concatenate([block, full[total_rows:]], axis=1)
    for n in range(GROUP):
        packed[n] = wide


def scatter_rows(offsets, parts1, parts2, shift):
    def mask(h, shape):
        lane = iota(shape, 1) - shift
        return (lane >= HEAD * h) & (lane < HEAD * (h + 1))

    total = None
    for level, part, rows in ((0, parts1, ROWS1), (1, parts2, ROWS2)):
        if part is None:
            continue
        place = jnp.concatenate(
            [jnp.where(chosen(offsets, level, h, (TOKENS, rows), 1), 1.0, 0.0) for h in range(HEADS)], axis=1
        ).astype(BF)
        part = jnp.concatenate(
            [jnp.where(mask(h, (rows, LANES)), part[h * rows : (h + 1) * rows], 0.0) for h in range(HEADS)], axis=0
        )
        high = part.astype(BF)
        low = (part - high.astype(F32)).astype(BF)
        got = nn(place, high) + nn(place, low)
        total = got if total is None else total + got
    return total


def grad_query_kernel(offsets, counts, qg, qg_top, st, kv, kvp, rows1, rows2, dq, kv1, keys2, values2):
    seq = lax.axis_index("seq")
    fill_level1(offsets, counts, rows1, kv1)
    fill_level2(offsets, counts, rows2, keys2, values2)
    own = key_helpers(full_mask(counts[seq]))
    other = key_helpers(full_mask(counts[seq ^ 1]))
    keys = (first_view(kv[...], own), first_view(kvp[...], other))
    values = (second_view(kv[...], own), second_view(kvp[...], other))

    def back(queries, grads, keys, values):
        total = None
        for kk, vv in zip(keys, values):
            weight = jnp.exp2(nt(queries, kk) * EXP2)
            score = (weight * nt(grads, vv)).astype(BF)
            part = nn(score, kk)
            total = part if total is None else total + part
        return total

    flat = qg[:TOKENS]
    mine = st[OWN : OWN + TOKENS]
    queries, grads = first_view(flat, mine), second_view(flat, mine)
    total = jnp.zeros((TOKENS, LANES), F32)
    for h in range(HEADS):
        q_mask = first_mask(h, (1, LANES)).astype(BF)
        g_mask = second_mask(h, (1, LANES)).astype(BF)
        part = back(queries * q_mask, grads * g_mask, keys, values)
        total = jnp.where(feature_mask(h, (TOKENS, LANES)), part, total)
    got = []
    for block, at, ks, vs in (
        (qg[TOKENS:], 0, kv1[0], kv1[1]),
        (qg_top[...], OWN + 2 * TOKENS, keys2[...], values2[...]),
    ):
        helpers = st[at : at + block.shape[0]]
        qs = head_stack(first_view(block, helpers), first_mask)
        gs = head_stack(second_view(block, helpers), second_mask)
        got.append(back(qs, gs, (ks,), (vs,)))
    total = (total + scatter_rows(offsets, got[0], got[1], 0)) * SCALE
    dq[...] = to_paired(total)


def key_back(keys, values, queries, grads):
    total_k = total_v = None
    for qq, gg in zip(queries, grads):
        weight = jnp.exp2(nt(keys, qq) * EXP2)
        score = (weight * nt(values, gg)).astype(BF)
        part_k = nn(score, qq)
        part_v = nn(weight.astype(BF), gg)
        total_k = part_k if total_k is None else total_k + part_k
        total_v = part_v if total_v is None else total_v + part_v
    return total_k, total_v


def grad_key_kernel(offsets, counts, kv, copies, qg, st, qgp, qg2, qg4, qg6, dk, dv, qs, gs):
    seq = lax.axis_index("seq")
    sources = ((qg, TOKENS), (qgp, TOKENS), *((ref, at) for ref in (qg2, qg4, qg6) for at in (0, ROWS1)))
    for i, (ref, at) in enumerate(sources):
        block = ref[at : at + ROWS1]
        helpers = st[i * ROWS1 : (i + 1) * ROWS1]
        qs[i * ROWS1 : (i + 1) * ROWS1] = first_view(block, helpers)
        gs[i * ROWS1 : (i + 1) * ROWS1] = second_view(block, helpers)
    own = key_helpers(full_mask(counts[seq]))
    keys, values = first_view(kv[...], own), second_view(kv[...], own)
    flat, other = qg[:TOKENS], qgp[:TOKENS]
    mine, next_st = st[OWN : OWN + TOKENS], st[OWN + TOKENS : OWN + 2 * TOKENS]
    queries = (first_view(flat, mine), first_view(other, next_st))
    grads = (second_view(flat, mine), second_view(other, next_st))
    total_k = jnp.zeros((TOKENS, LANES), F32)
    total_v = jnp.zeros((TOKENS, LANES), F32)
    for h in range(HEADS):
        k_mask = first_mask(h, (1, LANES)).astype(BF)
        v_mask = second_mask(h, (1, LANES)).astype(BF)
        part_k, part_v = key_back(keys * k_mask, values * v_mask, queries, grads)
        total_k = jnp.where(feature_mask(h, (TOKENS, LANES)), part_k, total_k)
        total_v = jnp.where(second_mask(h, (TOKENS, LANES)), part_v, total_v)
    helpers = key_helpers(dilated_mask(offsets, 0, counts[seq]))
    block = copies[0, :ROWS1]
    k1 = head_stack(first_view(block, helpers), first_mask)
    v1 = head_stack(second_view(block, helpers), second_mask)
    k1_part, v1_part = key_back(k1, v1, (qs[...],), (gs[...],))
    dk[...] = total_k + scatter_rows(offsets, k1_part, None, 0)
    dv[...] = total_v + scatter_rows(offsets, v1_part, None, LANES - FEAT)


def last_kernel(offsets, counts, rows, qg2, dk_in, dv_in, dk, dv):
    seq = lax.axis_index("seq")
    full = qg2[...].reshape(GROUP * GROUP * ROWS2, PAIR + SIDE)
    helpers = full[:, PAIR:]
    queries, grads = first_view(full[:, :PAIR], helpers), second_view(full[:, :PAIR], helpers)
    mine = key_helpers(dilated_mask(offsets, 1, counts[seq]))
    block = rows[0, ROWS1:]
    k2 = head_stack(first_view(block, mine), first_mask)
    v2 = head_stack(second_view(block, mine), second_mask)
    k2_part, v2_part = key_back(k2, v2, (queries,), (grads,))
    total_k = (dk_in[...] + scatter_rows(offsets, None, k2_part, 0)) * SCALE
    total_v = dv_in[...] + scatter_rows(offsets, None, v2_part, LANES - FEAT)
    dk[...] = to_paired(total_k)
    dv[...] = to_paired(total_v[:, LANES - FEAT :])


def call(kernel, outs, n_smem, *args, scratch=()):
    return pl.pallas_call(
        kernel,
        out_shape=[jax.ShapeDtypeStruct(s, d) for s, d in outs],
        in_specs=[SMEM] * n_smem + [VMEM] * (len(args) - n_smem),
        out_specs=[VMEM] * len(outs),
        scratch_shapes=[pltpu.VMEM(s, BF) for s in scratch],
        compiler_params=pltpu.CompilerParams(vmem_limit_bytes=VMEM_BYTES),
    )(*args)


def per_device(queries, keys, values, grad_y, out_weight, counts, offsets):
    n_seq = lax.axis_size("seq")
    rings = [[GROUP * b + i for i in range(GROUP)] for b in range(n_seq // GROUP)]
    planes = [[GROUP * b + i for b in range(n_seq // GROUP)] for i in range(GROUP)]

    def swap(x, bits):
        return lax.ppermute(x, "seq", [(i, i ^ bits) for i in range(n_seq)])

    def shift(x, step):
        return lax.ppermute(x, "seq", [(r[i], r[(i + step) % GROUP]) for r in rings for i in range(GROUP)])

    def exchange(copies, groups):
        return lax.all_to_all(copies, "seq", 0, 0, axis_index_groups=groups)

    def far(own, near):
        both = jnp.concatenate([own, near], axis=0)
        return tuple(shift(both, step) for step in (2, 4, 6))

    k_next, v_next = swap(keys, 1), swap(values, 1)
    (copies,) = call(rows_kernel, [((GROUP, ROWS, PAIR), BF)], 1, offsets, keys, values)
    copies, k_next, v_next = lax.optimization_barrier((copies, k_next, v_next))
    ring_kv = exchange(copies, rings)
    flat = (TOKENS, PAIR)
    kv, kvp = call(pairs_kernel, [(flat, BF)] * 2, 0, keys, values, k_next, v_next)
    gy = lax.all_gather(grad_y, "head", axis=0)
    qg, qg_top = call(
        proj_kernel, [((TOKENS + ROWS1, PAIR), BF), ((ROWS2, PAIR), BF)], 2, offsets, counts, gy, out_weight, queries
    )
    qgp = swap(qg, 1)
    (tail,) = call(
        forward_kernel, [((TAIL, PAIR), BF)], 2, offsets, counts, qg, qg_top, kv, kvp, ring_kv,
        scratch=[(2, GROUP * ROWS1, LANES)],
    )
    ring_kv, tail = lax.optimization_barrier((ring_kv, tail))
    tail_next = swap(tail, 1)
    (repeated,) = call(repeat_kernel, [((GROUP, GROUP * ROWS2, PAIR), BF)], 0, ring_kv)
    all_kv = exchange(repeated, planes)
    tails = far(tail[: 2 * ROWS2], tail_next[: 2 * ROWS2])
    tails, qgp = lax.optimization_barrier((jnp.concatenate([tail, tail_next, *tails], axis=0), qgp))
    big = (GROUP * GROUP * ROWS2, LANES)
    st_rows = OWN + 2 * TOKENS + GROUP * ROWS2
    st, packed = call(
        finish_kernel, [((st_rows, SIDE), BF), ((GROUP, GROUP * ROWS2, PAIR + SIDE), BF)], 2, offsets, counts,
        tails, all_kv, scratch=[big, big],
    )
    qgs = far(qg[TOKENS:], qgp[TOKENS:])
    all_qg = exchange(packed, planes)
    (dq,) = call(
        grad_query_kernel, [((HALF, PAIR), BF)], 2, offsets, counts, qg, qg_top, st, kv, kvp, ring_kv, all_kv,
        scratch=[(2, GROUP * ROWS1, LANES), big, big],
    )
    dk, dv = call(
        grad_key_kernel, [((TOKENS, LANES), F32)] * 2, 2, offsets, counts, kv, copies, qg, st, qgp, *qgs,
        scratch=[(GROUP * ROWS1, LANES)] * 2,
    )
    dk, dv = call(last_kernel, [((HALF, PAIR), BF)] * 2, 2, offsets, counts, copies, all_qg, dk, dv)
    return dq, dk, dv


def solution(mesh):
    split = P("seq", "head")
    return jax.shard_map(
        per_device,
        mesh=mesh,
        in_specs=(split, split, split, split, P("head", None), P(), P()),
        out_specs=(split, split, split),
        check_vma=False,
    )
```

time: 119 us -> 87.7 us (0.74)
  blocking collectives: 72.1 us -> 8.29 us
  starting transfers between devices: 14.6 us -> 37.1 us
  waiting for transfers between devices: 0.02 us -> 17.2 us
  local copies, waits for them, and re-layouts: 14.4 us -> 4.21 us
  Pallas kernels: 16.2 us -> 19.7 us
    all_to_all x2 -> x0, blocking collectives: 52 us -> none  [ring(): lax.all_to_all(copies, 'seq', 0, 0, axis_index_groups=rings)]
    ppermute x4 -> x10, starting transfers between devices: 4.05 us -> 17.2 us  [the longest x6 13.1 us: shift(): lax.ppermute(x, 'seq', [(r[i], r[(i + step) % GROUP]) for r in rings for...]
    ppermute x4 -> x10, waiting for transfers between devices: 0.01 us -> 12.1 us  [the longest x6 6.67 us: shift(): lax.ppermute(x, 'seq', [(r[i], r[(i + step) % GROUP]) for r in rings for...]
    all_gather x1, blocking collectives: 20.1 us -> 8.29 us  [per_device(): gy = lax.all_gather(grad_y, 'head', axis=0)]
    all_to_all x2 -> x3, starting transfers between devices: 10.5 us -> 19.8 us  [exchange(): return lax.all_to_all(copies, 'seq', 0, 0, axis_index_groups=groups)]
    all_to_all x2 -> x3, waiting for transfers between devices: 0.01 us -> 5.04 us  [exchange(): return lax.all_to_all(copies, 'seq', 0, 0, axis_index_groups=groups)]
    pallas_call x5 -> x9, Pallas kernels: 16.2 us -> 19.7 us  [call(): pl.pallas_call(kernel, out_shape=[jax.ShapeDtypeStruct(s, d) for s, d in...]
    slice x8 -> x4, local copies, waits for them, and re-layouts: 3.51 us -> 0.02 us  [the longest x2 0.01 us: per_device(): qgs = far(qg[TOKENS:], qgp[TOKENS:])]
  transfers between devices with their start and end apart: 6 -> 13, of which waited for: 0 -> 8; matrix products, arithmetic and copies ran while one was open for 3% -> 0% of each run, Pallas kernels for 5% -> 12%
where the time goes in v2:
time: 87.7 us; the launch traced here: 87.2 us
  starting transfers between devices  37.1 us (42%)
  Pallas kernels  19.7 us (22%)
  waiting for transfers between devices  17.2 us (20%)
  blocking collectives  8.29 us (9%)
  local copies, waits for them, and re-layouts  4.21 us (5%)
    all_to_all x3, starting transfers between devices, exchange(): return lax.all_to_all(copies, 'seq', 0, 0, axis_index_groups=groups)  19.8 us
    pallas_call x9, Pallas kernels, call(): pl.pallas_call(kernel, out_shape=[jax.ShapeDtypeStruct(s, d) for s, d in...  19.7 us
    ppermute x6, starting transfers between devices, shift(): lax.ppermute(x, 'seq', [(r[i], r[(i + step) % GROUP]) for r in rings for...  13.1 us
    all_gather x1, blocking collectives, per_device(): gy = lax.all_gather(grad_y, 'head', axis=0)  8.29 us
    ppermute x6, waiting for transfers between devices, shift(): lax.ppermute(x, 'seq', [(r[i], r[(i + step) % GROUP]) for r in rings for...  6.67 us
    ppermute x4, waiting for transfers between devices, swap(): return lax.ppermute(x, 'seq', [(i, i ^ bits) for i in range(n_seq)])  5.44 us
    all_to_all x3, waiting for transfers between devices, exchange(): return lax.all_to_all(copies, 'seq', 0, 0, axis_index_groups=groups)  5.04 us
    unnamed x26, local copies, waits for them, and re-layouts  4.18 us
  transfers between devices with their start and end apart: 13, of which 8 were waited for; matrix products, arithmetic and copies ran while one was open for 0% of the time, Pallas kernels for 12%

profile of v2, /device:TPU:2, one launch (start us, length us, event | category | flops | bytes accessed | tf_op | source)
XLA Modules:
  0.0 87.2 jit_solution(14450677938412108687)
XLA Ops:
  0.6 2.0 %collective-permute-start = (bf16[128,384]{1,0:T(8,128)(2,1)}, bf16[128,384]{1,0:T(8,128)(2,1)S(1)}, u32[]{:S(2)}, u32[]{:S(2)}) collective-permute-start(bf16[128,384]{1,0:T(8,128)(2,1)} %k.3), channel_id=1, source_target_pairs={{0,4},{4,0},{8,12},{12,8},{16,20},{20,16},{24,28},{28,24},{32,36},... | collective-permute-start | bytes 294920 | tf_op jit(solution)/shard_map/ppermute | solution.py:519
  2.6 0.1 collective-permute-start.1
  2.7 0.0 copy-start.1
  2.7 0.9 %copy-done.1 = bf16[128,384]{1,0:T(8,128)(2,1)S(1)} copy-done((bf16[128,384]{1,0:T(8,128)(2,1)S(1)}, bf16[128,384]{1,0:T(8,128)(2,1)}, u32[]{:S(2)}) %copy-start.1) | copy-done | bytes 98328
  3.6 0.0 copy-start.3
  3.6 0.9 %copy-done.3 = bf16[128,384]{1,0:T(8,128)(2,1)S(1)} copy-done((bf16[128,384]{1,0:T(8,128)(2,1)S(1)}, bf16[128,384]{1,0:T(8,128)(2,1)}, u32[]{:S(2)}) %copy-start.3) | copy-done | bytes 98328
  4.5 0.0 copy-start.7
  4.5 0.7 copy-done.7
  5.2 1.9 %shard_map.95.copies.rows = bf16[8,80,384]{2,1,0:T(8,128)(2,1)} custom-call(s32[2,16]{1,0:T(2,128)S(1)} %copy-done.7, bf16[128,384]{1,0:T(8,128)(2,1)S(1)} %copy-done.1, bf16[128,384]{1,0:T(8,128)(2,1)S(1)} %copy-done.3), custom_call_target="tpu_custom_call" | custom-call | tf_op jit(solution)/shard_map/pallas_call | solution.py:503
  7.1 0.0 copy-start.10
  7.1 0.0 collective-permute-done.k_next
  7.1 0.6 collective-permute-done.1.v_next
  7.7 8.3 %all-to-all-start = ((bf16[8,80,384]{2,1,0:T(8,128)(2,1)}), bf16[8,80,384]{2,1,0:T(8,128)(2,1)S(1)}, u32[]{:S(2)}, u32[]{:S(2)}) async-start(bf16[8,80,384]{2,1,0:T(8,128)(2,1)} %shard_map.95.copies.rows), calls=%async_computation | async-start | bytes 983040 | tf_op jit(solution)/shard_map/all_to_all | solution.py:525
  16.0 0.0 copy-done.10
  16.0 0.0 copy-start.5
  16.1 0.0 copy-start.6
  16.1 8.3 %all-gather = bf16[512,384]{1,0:T(8,128)(2,1)S(1)} all-gather(bf16[128,384]{1,0:T(8,128)(2,1)S(1)} %copy-done.10), channel_id=2, replica_groups=mesh['seq'=64,'head'=4] {'head'}, dimensions={0}, use_global_device_ids=true | all-gather | bytes 491520 | tf_op jit(solution)/shard_map/all_gather | solution.py:537
  24.4 0.0 copy-start.8
  24.4 0.0 copy-start.9
  24.4 0.0 copy-done.5
  24.4 0.0 copy-done.6
  24.4 0.7 copy-done.8
  25.0 0.0 copy-done.9
  25.0 0.0 copy-start.2
  25.0 0.0 copy-start.4
  25.0 1.4 %shard_map.94 = (bf16[320,384]{1,0:T(8,128)(2,1)S(1)}, bf16[16,384]{1,0:T(8,128)(2,1)S(1)}) custom-call(s32[2,16]{1,0:T(2,128)S(1)} %copy-done.8, s32[64]{0:T(128)S(1)} %copy-done.9, bf16[4,128,384]{2,1,0:T(8,128)(2,1)S(1)} %bitcast.1, bf16[192,768]{1,0:T(8,128)(2,1)S(1)} %copy-done.5, bf16[128,384]{1,0:T(8,128)(2,1)S(1)} %copy-done.6), custom_call_target="tpu_custom_call" | custom-call | tf_op jit(solution)/shard_map/pallas_call | solution.py:503
  26.4 0.0 copy-done.2
  26.5 0.0 copy-done.4
  26.5 0.4 shard_map.96
  26.9 5.0 %all-to-all-done.rows.rows1 = bf16[8,80,384]{2,1,0:T(8,128)(2,1)S(1)} async-done(((bf16[8,80,384]{2,1,0:T(8,128)(2,1)}), bf16[8,80,384]{2,1,0:T(8,128)(2,1)S(1)}, u32[]{:S(2)}, u32[]{:S(2)}) %all-to-all-start) | async-done | bytes 491552 | tf_op jit(solution)/shard_map/all_to_all | solution.py:525
  32.0 2.6 %shard_map.97 = bf16[80,384]{1,0:T(8,128)(2,1)S(1)} custom-call(s32[2,16]{1,0:T(2,128)S(1)} %copy-done.8, s32[64]{0:T(128)S(1)} %copy-done.9, bf16[320,384]{1,0:T(8,128)(2,1)S(1)} %get-tuple-element.20.qg, bf16[16,384]{1,0:T(8,128)(2,1)S(1)} %get-tuple-element.21.qg_top, bf16[256,384]{1,0:T(8,128)(2,1)S(1)} %get-tuple-element.25.kv, ...), custom_call_target="tpu_custom_call" | custom-call | tf_op jit(solution)/shard_map/pallas_call | solution.py:503
  34.5 1.0 %shard_map.98 = bf16[8,128,384]{2,1,0:T(8,128)(2,1)} custom-call(bf16[8,80,384]{2,1,0:T(8,128)(2,1)S(1)} %all-to-all-done.rows.rows1), custom_call_target="tpu_custom_call" | custom-call | tf_op jit(solution)/shard_map/pallas_call | solution.py:503
  35.5 5.8 %all-to-all-start.1 = ((bf16[8,128,384]{2,1,0:T(8,128)(2,1)}), bf16[8,128,384]{2,1,0:T(8,128)(2,1)S(1)}, u32[]{:S(2)}, u32[]{:S(2)}) async-start(bf16[8,128,384]{2,1,0:T(8,128)(2,1)} %shard_map.98), calls=%async_computation.1 | async-start | bytes 1572864 | tf_op jit(solution)/shard_map/all_to_all | solution.py:525
  41.4 0.6 collective-permute-start.6
  41.9 1.5 %collective-permute-start.2 = (bf16[80,384]{1,0:T(8,128)(2,1)S(1)}, bf16[80,384]{1,0:T(8,128)(2,1)S(1)}, u32[]{:S(2)}, u32[]{:S(2)}) collective-permute-start(bf16[80,384]{1,0:T(8,128)(2,1)S(1)} %shard_map.97), channel_id=1, source_target_pairs={{0,4},{4,0},{8,12},{12,8},{16,20},{20,16},{24,28},{28,24},{32,36},... | collective-permute-start | bytes 184328 | tf_op jit(solution)/shard_map/ppermute | solution.py:519
  43.4 4.8 %collective-permute-done.2 = bf16[80,384]{1,0:T(8,128)(2,1)S(1)} collective-permute-done((bf16[80,384]{1,0:T(8,128)(2,1)S(1)}, bf16[80,384]{1,0:T(8,128)(2,1)S(1)}, u32[]{:S(2)}, u32[]{:S(2)}) %collective-permute-start.2) | collective-permute-done | bytes 61472 | tf_op jit(solution)/shard_map/ppermute | solution.py:519
  48.2 0.1 collective-permute-start.3
  48.3 3.5 %collective-permute-start.4 = (bf16[64,384]{1,0:T(8,128)(2,1)S(1)}, bf16[64,384]{1,0:T(8,128)(2,1)S(1)}, u32[]{:S(2)}, u32[]{:S(2)}) collective-permute-start(bf16[64,384]{1,0:T(8,128)(2,1)S(1)} %pad_maximum_fusion.1), channel_id=1, source_target_pairs={{0,16},{4,20},{8,24},{12,28},{16,0},{20,4},{24,8},{28,12},{32,48},... | collective-permute-start | bytes 147464 | tf_op jit(solution)/shard_map/ppermute | solution.py:522
  51.8 3.1 %collective-permute-start.5 = (bf16[64,384]{1,0:T(8,128)(2,1)S(1)}, bf16[64,384]{1,0:T(8,128)(2,1)S(1)}, u32[]{:S(2)}, u32[]{:S(2)}) collective-permute-start(bf16[64,384]{1,0:T(8,128)(2,1)S(1)} %pad_maximum_fusion.1), channel_id=1, source_target_pairs={{0,24},{4,28},{8,0},{12,4},{16,8},{20,12},{24,16},{28,20},{32,56},... | collective-permute-start | bytes 147464 | tf_op jit(solution)/shard_map/ppermute | solution.py:522
  54.9 0.1 collective-permute-done.3
  55.1 1.3 %collective-permute-done.4 = bf16[64,384]{1,0:T(8,128)(2,1)S(1)} collective-permute-done((bf16[64,384]{1,0:T(8,128)(2,1)S(1)}, bf16[64,384]{1,0:T(8,128)(2,1)S(1)}, u32[]{:S(2)}, u32[]{:S(2)}) %collective-permute-start.4) | collective-permute-done | bytes 49184 | tf_op jit(solution)/shard_map/ppermute | solution.py:522
  56.4 2.0 %collective-permute-done.5 = bf16[64,384]{1,0:T(8,128)(2,1)S(1)} collective-permute-done((bf16[64,384]{1,0:T(8,128)(2,1)S(1)}, bf16[64,384]{1,0:T(8,128)(2,1)S(1)}, u32[]{:S(2)}, u32[]{:S(2)}) %collective-permute-start.5) | collective-permute-done | bytes 49184 | tf_op jit(solution)/shard_map/ppermute | solution.py:522
  58.5 0.0 collective-permute-done.6.qgp
  58.5 0.0 all-to-all-done.1.rows.rows2
  58.5 2.7 %shard_map.99 = (bf16[1152,128]{1,0:T(8,128)(2,1)S(1)}, bf16[8,128,512]{2,1,0:T(8,128)(2,1)S(1)}) custom-call(s32[2,16]{1,0:T(2,128)S(1)} %copy-done.8, s32[64]{0:T(128)S(1)} %copy-done.9, bf16[352,384]{1,0:T(8,128)(2,1)S(1)} %constant_dynamic-update-slice_fusion.tails, bf16[8,128,384]{2,1,0:T(8,128)(2,1)S(1)} %all-to-all-done.1.rows.rows2), custom_call_target="tpu_custom_call" | custom-call | tf_op jit(solution)/shard_map/pallas_call | solution.py:503
  61.2 0.0 copy-start
  61.2 1.0 %copy-done = bf16[8,128,512]{2,1,0:T(8,128)(2,1)} copy-done((bf16[8,128,512]{2,1,0:T(8,128)(2,1)}, bf16[8,128,512]{2,1,0:T(8,128)(2,1)S(1)}, u32[]{:S(2)}) %copy-start) | copy-done | bytes 1048600
  62.2 5.7 %all-to-all-start.2 = ((bf16[8,128,512]{2,1,0:T(8,128)(2,1)}), bf16[8,128,512]{2,1,0:T(8,128)(2,1)S(1)}, u32[]{:S(2)}, u32[]{:S(2)}) async-start(bf16[8,128,512]{2,1,0:T(8,128)(2,1)} %copy-done), calls=%async_computation.2 | async-start | bytes 2097152 | tf_op jit(solution)/shard_map/all_to_all | solution.py:525
  68.0 2.6 %collective-permute-start.7 = (bf16[128,384]{1,0:T(8,128)(2,1)S(1)}, bf16[128,384]{1,0:T(8,128)(2,1)S(1)}, u32[]{:S(2)}, u32[]{:S(2)}) collective-permute-start(bf16[128,384]{1,0:T(8,128)(2,1)S(1)} %pad_maximum_fusion), channel_id=1, source_target_pairs={{0,8},{4,12},{8,16},{12,20},{16,24},{20,28},{24,0},{28,4},{32,40},... | collective-permute-start | bytes 294920 | tf_op jit(solution)/shard_map/ppermute | solution.py:522
  70.6 3.4 %collective-permute-start.8 = (bf16[128,384]{1,0:T(8,128)(2,1)S(1)}, bf16[128,384]{1,0:T(8,128)(2,1)S(1)}, u32[]{:S(2)}, u32[]{:S(2)}) collective-permute-start(bf16[128,384]{1,0:T(8,128)(2,1)S(1)} %pad_maximum_fusion), channel_id=1, source_target_pairs={{0,16},{4,20},{8,24},{12,28},{16,0},{20,4},{24,8},{28,12},{32,48},... | collective-permute-start | bytes 294920 | tf_op jit(solution)/shard_map/ppermute | solution.py:522
  74.0 0.4 collective-permute-start.9
  74.4 3.6 %shard_map.100 = bf16[128,384]{1,0:T(8,128)(2,1)} custom-call(s32[2,16]{1,0:T(2,128)S(1)} %copy-done.8, s32[64]{0:T(128)S(1)} %copy-done.9, bf16[320,384]{1,0:T(8,128)(2,1)S(1)} %get-tuple-element.20.qg, bf16[16,384]{1,0:T(8,128)(2,1)S(1)} %get-tuple-element.21.qg_top, bf16[1152,128]{1,0:T(8,128)(2,1)S(1)} %get-tuple-element.30.st, ...), custom_call_target="tpu_custom_call" | custom-call | tf_op jit(solution)/shard_map/pallas_call | solution.py:503
  78.0 0.0 collective-permute-done.7.qg2
  78.0 1.1 %collective-permute-done.8.qg4 = bf16[128,384]{1,0:T(8,128)(2,1)S(1)} collective-permute-done((bf16[128,384]{1,0:T(8,128)(2,1)S(1)}, bf16[128,384]{1,0:T(8,128)(2,1)S(1)}, u32[]{:S(2)}, u32[]{:S(2)}) %collective-permute-start.8) | collective-permute-done | bytes 98336 | tf_op jit(solution)/shard_map/ppermute | solution.py:522
  79.1 2.1 %collective-permute-done.9.qg6 = bf16[128,384]{1,0:T(8,128)(2,1)S(1)} collective-permute-done((bf16[128,384]{1,0:T(8,128)(2,1)S(1)}, bf16[128,384]{1,0:T(8,128)(2,1)S(1)}, u32[]{:S(2)}, u32[]{:S(2)}) %collective-permute-start.9) | collective-permute-done | bytes 98336 | tf_op jit(solution)/shard_map/ppermute | solution.py:522
  81.2 3.3 %shard_map.101 = (f32[256,256]{1,0:T(8,128)S(1)}, f32[256,256]{1,0:T(8,128)S(1)}) custom-call(s32[2,16]{1,0:T(2,128)S(1)} %copy-done.8, s32[64]{0:T(128)S(1)} %copy-done.9, bf16[256,384]{1,0:T(8,128)(2,1)S(1)} %get-tuple-element.25.kv, bf16[8,80,384]{2,1,0:T(8,128)(2,1)} %shard_map.95.copies.rows, bf16[320,384]{1,0:T(8,128)(2,1)S(1)} %get-tuple-element.20.qg, ...), custom_call_target="tpu_custom_call" | custom-call | tf_op jit(solution)/shard_map/pallas_call | solution.py:503
  84.5 0.0 all-to-all-done.2.qg2
  84.5 2.7 %shard_map.102 = (bf16[128,384]{1,0:T(8,128)(2,1)}, bf16[128,384]{1,0:T(8,128)(2,1)}) custom-call(s32[2,16]{1,0:T(2,128)S(1)} %copy-done.8, s32[64]{0:T(128)S(1)} %copy-done.9, bf16[8,80,384]{2,1,0:T(8,128)(2,1)} %shard_map.95.copies.rows, bf16[8,128,512]{2,1,0:T(8,128)(2,1)S(1)} %all-to-all-done.2.qg2, f32[256,256]{1,0:T(8,128)S(1)} %get-tuple-element.33.dk_in, ...), custom_call_target="tpu_custom_call" | custom-call | tf_op jit(solution)/shard_map/pallas_call | solution.py:503
  (11 shorter events, 0.1 us)
Async XLA Ops:
  0.6 6.5 %collective-permute-start = (bf16[128,384]{1,0:T(8,128)(2,1)}, bf16[128,384]{1,0:T(8,128)(2,1)S(1)}, u32[]{:S(2)}, u32[]{:S(2)}) collective-permute-start(bf16[128,384]{1,0:T(8,128)(2,1)} %k.3), channel_id=1, source_target_pairs={{0,4},{4,0},{8,12},{12,8},{16,20},{20,16},{24,28},{28,24},{32,36},... | collective-permute-start | bytes 294920 | tf_op jit(solution)/shard_map/ppermute | solution.py:519
  2.6 5.1 %collective-permute-start.1 = (bf16[128,384]{1,0:T(8,128)(2,1)}, bf16[128,384]{1,0:T(8,128)(2,1)S(1)}, u32[]{:S(2)}, u32[]{:S(2)}) collective-permute-start(bf16[128,384]{1,0:T(8,128)(2,1)} %v.3), channel_id=1, source_target_pairs={{0,4},{4,0},{8,12},{12,8},{16,20},{20,16},{24,28},{28,24},{32,36},... | collective-permute-start | bytes 294920 | tf_op jit(solution)/shard_map/ppermute | solution.py:519
  2.7 0.9 %copy-start.1 = (bf16[128,384]{1,0:T(8,128)(2,1)S(1)}, bf16[128,384]{1,0:T(8,128)(2,1)}, u32[]{:S(2)}) copy-start(bf16[128,384]{1,0:T(8,128)(2,1)} %k.3) | copy-start | bytes 294916
  3.6 0.9 %copy-start.3 = (bf16[128,384]{1,0:T(8,128)(2,1)S(1)}, bf16[128,384]{1,0:T(8,128)(2,1)}, u32[]{:S(2)}) copy-start(bf16[128,384]{1,0:T(8,128)(2,1)} %v.3) | copy-start | bytes 294916
  4.5 0.7 copy-start.7
  7.1 8.9 %copy-start.10 = (bf16[128,384]{1,0:T(8,128)(2,1)S(1)}, bf16[128,384]{1,0:T(8,128)(2,1)}, u32[]{:S(2)}) copy-start(bf16[128,384]{1,0:T(8,128)(2,1)} %param.10) | copy-start | bytes 294916
  7.7 24.2 %all-to-all-start = ((bf16[8,80,384]{2,1,0:T(8,128)(2,1)}), bf16[8,80,384]{2,1,0:T(8,128)(2,1)S(1)}, u32[]{:S(2)}, u32[]{:S(2)}) async-start(bf16[8,80,384]{2,1,0:T(8,128)(2,1)} %shard_map.95.copies.rows), calls=%async_computation | async-start | bytes 983040 | tf_op jit(solution)/shard_map/all_to_all | solution.py:525
  16.0 8.3 %copy-start.5 = (bf16[192,768]{1,0:T(8,128)(2,1)S(1)}, bf16[192,768]{1,0:T(8,128)(2,1)}, u32[]{:S(2)}) copy-start(bf16[192,768]{1,0:T(8,128)(2,1)} %w.1) | copy-start | bytes 884740
  16.1 8.3 %copy-start.6 = (bf16[128,384]{1,0:T(8,128)(2,1)S(1)}, bf16[128,384]{1,0:T(8,128)(2,1)}, u32[]{:S(2)}) copy-start(bf16[128,384]{1,0:T(8,128)(2,1)} %q.1) | copy-start | bytes 294916
  24.4 0.7 copy-start.8
  24.4 0.7 copy-start.9
  25.0 1.4 %copy-start.2 = (bf16[128,384]{1,0:T(8,128)(2,1)S(1)}, bf16[128,384]{1,0:T(8,128)(2,1)}, u32[]{:S(2)}) copy-start(bf16[128,384]{1,0:T(8,128)(2,1)} %k.3) | copy-start | bytes 294916
  25.0 1.4 %copy-start.4 = (bf16[128,384]{1,0:T(8,128)(2,1)S(1)}, bf16[128,384]{1,0:T(8,128)(2,1)}, u32[]{:S(2)}) copy-start(bf16[128,384]{1,0:T(8,128)(2,1)} %v.3) | copy-start | bytes 294916
  35.5 23.0 %all-to-all-start.1 = ((bf16[8,128,384]{2,1,0:T(8,128)(2,1)}), bf16[8,128,384]{2,1,0:T(8,128)(2,1)S(1)}, u32[]{:S(2)}, u32[]{:S(2)}) async-start(bf16[8,128,384]{2,1,0:T(8,128)(2,1)} %shard_map.98), calls=%async_computation.1 | async-start | bytes 1572864 | tf_op jit(solution)/shard_map/all_to_all | solution.py:525
  41.4 17.1 %collective-permute-start.6 = (bf16[320,384]{1,0:T(8,128)(2,1)S(1)}, bf16[320,384]{1,0:T(8,128)(2,1)S(1)}, u32[]{:S(2)}, u32[]{:S(2)}) collective-permute-start(bf16[320,384]{1,0:T(8,128)(2,1)S(1)} %get-tuple-element.20.qg), channel_id=1, source_target_pairs={{0,4},{4,0},{8,12},{12,8},{16,20},{20,16},{24,28},{28,24},{32,36},... | collective-permute-start | bytes 737288 | tf_op jit(solution)/shard_map/ppermute | solution.py:519
  41.9 6.3 %collective-permute-start.2 = (bf16[80,384]{1,0:T(8,128)(2,1)S(1)}, bf16[80,384]{1,0:T(8,128)(2,1)S(1)}, u32[]{:S(2)}, u32[]{:S(2)}) collective-permute-start(bf16[80,384]{1,0:T(8,128)(2,1)S(1)} %shard_map.97), channel_id=1, source_target_pairs={{0,4},{4,0},{8,12},{12,8},{16,20},{20,16},{24,28},{28,24},{32,36},... | collective-permute-start | bytes 184328 | tf_op jit(solution)/shard_map/ppermute | solution.py:519
  48.2 6.8 %collective-permute-start.3 = (bf16[64,384]{1,0:T(8,128)(2,1)S(1)}, bf16[64,384]{1,0:T(8,128)(2,1)S(1)}, u32[]{:S(2)}, u32[]{:S(2)}) collective-permute-start(bf16[64,384]{1,0:T(8,128)(2,1)S(1)} %pad_maximum_fusion.1), channel_id=1, source_target_pairs={{0,8},{4,12},{8,16},{12,20},{16,24},{20,28},{24,0},{28,4},{32,40},... | collective-permute-start | bytes 147464 | tf_op jit(solution)/shard_map/ppermute | solution.py:522
  48.3 8.1 %collective-permute-start.4 = (bf16[64,384]{1,0:T(8,128)(2,1)S(1)}, bf16[64,384]{1,0:T(8,128)(2,1)S(1)}, u32[]{:S(2)}, u32[]{:S(2)}) collective-permute-start(bf16[64,384]{1,0:T(8,128)(2,1)S(1)} %pad_maximum_fusion.1), channel_id=1, source_target_pairs={{0,16},{4,20},{8,24},{12,28},{16,0},{20,4},{24,8},{28,12},{32,48},... | collective-permute-start | bytes 147464 | tf_op jit(solution)/shard_map/ppermute | solution.py:522
  51.8 6.7 %collective-permute-start.5 = (bf16[64,384]{1,0:T(8,128)(2,1)S(1)}, bf16[64,384]{1,0:T(8,128)(2,1)S(1)}, u32[]{:S(2)}, u32[]{:S(2)}) collective-permute-start(bf16[64,384]{1,0:T(8,128)(2,1)S(1)} %pad_maximum_fusion.1), channel_id=1, source_target_pairs={{0,24},{4,28},{8,0},{12,4},{16,8},{20,12},{24,16},{28,20},{32,56},... | collective-permute-start | bytes 147464 | tf_op jit(solution)/shard_map/ppermute | solution.py:522
  61.2 1.0 %copy-start = (bf16[8,128,512]{2,1,0:T(8,128)(2,1)}, bf16[8,128,512]{2,1,0:T(8,128)(2,1)S(1)}, u32[]{:S(2)}) copy-start(bf16[8,128,512]{2,1,0:T(8,128)(2,1)S(1)} %get-tuple-element.31) | copy-start | bytes 3145732
  62.2 22.3 %all-to-all-start.2 = ((bf16[8,128,512]{2,1,0:T(8,128)(2,1)}), bf16[8,128,512]{2,1,0:T(8,128)(2,1)S(1)}, u32[]{:S(2)}, u32[]{:S(2)}) async-start(bf16[8,128,512]{2,1,0:T(8,128)(2,1)} %copy-done), calls=%async_computation.2 | async-start | bytes 2097152 | tf_op jit(solution)/shard_map/all_to_all | solution.py:525
  68.0 10.1 %collective-permute-start.7 = (bf16[128,384]{1,0:T(8,128)(2,1)S(1)}, bf16[128,384]{1,0:T(8,128)(2,1)S(1)}, u32[]{:S(2)}, u32[]{:S(2)}) collective-permute-start(bf16[128,384]{1,0:T(8,128)(2,1)S(1)} %pad_maximum_fusion), channel_id=1, source_target_pairs={{0,8},{4,12},{8,16},{12,20},{16,24},{20,28},{24,0},{28,4},{32,40},... | collective-permute-start | bytes 294920 | tf_op jit(solution)/shard_map/ppermute | solution.py:522
  70.6 8.5 %collective-permute-start.8 = (bf16[128,384]{1,0:T(8,128)(2,1)S(1)}, bf16[128,384]{1,0:T(8,128)(2,1)S(1)}, u32[]{:S(2)}, u32[]{:S(2)}) collective-permute-start(bf16[128,384]{1,0:T(8,128)(2,1)S(1)} %pad_maximum_fusion), channel_id=1, source_target_pairs={{0,16},{4,20},{8,24},{12,28},{16,0},{20,4},{24,8},{28,12},{32,48},... | collective-permute-start | bytes 294920 | tf_op jit(solution)/shard_map/ppermute | solution.py:522
  74.0 7.2 %collective-permute-start.9 = (bf16[128,384]{1,0:T(8,128)(2,1)S(1)}, bf16[128,384]{1,0:T(8,128)(2,1)S(1)}, u32[]{:S(2)}, u32[]{:S(2)}) collective-permute-start(bf16[128,384]{1,0:T(8,128)(2,1)S(1)} %pad_maximum_fusion), channel_id=1, source_target_pairs={{0,24},{4,28},{8,0},{12,4},{16,8},{20,12},{24,16},{28,20},{32,56},... | collective-permute-start | bytes 294920 | tf_op jit(solution)/shard_map/ppermute | solution.py:522

commit v3 on v2

--- a/solution.py
+++ b/solution.py
@@ -119,11 +119,12 @@
 
 
 def to_paired(flat):
+    flat = flat.astype(BF)
     pieces = []
     for h in range(HEADS):
         for t in range(2):
             pieces.append(flat[t * HALF : (t + 1) * HALF, h * HEAD : (h + 1) * HEAD])
-    return jnp.concatenate(pieces, axis=1).astype(BF)
+    return jnp.concatenate(pieces, axis=1)
 
 
 def place_of(offsets, level, h, shape, dim):
@@ -191,7 +192,7 @@
 
 def pairs_kernel(k, v, k_next, v_next, kv, kv_next):
     for a, b, out in ((k, v, kv), (k_next, v_next, kv_next)):
-        out[...] = jnp.concatenate([by_parity(a[...].astype(F32)), by_parity(b[...].astype(F32))], axis=1).astype(BF)
+        out[...] = jnp.concatenate([by_parity(a[...]), by_parity(b[...])], axis=1)
 
 
 def repeat_kernel(rows, out):
@@ -203,10 +204,10 @@
 def proj_kernel(offsets, counts, gy, w, q, qg, qg_top):
     total = jnp.zeros((TOKENS, FEAT), F32)
     for i in range(4):
-        flat = by_parity(gy[i].astype(F32)).astype(BF)
+        flat = by_parity(gy[i])
         total = total + nt(flat, w[:, i * FEAT : (i + 1) * FEAT])
     total = jnp.where(positions((TOKENS, FEAT)) < counts[lax.axis_index("seq")], total, 0.0)
-    flat = jnp.concatenate([by_parity(q[...].astype(F32)), total], axis=1).astype(BF)
+    flat = jnp.concatenate([by_parity(q[...]), total.astype(BF)], axis=1)
     qg[:TOKENS] = flat
 
     def mask(h, shape):
@@ -266,22 +267,27 @@
         kv1[1, s * ROWS1 : (s + 1) * ROWS1] = second_view(block, helpers)
 
 
-def forward_kernel(offsets, counts, qg, qg_top, kv, kvp, rows, tail, kv1):
+def by_head(x, width):
+    return jnp.concatenate([x[:, h * width : (h + 1) * width] for h in range(HEADS)], axis=0)
+
+
+def level0_kernel(counts, qg, kv, kvp, stats):
     seq = lax.axis_index("seq")
-    fill_level1(offsets, counts, rows, kv1)
     flat = qg[:TOKENS]
-    queries = first_view(flat, query_helpers(TOKENS))
-    grads = second_view(flat, jnp.zeros((TOKENS, SIDE), BF))
+    queries = head_stack(first_view(flat, query_helpers(TOKENS)), first_mask)
+    grads = head_stack(second_view(flat, jnp.zeros((TOKENS, SIDE), BF)), second_mask)
     own = key_helpers(full_mask(counts[seq]))
     other = key_helpers(full_mask(counts[seq ^ 1]))
     keys = (first_view(kv[...], own), first_view(kvp[...], other))
     values = (second_view(kv[...], own), second_view(kvp[...], other))
-    parts = []
-    for h in range(HEADS):
-        q_mask = first_mask(h, (1, LANES)).astype(BF)
-        g_mask = second_mask(h, (1, LANES)).astype(BF)
-        parts.append(level_stats(keys, values, queries * q_mask, grads * g_mask))
-    level0 = [jnp.concatenate([p[i] for p in parts], axis=0) for i in range(3)]
+    for i, x in enumerate(level_stats(keys, values, queries, grads)):
+        stats[4 * i : 4 * i + 4] = by_head(x, TOKENS)
+    stats[12:16] = jnp.zeros((4, TOKENS), F32)
+
+
+def level1_kernel(offsets, counts, qg, qg_top, rows, stats, tail, kv1):
+    fill_level1(offsets, counts, rows, kv1)
+    level0 = (stats[0:4], stats[4:8], stats[8:12])
     block = qg[TOKENS : TOKENS + ROWS1]
     q1 = head_stack(first_view(block, query_helpers(ROWS1)), first_mask)
     g1 = head_stack(second_view(block, jnp.zeros((ROWS1, SIDE), BF)), second_mask)
@@ -321,7 +327,7 @@
     return wide[:, :SIDE] + wide[:, SIDE : 2 * SIDE] + wide[:, 2 * SIDE :]
 
 
-def finish_kernel(offsets, counts, tails, rows, st, packed, keys, values):
+def finish_kernel(offsets, counts, tails, rows, st1, st, packed, keys, values):
     fill_level2(offsets, counts, rows, keys, values)
     starts = [0, TAIL] + [2 * TAIL + 2 * ROWS2 * i for i in range(GROUP - 2)]
     block = jnp.concatenate([tails[at : at + ROWS2] for at in starts], axis=0)
@@ -329,7 +335,7 @@
     q2 = head_stack(first_view(block, query_helpers(width)), first_mask)
     g2 = head_stack(second_view(block, jnp.zeros((width, SIDE), BF)), second_mask)
     flat = level_stats((keys[...],), (values[...],), q2, g2)
-    level2 = [jnp.concatenate([x[:, h * width : (h + 1) * width] for h in range(HEADS)], axis=0) for x in flat]
+    level2 = [by_head(x, width) for x in flat]
     small = [summed_terms(tails, at + ROWS2) for at in starts]
     early1 = jnp.concatenate([x[:, :ROWS1] for x in small], axis=1)
     early2 = jnp.concatenate([x[:, ROWS1:ROWS] for x in small], axis=1)
@@ -372,7 +378,8 @@
     slot = jnp.where(s < 3, s, jnp.where(s < 6, s + 1, jnp.where(s == 6, 3, 7)))
     place = jnp.where((iota((8 * HEADS, SIDE), 1) & 63) == 8 * h + slot, 1.0, 0.0).astype(BF)
     full = nn(columns.T.astype(BF), place).astype(BF)
-    st[...] = full
+    st1[...] = full[:OWN]
+    st[...] = full[OWN:]
     wide = jnp.concatenate([block, full[total_rows:]], axis=1)
     for n in range(GROUP):
         packed[n] = wide
@@ -400,7 +407,7 @@
     return total
 
 
-def grad_query_kernel(offsets, counts, qg, qg_top, st, kv, kvp, rows1, rows2, dq, kv1, keys2, values2):
+def grad_query_kernel(offsets, counts, qg, qg_top, st1, st, kv, kvp, rows1, rows2, dq, kv1, keys2, values2):
     seq = lax.axis_index("seq")
     fill_level1(offsets, counts, rows1, kv1)
     fill_level2(offsets, counts, rows2, keys2, values2)
@@ -419,20 +426,15 @@
         return total
 
     flat = qg[:TOKENS]
-    mine = st[OWN : OWN + TOKENS]
+    mine = st[:TOKENS]
     queries, grads = first_view(flat, mine), second_view(flat, mine)
-    total = jnp.zeros((TOKENS, LANES), F32)
-    for h in range(HEADS):
-        q_mask = first_mask(h, (1, LANES)).astype(BF)
-        g_mask = second_mask(h, (1, LANES)).astype(BF)
-        part = back(queries * q_mask, grads * g_mask, keys, values)
-        total = jnp.where(feature_mask(h, (TOKENS, LANES)), part, total)
+    part = back(head_stack(queries, first_mask), head_stack(grads, second_mask), keys, values)
+    total = folded(part, TOKENS, feature_mask)
     got = []
-    for block, at, ks, vs in (
-        (qg[TOKENS:], 0, kv1[0], kv1[1]),
-        (qg_top[...], OWN + 2 * TOKENS, keys2[...], values2[...]),
+    for block, helpers, ks, vs in (
+        (qg[TOKENS:], st1[:ROWS1], kv1[0], kv1[1]),
+        (qg_top[...], st[2 * TOKENS : 2 * TOKENS + ROWS2], keys2[...], values2[...]),
     ):
-        helpers = st[at : at + block.shape[0]]
         qs = head_stack(first_view(block, helpers), first_mask)
         gs = head_stack(second_view(block, helpers), second_mask)
         got.append(back(qs, gs, (ks,), (vs,)))
@@ -452,51 +454,44 @@
     return total_k, total_v
 
 
-def grad_key_kernel(offsets, counts, kv, copies, qg, st, qgp, qg2, qg4, qg6, dk, dv, qs, gs):
-    seq = lax.axis_index("seq")
-    sources = ((qg, TOKENS), (qgp, TOKENS), *((ref, at) for ref in (qg2, qg4, qg6) for at in (0, ROWS1)))
-    for i, (ref, at) in enumerate(sources):
-        block = ref[at : at + ROWS1]
-        helpers = st[i * ROWS1 : (i + 1) * ROWS1]
+def grad_key_kernel(counts, kv, qg, st, qgp, out):
+    own = key_helpers(full_mask(counts[lax.axis_index("seq")]))
+    keys, values = first_view(kv[...], own), second_view(kv[...], own)
+    flat, other = qg[:TOKENS], qgp[:TOKENS]
+    mine, next_st = st[:TOKENS], st[TOKENS : 2 * TOKENS]
+    queries = (first_view(flat, mine), first_view(other, next_st))
+    grads = (second_view(flat, mine), second_view(other, next_st))
+    part_k, part_v = key_back(head_stack(keys, first_mask), head_stack(values, second_mask), queries, grads)
+    out[:, :FEAT] = folded(part_k, TOKENS, feature_mask)[:, :FEAT]
+    out[:, FEAT:] = folded(part_v, TOKENS, second_mask)[:, LANES - FEAT :]
+
+
+def level1_keys_kernel(offsets, counts, copies, near, far2, far4, far6, st1, level0, out, qs, gs):
+    for i in range(GROUP):
+        block = (near, far2, far4, far6)[i // 2][(i & 1) * ROWS1 : (i & 1) * ROWS1 + ROWS1]
+        helpers = st1[i * ROWS1 : (i + 1) * ROWS1]
         qs[i * ROWS1 : (i + 1) * ROWS1] = first_view(block, helpers)
         gs[i * ROWS1 : (i + 1) * ROWS1] = second_view(block, helpers)
-    own = key_helpers(full_mask(counts[seq]))
-    keys, values = first_view(kv[...], own), second_view(kv[...], own)
-    flat, other = qg[:TOKENS], qgp[:TOKENS]
-    mine, next_st = st[OWN : OWN + TOKENS], st[OWN + TOKENS : OWN + 2 * TOKENS]
-    queries = (first_view(flat, mine), first_view(other, next_st))
-    grads = (second_view(flat, mine), second_view(other, next_st))
-    total_k = jnp.zeros((TOKENS, LANES), F32)
-    total_v = jnp.zeros((TOKENS, LANES), F32)
-    for h in range(HEADS):
-        k_mask = first_mask(h, (1, LANES)).astype(BF)
-        v_mask = second_mask(h, (1, LANES)).astype(BF)
-        part_k, part_v = key_back(keys * k_mask, values * v_mask, queries, grads)
-        total_k = jnp.where(feature_mask(h, (TOKENS, LANES)), part_k, total_k)
-        total_v = jnp.where(second_mask(h, (TOKENS, LANES)), part_v, total_v)
-    helpers = key_helpers(dilated_mask(offsets, 0, counts[seq]))
+    mine = key_helpers(dilated_mask(offsets, 0, counts[lax.axis_index("seq")]))
     block = copies[0, :ROWS1]
-    k1 = head_stack(first_view(block, helpers), first_mask)
-    v1 = head_stack(second_view(block, helpers), second_mask)
+    k1 = head_stack(first_view(block, mine), first_mask)
+    v1 = head_stack(second_view(block, mine), second_mask)
     k1_part, v1_part = key_back(k1, v1, (qs[...],), (gs[...],))
-    dk[...] = total_k + scatter_rows(offsets, k1_part, None, 0)
-    dv[...] = total_v + scatter_rows(offsets, v1_part, None, LANES - FEAT)
-
-
-def last_kernel(offsets, counts, rows, qg2, dk_in, dv_in, dk, dv):
-    seq = lax.axis_index("seq")
-    full = qg2[...].reshape(GROUP * GROUP * ROWS2, PAIR + SIDE)
+    out[:, :FEAT] = level0[:, :FEAT] + scatter_rows(offsets, k1_part, None, 0)[:, :FEAT]
+    out[:, FEAT:] = level0[:, FEAT:] + scatter_rows(offsets, v1_part, None, LANES - FEAT)[:, LANES - FEAT :]
+
+
+def last_kernel(offsets, counts, copies, all_qg, early, dk, dv):
+    full = all_qg[...].reshape(GROUP * GROUP * ROWS2, PAIR + SIDE)
     helpers = full[:, PAIR:]
     queries, grads = first_view(full[:, :PAIR], helpers), second_view(full[:, :PAIR], helpers)
-    mine = key_helpers(dilated_mask(offsets, 1, counts[seq]))
-    block = rows[0, ROWS1:]
+    mine = key_helpers(dilated_mask(offsets, 1, counts[lax.axis_index("seq")]))
+    block = copies[0, ROWS1:]
     k2 = head_stack(first_view(block, mine), first_mask)
     v2 = head_stack(second_view(block, mine), second_mask)
     k2_part, v2_part = key_back(k2, v2, (queries,), (grads,))
-    total_k = (dk_in[...] + scatter_rows(offsets, None, k2_part, 0)) * SCALE
-    total_v = dv_in[...] + scatter_rows(offsets, None, v2_part, LANES - FEAT)
-    dk[...] = to_paired(total_k)
-    dv[...] = to_paired(total_v[:, LANES - FEAT :])
+    dk[...] = to_paired((early[:, :FEAT] + scatter_rows(offsets, None, k2_part, 0)[:, :FEAT]) * SCALE)
+    dv[...] = to_paired(early[:, FEAT:] + scatter_rows(offsets, None, v2_part, LANES - FEAT)[:, LANES - FEAT :])
 
 
 def call(kernel, outs, n_smem, *args, scratch=()):
@@ -539,33 +534,37 @@
         proj_kernel, [((TOKENS + ROWS1, PAIR), BF), ((ROWS2, PAIR), BF)], 2, offsets, counts, gy, out_weight, queries
     )
     qgp = swap(qg, 1)
+    (stats,) = call(level0_kernel, [((16, TOKENS), F32)], 1, counts, qg, kv, kvp)
+    ring_kv, stats = lax.optimization_barrier((ring_kv, stats))
     (tail,) = call(
-        forward_kernel, [((TAIL, PAIR), BF)], 2, offsets, counts, qg, qg_top, kv, kvp, ring_kv,
+        level1_kernel, [((TAIL, PAIR), BF)], 2, offsets, counts, qg, qg_top, ring_kv, stats,
         scratch=[(2, GROUP * ROWS1, LANES)],
     )
-    ring_kv, tail = lax.optimization_barrier((ring_kv, tail))
     tail_next = swap(tail, 1)
+    ring_kv, tail_next, qgp = lax.optimization_barrier((ring_kv, tail_next, qgp))
     (repeated,) = call(repeat_kernel, [((GROUP, GROUP * ROWS2, PAIR), BF)], 0, ring_kv)
     all_kv = exchange(repeated, planes)
     tails = far(tail[: 2 * ROWS2], tail_next[: 2 * ROWS2])
     tails, qgp = lax.optimization_barrier((jnp.concatenate([tail, tail_next, *tails], axis=0), qgp))
     big = (GROUP * GROUP * ROWS2, LANES)
-    st_rows = OWN + 2 * TOKENS + GROUP * ROWS2
-    st, packed = call(
-        finish_kernel, [((st_rows, SIDE), BF), ((GROUP, GROUP * ROWS2, PAIR + SIDE), BF)], 2, offsets, counts,
+    st_rows = 2 * TOKENS + GROUP * ROWS2
+    st1, st, packed = call(
+        finish_kernel, [((OWN, SIDE), BF), ((st_rows, SIDE), BF), ((GROUP, GROUP * ROWS2, PAIR + SIDE), BF)], 2, offsets, counts,
         tails, all_kv, scratch=[big, big],
     )
-    qgs = far(qg[TOKENS:], qgp[TOKENS:])
+    near = jnp.concatenate([qg[TOKENS:], qgp[TOKENS:]], axis=0)
+    qgs = tuple(shift(near, step) for step in (2, 4, 6))
     all_qg = exchange(packed, planes)
     (dq,) = call(
-        grad_query_kernel, [((HALF, PAIR), BF)], 2, offsets, counts, qg, qg_top, st, kv, kvp, ring_kv, all_kv,
+        grad_query_kernel, [((HALF, PAIR), BF)], 2, offsets, counts, qg, qg_top, st1, st, kv, kvp, ring_kv, all_kv,
         scratch=[(2, GROUP * ROWS1, LANES), big, big],
     )
-    dk, dv = call(
-        grad_key_kernel, [((TOKENS, LANES), F32)] * 2, 2, offsets, counts, kv, copies, qg, st, qgp, *qgs,
-        scratch=[(GROUP * ROWS1, LANES)] * 2,
-    )
-    dk, dv = call(last_kernel, [((HALF, PAIR), BF)] * 2, 2, offsets, counts, copies, all_qg, dk, dv)
+    (level0,) = call(grad_key_kernel, [((TOKENS, PAIR), F32)], 1, counts, kv, qg, st, qgp)
+    (early,) = call(
+        level1_keys_kernel, [((TOKENS, PAIR), F32)], 2, offsets, counts, copies, near, *qgs, st1, level0,
+        scratch=[(OWN, LANES)] * 2,
+    )
+    dk, dv = call(last_kernel, [((HALF, PAIR), BF)] * 2, 2, offsets, counts, copies, all_qg, early)
     return dq, dk, dv
 
 

time: 87.7 us -> 84.7 us (0.966)
  waiting for transfers between devices: 17.2 us -> 9.67 us
  starting transfers between devices: 37.1 us -> 40.2 us
    all_to_all x3, waiting for transfers between devices: 5.04 us -> 1.53 us  [exchange(): return lax.all_to_all(copies, 'seq', 0, 0, axis_index_groups=groups)]
    ppermute x6, waiting for transfers between devices: 6.67 us -> 3.87 us  [shift(): lax.ppermute(x, 'seq', [(r[i], r[(i + step) % GROUP]) for r in rings for...]
    ppermute x6, starting transfers between devices: 13.1 us -> 15.4 us  [shift(): lax.ppermute(x, 'seq', [(r[i], r[(i + step) % GROUP]) for r in rings for...]
    ppermute x4, waiting for transfers between devices: 5.44 us -> 4.27 us  [swap(): return lax.ppermute(x, 'seq', [(i, i ^ bits) for i in range(n_seq)])]
    pallas_call x9 -> x11, Pallas kernels: 19.7 us -> 20.3 us  [call(): pl.pallas_call(kernel, out_shape=[jax.ShapeDtypeStruct(s, d) for s, d in...]
  transfers between devices with their start and end apart: 13 -> 13, of which waited for: 8 -> 8; matrix products, arithmetic and copies ran while one was open for 0% -> 0% of each run, Pallas kernels for 12% -> 17%
where the time goes in v3:
time: 84.7 us; the launch traced here: 83.5 us
  starting transfers between devices  40.2 us (47%)
  Pallas kernels  20.3 us (24%)
  waiting for transfers between devices  9.67 us (11%)
  blocking collectives  8.29 us (10%)
  local copies, waits for them, and re-layouts  4.22 us (5%)
    pallas_call x11, Pallas kernels, call(): pl.pallas_call(kernel, out_shape=[jax.ShapeDtypeStruct(s, d) for s, d in...  20.3 us
    all_to_all x3, starting transfers between devices, exchange(): return lax.all_to_all(copies, 'seq', 0, 0, axis_index_groups=groups)  19.9 us
    ppermute x6, starting transfers between devices, shift(): lax.ppermute(x, 'seq', [(r[i], r[(i + step) % GROUP]) for r in rings for...  15.4 us
    all_gather x1, blocking collectives, per_device(): gy = lax.all_gather(grad_y, 'head', axis=0)  8.29 us
    ppermute x4, starting transfers between devices, swap(): return lax.ppermute(x, 'seq', [(i, i ^ bits) for i in range(n_seq)])  4.86 us
    ppermute x4, waiting for transfers between devices, swap(): return lax.ppermute(x, 'seq', [(i, i ^ bits) for i in range(n_seq)])  4.27 us
    unnamed x26, local copies, waits for them, and re-layouts  4.18 us
    ppermute x6, waiting for transfers between devices, shift(): lax.ppermute(x, 'seq', [(r[i], r[(i + step) % GROUP]) for r in rings for...  3.87 us
  transfers between devices with their start and end apart: 13, of which 8 were waited for; matrix products, arithmetic and copies ran while one was open for 0% of the time, Pallas kernels for 17%

profile of v3, /device:TPU:2, one launch (start us, length us, event | category | flops | bytes accessed | tf_op | source)
XLA Modules:
  0.0 83.5 jit_solution(14599298384909497279)
XLA Ops:
  0.6 2.0 %collective-permute-start = (bf16[128,384]{1,0:T(8,128)(2,1)}, bf16[128,384]{1,0:T(8,128)(2,1)S(1)}, u32[]{:S(2)}, u32[]{:S(2)}) collective-permute-start(bf16[128,384]{1,0:T(8,128)(2,1)} %k.3), channel_id=1, source_target_pairs={{0,4},{4,0},{8,12},{12,8},{16,20},{20,16},{24,28},{28,24},{32,36},... | collective-permute-start | bytes 294920 | tf_op jit(solution)/shard_map/ppermute | solution.py:514
  2.6 0.1 collective-permute-start.1
  2.7 0.0 copy-start.1
  2.7 0.9 %copy-done.1 = bf16[128,384]{1,0:T(8,128)(2,1)S(1)} copy-done((bf16[128,384]{1,0:T(8,128)(2,1)S(1)}, bf16[128,384]{1,0:T(8,128)(2,1)}, u32[]{:S(2)}) %copy-start.1) | copy-done | bytes 98328
  3.6 0.0 copy-start.3
  3.6 0.9 %copy-done.3 = bf16[128,384]{1,0:T(8,128)(2,1)S(1)} copy-done((bf16[128,384]{1,0:T(8,128)(2,1)S(1)}, bf16[128,384]{1,0:T(8,128)(2,1)}, u32[]{:S(2)}) %copy-start.3) | copy-done | bytes 98328
  4.5 0.0 copy-start.7
  4.5 0.7 copy-done.7
  5.2 1.9 %shard_map.95.copies = bf16[8,80,384]{2,1,0:T(8,128)(2,1)} custom-call(s32[2,16]{1,0:T(2,128)S(1)} %copy-done.7, bf16[128,384]{1,0:T(8,128)(2,1)S(1)} %copy-done.1, bf16[128,384]{1,0:T(8,128)(2,1)S(1)} %copy-done.3), custom_call_target="tpu_custom_call" | custom-call | tf_op jit(solution)/shard_map/pallas_call | solution.py:498
  7.1 0.0 copy-start.10
  7.1 0.0 collective-permute-done.k_next
  7.1 0.6 collective-permute-done.1.v_next
  7.7 8.3 %all-to-all-start = ((bf16[8,80,384]{2,1,0:T(8,128)(2,1)}), bf16[8,80,384]{2,1,0:T(8,128)(2,1)S(1)}, u32[]{:S(2)}, u32[]{:S(2)}) async-start(bf16[8,80,384]{2,1,0:T(8,128)(2,1)} %shard_map.95.copies), calls=%async_computation | async-start | bytes 983040 | tf_op jit(solution)/shard_map/all_to_all | solution.py:520
  16.0 0.0 copy-done.10
  16.0 0.0 copy-start.5
  16.1 0.0 copy-start.6
  16.1 8.3 %all-gather = bf16[512,384]{1,0:T(8,128)(2,1)S(1)} all-gather(bf16[128,384]{1,0:T(8,128)(2,1)S(1)} %copy-done.10), channel_id=2, replica_groups=mesh['seq'=64,'head'=4] {'head'}, dimensions={0}, use_global_device_ids=true | all-gather | bytes 491520 | tf_op jit(solution)/shard_map/all_gather | solution.py:532
  24.4 0.0 copy-start.8
  24.4 0.0 copy-start.9
  24.4 0.0 copy-done.5
  24.4 0.0 copy-done.6
  24.4 0.7 copy-done.8
  25.0 0.0 copy-done.9
  25.0 0.0 copy-start.2
  25.0 0.0 copy-start.4
  25.0 1.4 %shard_map.94 = (bf16[320,384]{1,0:T(8,128)(2,1)S(1)}, bf16[16,384]{1,0:T(8,128)(2,1)S(1)}) custom-call(s32[2,16]{1,0:T(2,128)S(1)} %copy-done.8, s32[64]{0:T(128)S(1)} %copy-done.9, bf16[4,128,384]{2,1,0:T(8,128)(2,1)S(1)} %bitcast.1, bf16[192,768]{1,0:T(8,128)(2,1)S(1)} %copy-done.5, bf16[128,384]{1,0:T(8,128)(2,1)S(1)} %copy-done.6), custom_call_target="tpu_custom_call" | custom-call | tf_op jit(solution)/shard_map/pallas_call | solution.py:498
  26.4 2.1 %collective-permute-start.3 = (bf16[320,384]{1,0:T(8,128)(2,1)S(1)}, bf16[320,384]{1,0:T(8,128)(2,1)S(1)}, u32[]{:S(2)}, u32[]{:S(2)}) collective-permute-start(bf16[320,384]{1,0:T(8,128)(2,1)S(1)} %get-tuple-element.22.qg), channel_id=1, source_target_pairs={{0,4},{4,0},{8,12},{12,8},{16,20},{20,16},{24,28},{28,24},{32,36},... | collective-permute-start | bytes 737288 | tf_op jit(solution)/shard_map/ppermute | solution.py:514
  28.5 0.0 copy-done.2
  28.5 0.0 copy-done.4
  28.5 0.4 shard_map.96
  29.0 1.5 %shard_map.97.stats = f32[16,256]{1,0:T(8,128)S(1)} custom-call(s32[64]{0:T(128)S(1)} %copy-done.9, bf16[320,384]{1,0:T(8,128)(2,1)S(1)} %get-tuple-element.22.qg, bf16[256,384]{1,0:T(8,128)(2,1)S(1)} %get-tuple-element.27.kv, bf16[256,384]{1,0:T(8,128)(2,1)S(1)} %get-tuple-element.28.kvp), custom_call_target="tpu_custom_call" | custom-call | tf_op jit(solution)/shard_map/pallas_call | solution.py:498
  30.4 1.5 %all-to-all-done.rows.rows1 = bf16[8,80,384]{2,1,0:T(8,128)(2,1)S(1)} async-done(((bf16[8,80,384]{2,1,0:T(8,128)(2,1)}), bf16[8,80,384]{2,1,0:T(8,128)(2,1)S(1)}, u32[]{:S(2)}, u32[]{:S(2)}) %all-to-all-start) | async-done | bytes 491552 | tf_op jit(solution)/shard_map/all_to_all | solution.py:520
  32.0 1.6 %shard_map.98 = bf16[80,384]{1,0:T(8,128)(2,1)S(1)} custom-call(s32[2,16]{1,0:T(2,128)S(1)} %copy-done.8, s32[64]{0:T(128)S(1)} %copy-done.9, bf16[320,384]{1,0:T(8,128)(2,1)S(1)} %get-tuple-element.22.qg, bf16[16,384]{1,0:T(8,128)(2,1)S(1)} %get-tuple-element.23.qg_top, bf16[8,80,384]{2,1,0:T(8,128)(2,1)S(1)} %all-to-all-done.rows.rows1, ...), custom_call_target="tpu_custom_call" | custom-call | tf_op jit(solution)/shard_map/pallas_call | solution.py:498
  33.6 0.7 collective-permute-start.2
  34.3 0.8 %collective-permute-done.3.qgp = bf16[320,384]{1,0:T(8,128)(2,1)S(1)} collective-permute-done((bf16[320,384]{1,0:T(8,128)(2,1)S(1)}, bf16[320,384]{1,0:T(8,128)(2,1)S(1)}, u32[]{:S(2)}, u32[]{:S(2)}) %collective-permute-start.3) | collective-permute-done | bytes 245792 | tf_op jit(solution)/shard_map/ppermute | solution.py:514
  35.1 2.8 %collective-permute-done.2 = bf16[80,384]{1,0:T(8,128)(2,1)S(1)} collective-permute-done((bf16[80,384]{1,0:T(8,128)(2,1)S(1)}, bf16[80,384]{1,0:T(8,128)(2,1)S(1)}, u32[]{:S(2)}, u32[]{:S(2)}) %collective-permute-start.2) | collective-permute-done | bytes 61472 | tf_op jit(solution)/shard_map/ppermute | solution.py:514
  37.9 1.0 %shard_map.99 = bf16[8,128,384]{2,1,0:T(8,128)(2,1)} custom-call(bf16[8,80,384]{2,1,0:T(8,128)(2,1)S(1)} %all-to-all-done.rows.rows1), custom_call_target="tpu_custom_call" | custom-call | tf_op jit(solution)/shard_map/pallas_call | solution.py:498
  38.9 6.0 %all-to-all-start.1 = ((bf16[8,128,384]{2,1,0:T(8,128)(2,1)}), bf16[8,128,384]{2,1,0:T(8,128)(2,1)S(1)}, u32[]{:S(2)}, u32[]{:S(2)}) async-start(bf16[8,128,384]{2,1,0:T(8,128)(2,1)} %shard_map.99), calls=%async_computation.1 | async-start | bytes 1572864 | tf_op jit(solution)/shard_map/all_to_all | solution.py:520
  44.9 1.2 %collective-permute-start.4 = (bf16[64,384]{1,0:T(8,128)(2,1)S(1)}, bf16[64,384]{1,0:T(8,128)(2,1)S(1)}, u32[]{:S(2)}, u32[]{:S(2)}) collective-permute-start(bf16[64,384]{1,0:T(8,128)(2,1)S(1)} %pad_maximum_fusion.1), channel_id=1, source_target_pairs={{0,8},{4,12},{8,16},{12,20},{16,24},{20,28},{24,0},{28,4},{32,40},... | collective-permute-start | bytes 147464 | tf_op jit(solution)/shard_map/ppermute | solution.py:517
  46.0 2.9 %collective-permute-start.5 = (bf16[64,384]{1,0:T(8,128)(2,1)S(1)}, bf16[64,384]{1,0:T(8,128)(2,1)S(1)}, u32[]{:S(2)}, u32[]{:S(2)}) collective-permute-start(bf16[64,384]{1,0:T(8,128)(2,1)S(1)} %pad_maximum_fusion.1), channel_id=1, source_target_pairs={{0,16},{4,20},{8,24},{12,28},{16,0},{20,4},{24,8},{28,12},{32,48},... | collective-permute-start | bytes 147464 | tf_op jit(solution)/shard_map/ppermute | solution.py:517
  49.0 3.6 %collective-permute-start.6 = (bf16[64,384]{1,0:T(8,128)(2,1)S(1)}, bf16[64,384]{1,0:T(8,128)(2,1)S(1)}, u32[]{:S(2)}, u32[]{:S(2)}) collective-permute-start(bf16[64,384]{1,0:T(8,128)(2,1)S(1)} %pad_maximum_fusion.1), channel_id=1, source_target_pairs={{0,24},{4,28},{8,0},{12,4},{16,8},{20,12},{24,16},{28,20},{32,56},... | collective-permute-start | bytes 147464 | tf_op jit(solution)/shard_map/ppermute | solution.py:517
  52.5 0.0 collective-permute-done.4
  52.6 1.5 %collective-permute-done.5 = bf16[64,384]{1,0:T(8,128)(2,1)S(1)} collective-permute-done((bf16[64,384]{1,0:T(8,128)(2,1)S(1)}, bf16[64,384]{1,0:T(8,128)(2,1)S(1)}, u32[]{:S(2)}, u32[]{:S(2)}) %collective-permute-start.5) | collective-permute-done | bytes 49184 | tf_op jit(solution)/shard_map/ppermute | solution.py:517
  54.0 1.0 %collective-permute-done.6 = bf16[64,384]{1,0:T(8,128)(2,1)S(1)} collective-permute-done((bf16[64,384]{1,0:T(8,128)(2,1)S(1)}, bf16[64,384]{1,0:T(8,128)(2,1)S(1)}, u32[]{:S(2)}, u32[]{:S(2)}) %collective-permute-start.6) | collective-permute-done | bytes 49184 | tf_op jit(solution)/shard_map/ppermute | solution.py:517
  55.1 0.0 all-to-all-done.1.rows.rows2
  55.1 2.7 %shard_map.100 = (bf16[512,128]{1,0:T(8,128)(2,1)S(1)}, bf16[640,128]{1,0:T(8,128)(2,1)S(1)}, bf16[8,128,512]{2,1,0:T(8,128)(2,1)S(1)}) custom-call(s32[2,16]{1,0:T(2,128)S(1)} %copy-done.8, s32[64]{0:T(128)S(1)} %copy-done.9, bf16[352,384]{1,0:T(8,128)(2,1)S(1)} %constant_dynamic-update-slice_fusion.tails, bf16[8,128,384]{2,1,0:T(8,128)(2,1)S(1)} %all-to-all-done.1.rows.rows2), custom_call_target="tpu_custom_call" | custom-call | tf_op jit(solution)/shard_map/pallas_call | solution.py:498
  57.9 0.0 copy-start
  57.9 1.0 %copy-done = bf16[8,128,512]{2,1,0:T(8,128)(2,1)} copy-done((bf16[8,128,512]{2,1,0:T(8,128)(2,1)}, bf16[8,128,512]{2,1,0:T(8,128)(2,1)S(1)}, u32[]{:S(2)}) %copy-start) | copy-done | bytes 1048600
  58.8 5.7 %all-to-all-start.2 = ((bf16[8,128,512]{2,1,0:T(8,128)(2,1)}), bf16[8,128,512]{2,1,0:T(8,128)(2,1)S(1)}, u32[]{:S(2)}, u32[]{:S(2)}) async-start(bf16[8,128,512]{2,1,0:T(8,128)(2,1)} %copy-done), calls=%async_computation.2 | async-start | bytes 2097152 | tf_op jit(solution)/shard_map/all_to_all | solution.py:520
  64.6 3.3 %collective-permute-start.7 = (bf16[128,384]{1,0:T(8,128)(2,1)S(1)}, bf16[128,384]{1,0:T(8,128)(2,1)S(1)}, u32[]{:S(2)}, u32[]{:S(2)}) collective-permute-start(bf16[128,384]{1,0:T(8,128)(2,1)S(1)} %pad_maximum_fusion.near), channel_id=1, source_target_pairs={{0,8},{4,12},{8,16},{12,20},{16,24},{20,28},{24,0},{28,4},{32,40},... | collective-permute-start | bytes 294920 | tf_op jit(solution)/shard_map/ppermute | solution.py:517
  67.9 3.3 %collective-permute-start.8 = (bf16[128,384]{1,0:T(8,128)(2,1)S(1)}, bf16[128,384]{1,0:T(8,128)(2,1)S(1)}, u32[]{:S(2)}, u32[]{:S(2)}) collective-permute-start(bf16[128,384]{1,0:T(8,128)(2,1)S(1)} %pad_maximum_fusion.near), channel_id=1, source_target_pairs={{0,16},{4,20},{8,24},{12,28},{16,0},{20,4},{24,8},{28,12},{32,48},... | collective-permute-start | bytes 294920 | tf_op jit(solution)/shard_map/ppermute | solution.py:517
  71.2 1.1 %collective-permute-start.9 = (bf16[128,384]{1,0:T(8,128)(2,1)S(1)}, bf16[128,384]{1,0:T(8,128)(2,1)S(1)}, u32[]{:S(2)}, u32[]{:S(2)}) collective-permute-start(bf16[128,384]{1,0:T(8,128)(2,1)S(1)} %pad_maximum_fusion.near), channel_id=1, source_target_pairs={{0,24},{4,28},{8,0},{12,4},{16,8},{20,12},{24,16},{28,20},{32,56},... | collective-permute-start | bytes 294920 | tf_op jit(solution)/shard_map/ppermute | solution.py:517
  72.3 1.8 %shard_map.102.level0 = f32[256,384]{1,0:T(8,128)S(1)} custom-call(s32[64]{0:T(128)S(1)} %copy-done.9, bf16[256,384]{1,0:T(8,128)(2,1)S(1)} %get-tuple-element.27.kv, bf16[320,384]{1,0:T(8,128)(2,1)S(1)} %get-tuple-element.22.qg, bf16[640,128]{1,0:T(8,128)(2,1)S(1)} %get-tuple-element.36.st, bf16[320,384]{1,0:T(8,128)(2,1)S(1)} %collective-permute-done.3.qgp), custom_call_target="tpu_custom_call" | custom-call | tf_op jit(solution)/shard_map/pallas_call | solution.py:498
  74.2 3.3 %shard_map.101 = bf16[128,384]{1,0:T(8,128)(2,1)} custom-call(s32[2,16]{1,0:T(2,128)S(1)} %copy-done.8, s32[64]{0:T(128)S(1)} %copy-done.9, bf16[320,384]{1,0:T(8,128)(2,1)S(1)} %get-tuple-element.22.qg, bf16[16,384]{1,0:T(8,128)(2,1)S(1)} %get-tuple-element.23.qg_top, bf16[512,128]{1,0:T(8,128)(2,1)S(1)} %get-tuple-element.35.st1, ...), custom_call_target="tpu_custom_call" | custom-call | tf_op jit(solution)/shard_map/pallas_call | solution.py:498
  77.5 0.0 collective-permute-done.7.far2
  77.5 0.9 %collective-permute-done.8.far4 = bf16[128,384]{1,0:T(8,128)(2,1)S(1)} collective-permute-done((bf16[128,384]{1,0:T(8,128)(2,1)S(1)}, bf16[128,384]{1,0:T(8,128)(2,1)S(1)}, u32[]{:S(2)}, u32[]{:S(2)}) %collective-permute-start.8) | collective-permute-done | bytes 98336 | tf_op jit(solution)/shard_map/ppermute | solution.py:517
  78.4 0.5 collective-permute-done.9.far6
  78.9 1.8 %shard_map.103.early = f32[256,384]{1,0:T(8,128)S(1)} custom-call(s32[2,16]{1,0:T(2,128)S(1)} %copy-done.8, s32[64]{0:T(128)S(1)} %copy-done.9, bf16[8,80,384]{2,1,0:T(8,128)(2,1)} %shard_map.95.copies, bf16[128,384]{1,0:T(8,128)(2,1)S(1)} %pad_maximum_fusion.near, bf16[128,384]{1,0:T(8,128)(2,1)S(1)} %collective-permute-done.7.far2, ...), custom_call_target="tpu_custom_call" | custom-call | tf_op jit(solution)/shard_map/pallas_call | solution.py:498
  80.7 0.0 all-to-all-done.2.all_qg
  80.7 2.7 %shard_map.104 = (bf16[128,384]{1,0:T(8,128)(2,1)}, bf16[128,384]{1,0:T(8,128)(2,1)}) custom-call(s32[2,16]{1,0:T(2,128)S(1)} %copy-done.8, s32[64]{0:T(128)S(1)} %copy-done.9, bf16[8,80,384]{2,1,0:T(8,128)(2,1)} %shard_map.95.copies, bf16[8,128,512]{2,1,0:T(8,128)(2,1)S(1)} %all-to-all-done.2.all_qg, f32[256,384]{1,0:T(8,128)S(1)} %shard_map.103.early), custom_call_target="tpu_custom_call" | custom-call | tf_op jit(solution)/shard_map/pallas_call | solution.py:498
  (11 shorter events, 0.1 us)
Async XLA Ops:
  0.6 6.5 %collective-permute-start = (bf16[128,384]{1,0:T(8,128)(2,1)}, bf16[128,384]{1,0:T(8,128)(2,1)S(1)}, u32[]{:S(2)}, u32[]{:S(2)}) collective-permute-start(bf16[128,384]{1,0:T(8,128)(2,1)} %k.3), channel_id=1, source_target_pairs={{0,4},{4,0},{8,12},{12,8},{16,20},{20,16},{24,28},{28,24},{32,36},... | collective-permute-start | bytes 294920 | tf_op jit(solution)/shard_map/ppermute | solution.py:514
  2.6 5.1 %collective-permute-start.1 = (bf16[128,384]{1,0:T(8,128)(2,1)}, bf16[128,384]{1,0:T(8,128)(2,1)S(1)}, u32[]{:S(2)}, u32[]{:S(2)}) collective-permute-start(bf16[128,384]{1,0:T(8,128)(2,1)} %v.3), channel_id=1, source_target_pairs={{0,4},{4,0},{8,12},{12,8},{16,20},{20,16},{24,28},{28,24},{32,36},... | collective-permute-start | bytes 294920 | tf_op jit(solution)/shard_map/ppermute | solution.py:514
  2.7 0.9 %copy-start.1 = (bf16[128,384]{1,0:T(8,128)(2,1)S(1)}, bf16[128,384]{1,0:T(8,128)(2,1)}, u32[]{:S(2)}) copy-start(bf16[128,384]{1,0:T(8,128)(2,1)} %k.3) | copy-start | bytes 294916
  3.6 0.9 %copy-start.3 = (bf16[128,384]{1,0:T(8,128)(2,1)S(1)}, bf16[128,384]{1,0:T(8,128)(2,1)}, u32[]{:S(2)}) copy-start(bf16[128,384]{1,0:T(8,128)(2,1)} %v.3) | copy-start | bytes 294916
  4.5 0.7 copy-start.7
  7.1 8.9 %copy-start.10 = (bf16[128,384]{1,0:T(8,128)(2,1)S(1)}, bf16[128,384]{1,0:T(8,128)(2,1)}, u32[]{:S(2)}) copy-start(bf16[128,384]{1,0:T(8,128)(2,1)} %param.10) | copy-start | bytes 294916
  7.7 24.2 %all-to-all-start = ((bf16[8,80,384]{2,1,0:T(8,128)(2,1)}), bf16[8,80,384]{2,1,0:T(8,128)(2,1)S(1)}, u32[]{:S(2)}, u32[]{:S(2)}) async-start(bf16[8,80,384]{2,1,0:T(8,128)(2,1)} %shard_map.95.copies), calls=%async_computation | async-start | bytes 983040 | tf_op jit(solution)/shard_map/all_to_all | solution.py:520
  16.0 8.3 %copy-start.5 = (bf16[192,768]{1,0:T(8,128)(2,1)S(1)}, bf16[192,768]{1,0:T(8,128)(2,1)}, u32[]{:S(2)}) copy-start(bf16[192,768]{1,0:T(8,128)(2,1)} %w.1) | copy-start | bytes 884740
  16.1 8.3 %copy-start.6 = (bf16[128,384]{1,0:T(8,128)(2,1)S(1)}, bf16[128,384]{1,0:T(8,128)(2,1)}, u32[]{:S(2)}) copy-start(bf16[128,384]{1,0:T(8,128)(2,1)} %q.1) | copy-start | bytes 294916
  24.4 0.7 copy-start.8
  24.4 0.7 copy-start.9
  25.0 3.5 %copy-start.2 = (bf16[128,384]{1,0:T(8,128)(2,1)S(1)}, bf16[128,384]{1,0:T(8,128)(2,1)}, u32[]{:S(2)}) copy-start(bf16[128,384]{1,0:T(8,128)(2,1)} %k.3) | copy-start | bytes 294916
  25.0 3.5 %copy-start.4 = (bf16[128,384]{1,0:T(8,128)(2,1)S(1)}, bf16[128,384]{1,0:T(8,128)(2,1)}, u32[]{:S(2)}) copy-start(bf16[128,384]{1,0:T(8,128)(2,1)} %v.3) | copy-start | bytes 294916
  26.4 8.7 %collective-permute-start.3 = (bf16[320,384]{1,0:T(8,128)(2,1)S(1)}, bf16[320,384]{1,0:T(8,128)(2,1)S(1)}, u32[]{:S(2)}, u32[]{:S(2)}) collective-permute-start(bf16[320,384]{1,0:T(8,128)(2,1)S(1)} %get-tuple-element.22.qg), channel_id=1, source_target_pairs={{0,4},{4,0},{8,12},{12,8},{16,20},{20,16},{24,28},{28,24},{32,36},... | collective-permute-start | bytes 737288 | tf_op jit(solution)/shard_map/ppermute | solution.py:514
  33.6 4.3 %collective-permute-start.2 = (bf16[80,384]{1,0:T(8,128)(2,1)S(1)}, bf16[80,384]{1,0:T(8,128)(2,1)S(1)}, u32[]{:S(2)}, u32[]{:S(2)}) collective-permute-start(bf16[80,384]{1,0:T(8,128)(2,1)S(1)} %shard_map.98), channel_id=1, source_target_pairs={{0,4},{4,0},{8,12},{12,8},{16,20},{20,16},{24,28},{28,24},{32,36},... | collective-permute-start | bytes 184328 | tf_op jit(solution)/shard_map/ppermute | solution.py:514
  38.9 16.2 %all-to-all-start.1 = ((bf16[8,128,384]{2,1,0:T(8,128)(2,1)}), bf16[8,128,384]{2,1,0:T(8,128)(2,1)S(1)}, u32[]{:S(2)}, u32[]{:S(2)}) async-start(bf16[8,128,384]{2,1,0:T(8,128)(2,1)} %shard_map.99), calls=%async_computation.1 | async-start | bytes 1572864 | tf_op jit(solution)/shard_map/all_to_all | solution.py:520
  44.9 7.7 %collective-permute-start.4 = (bf16[64,384]{1,0:T(8,128)(2,1)S(1)}, bf16[64,384]{1,0:T(8,128)(2,1)S(1)}, u32[]{:S(2)}, u32[]{:S(2)}) collective-permute-start(bf16[64,384]{1,0:T(8,128)(2,1)S(1)} %pad_maximum_fusion.1), channel_id=1, source_target_pairs={{0,8},{4,12},{8,16},{12,20},{16,24},{20,28},{24,0},{28,4},{32,40},... | collective-permute-start | bytes 147464 | tf_op jit(solution)/shard_map/ppermute | solution.py:517
  46.0 8.0 %collective-permute-start.5 = (bf16[64,384]{1,0:T(8,128)(2,1)S(1)}, bf16[64,384]{1,0:T(8,128)(2,1)S(1)}, u32[]{:S(2)}, u32[]{:S(2)}) collective-permute-start(bf16[64,384]{1,0:T(8,128)(2,1)S(1)} %pad_maximum_fusion.1), channel_id=1, source_target_pairs={{0,16},{4,20},{8,24},{12,28},{16,0},{20,4},{24,8},{28,12},{32,48},... | collective-permute-start | bytes 147464 | tf_op jit(solution)/shard_map/ppermute | solution.py:517
  49.0 6.1 %collective-permute-start.6 = (bf16[64,384]{1,0:T(8,128)(2,1)S(1)}, bf16[64,384]{1,0:T(8,128)(2,1)S(1)}, u32[]{:S(2)}, u32[]{:S(2)}) collective-permute-start(bf16[64,384]{1,0:T(8,128)(2,1)S(1)} %pad_maximum_fusion.1), channel_id=1, source_target_pairs={{0,24},{4,28},{8,0},{12,4},{16,8},{20,12},{24,16},{28,20},{32,56},... | collective-permute-start | bytes 147464 | tf_op jit(solution)/shard_map/ppermute | solution.py:517
  57.9 1.0 %copy-start = (bf16[8,128,512]{2,1,0:T(8,128)(2,1)}, bf16[8,128,512]{2,1,0:T(8,128)(2,1)S(1)}, u32[]{:S(2)}) copy-start(bf16[8,128,512]{2,1,0:T(8,128)(2,1)S(1)} %get-tuple-element.37) | copy-start | bytes 3145732
  58.8 21.9 %all-to-all-start.2 = ((bf16[8,128,512]{2,1,0:T(8,128)(2,1)}), bf16[8,128,512]{2,1,0:T(8,128)(2,1)S(1)}, u32[]{:S(2)}, u32[]{:S(2)}) async-start(bf16[8,128,512]{2,1,0:T(8,128)(2,1)} %copy-done), calls=%async_computation.2 | async-start | bytes 2097152 | tf_op jit(solution)/shard_map/all_to_all | solution.py:520
  64.6 12.9 %collective-permute-start.7 = (bf16[128,384]{1,0:T(8,128)(2,1)S(1)}, bf16[128,384]{1,0:T(8,128)(2,1)S(1)}, u32[]{:S(2)}, u32[]{:S(2)}) collective-permute-start(bf16[128,384]{1,0:T(8,128)(2,1)S(1)} %pad_maximum_fusion.near), channel_id=1, source_target_pairs={{0,8},{4,12},{8,16},{12,20},{16,24},{20,28},{24,0},{28,4},{32,40},... | collective-permute-start | bytes 294920 | tf_op jit(solution)/shard_map/ppermute | solution.py:517
  67.9 10.5 %collective-permute-start.8 = (bf16[128,384]{1,0:T(8,128)(2,1)S(1)}, bf16[128,384]{1,0:T(8,128)(2,1)S(1)}, u32[]{:S(2)}, u32[]{:S(2)}) collective-permute-start(bf16[128,384]{1,0:T(8,128)(2,1)S(1)} %pad_maximum_fusion.near), channel_id=1, source_target_pairs={{0,16},{4,20},{8,24},{12,28},{16,0},{20,4},{24,8},{28,12},{32,48},... | collective-permute-start | bytes 294920 | tf_op jit(solution)/shard_map/ppermute | solution.py:517
  71.2 7.7 %collective-permute-start.9 = (bf16[128,384]{1,0:T(8,128)(2,1)S(1)}, bf16[128,384]{1,0:T(8,128)(2,1)S(1)}, u32[]{:S(2)}, u32[]{:S(2)}) collective-permute-start(bf16[128,384]{1,0:T(8,128)(2,1)S(1)} %pad_maximum_fusion.near), channel_id=1, source_target_pairs={{0,24},{4,28},{8,0},{12,4},{16,8},{20,12},{24,16},{28,20},{32,56},... | collective-permute-start | bytes 294920 | tf_op jit(solution)/shard_map/ppermute | solution.py:517

commit v4 on v3

--- a/solution.py
+++ b/solution.py
@@ -184,8 +184,9 @@
     return jnp.concatenate(parts, axis=0)
 
 
-def rows_kernel(offsets, k, v, copies):
+def rows_kernel(offsets, k, v, own, copies):
     both = jnp.concatenate([paired_rows(offsets, k), paired_rows(offsets, v)], axis=1).astype(BF)
+    own[...] = both
     for i in range(GROUP):
         copies[i] = both
 
@@ -466,14 +467,14 @@
     out[:, FEAT:] = folded(part_v, TOKENS, second_mask)[:, LANES - FEAT :]
 
 
-def level1_keys_kernel(offsets, counts, copies, near, far2, far4, far6, st1, level0, out, qs, gs):
+def level1_keys_kernel(offsets, counts, own, near, far2, far4, far6, st1, level0, out, qs, gs):
     for i in range(GROUP):
         block = (near, far2, far4, far6)[i // 2][(i & 1) * ROWS1 : (i & 1) * ROWS1 + ROWS1]
         helpers = st1[i * ROWS1 : (i + 1) * ROWS1]
         qs[i * ROWS1 : (i + 1) * ROWS1] = first_view(block, helpers)
         gs[i * ROWS1 : (i + 1) * ROWS1] = second_view(block, helpers)
     mine = key_helpers(dilated_mask(offsets, 0, counts[lax.axis_index("seq")]))
-    block = copies[0, :ROWS1]
+    block = own[:ROWS1]
     k1 = head_stack(first_view(block, mine), first_mask)
     v1 = head_stack(second_view(block, mine), second_mask)
     k1_part, v1_part = key_back(k1, v1, (qs[...],), (gs[...],))
@@ -481,12 +482,12 @@
     out[:, FEAT:] = level0[:, FEAT:] + scatter_rows(offsets, v1_part, None, LANES - FEAT)[:, LANES - FEAT :]
 
 
-def last_kernel(offsets, counts, copies, all_qg, early, dk, dv):
+def last_kernel(offsets, counts, own, all_qg, early, dk, dv):
     full = all_qg[...].reshape(GROUP * GROUP * ROWS2, PAIR + SIDE)
     helpers = full[:, PAIR:]
     queries, grads = first_view(full[:, :PAIR], helpers), second_view(full[:, :PAIR], helpers)
     mine = key_helpers(dilated_mask(offsets, 1, counts[lax.axis_index("seq")]))
-    block = copies[0, ROWS1:]
+    block = own[ROWS1:]
     k2 = head_stack(first_view(block, mine), first_mask)
     v2 = head_stack(second_view(block, mine), second_mask)
     k2_part, v2_part = key_back(k2, v2, (queries,), (grads,))
@@ -524,7 +525,9 @@
         return tuple(shift(both, step) for step in (2, 4, 6))
 
     k_next, v_next = swap(keys, 1), swap(values, 1)
-    (copies,) = call(rows_kernel, [((GROUP, ROWS, PAIR), BF)], 1, offsets, keys, values)
+    own, copies = call(
+        rows_kernel, [((ROWS, PAIR), BF), ((GROUP, ROWS, PAIR), BF)], 1, offsets, keys, values
+    )
     copies, k_next, v_next = lax.optimization_barrier((copies, k_next, v_next))
     ring_kv = exchange(copies, rings)
     flat = (TOKENS, PAIR)
@@ -541,8 +544,8 @@
         scratch=[(2, GROUP * ROWS1, LANES)],
     )
     tail_next = swap(tail, 1)
-    ring_kv, tail_next, qgp = lax.optimization_barrier((ring_kv, tail_next, qgp))
     (repeated,) = call(repeat_kernel, [((GROUP, GROUP * ROWS2, PAIR), BF)], 0, ring_kv)
+    repeated, tail_next, qgp = lax.optimization_barrier((repeated, tail_next, qgp))
     all_kv = exchange(repeated, planes)
     tails = far(tail[: 2 * ROWS2], tail_next[: 2 * ROWS2])
     tails, qgp = lax.optimization_barrier((jnp.concatenate([tail, tail_next, *tails], axis=0), qgp))
@@ -561,10 +564,10 @@
     )
     (level0,) = call(grad_key_kernel, [((TOKENS, PAIR), F32)], 1, counts, kv, qg, st, qgp)
     (early,) = call(
-        level1_keys_kernel, [((TOKENS, PAIR), F32)], 2, offsets, counts, copies, near, *qgs, st1, level0,
+        level1_keys_kernel, [((TOKENS, PAIR), F32)], 2, offsets, counts, own, near, *qgs, st1, level0,
         scratch=[(OWN, LANES)] * 2,
     )
-    dk, dv = call(last_kernel, [((HALF, PAIR), BF)] * 2, 2, offsets, counts, copies, all_qg, early)
+    dk, dv = call(last_kernel, [((HALF, PAIR), BF)] * 2, 2, offsets, counts, own, all_qg, early)
     return dq, dk, dv
 
 

time: 84.7 us -> 81.7 us (0.965); the launches traced: 83.5 us -> 81.3 us
  Pallas kernels: 20.3 us -> 19.3 us
    ppermute x4, waiting for transfers between devices: 4.27 us -> 3.26 us  [swap(): return lax.ppermute(x, 'seq', [(i, i ^ bits) for i in range(n_seq)])]
    pallas_call x11, Pallas kernels: 20.3 us -> 19.3 us  [call(): pl.pallas_call(kernel, out_shape=[jax.ShapeDtypeStruct(s, d) for s, d in...]
    unnamed x26 -> x30, local copies, waits for them, and re-layouts: 4.18 us -> 4.18 us
  transfers between devices with their start and end apart: 13 -> 13, of which waited for: 8 -> 6; matrix products, arithmetic and copies ran while one was open for 0% -> 0% of each run, Pallas kernels for 17% -> 18%
where the time goes in v4:
time: 81.7 us; the launch traced here: 81.3 us
  starting transfers between devices  39.7 us (49%)
  Pallas kernels  19.3 us (24%)
  waiting for transfers between devices  9.01 us (11%)
  blocking collectives  8.29 us (10%)
  local copies, waits for them, and re-layouts  4.21 us (5%)
    all_to_all x3, starting transfers between devices, exchange(): return lax.all_to_all(copies, 'seq', 0, 0, axis_index_groups=groups)  20.1 us
    pallas_call x11, Pallas kernels, call(): pl.pallas_call(kernel, out_shape=[jax.ShapeDtypeStruct(s, d) for s, d in...  19.3 us
    ppermute x6, starting transfers between devices, shift(): lax.ppermute(x, 'seq', [(r[i], r[(i + step) % GROUP]) for r in rings for...  14.7 us
    all_gather x1, blocking collectives, per_device(): gy = lax.all_gather(grad_y, 'head', axis=0)  8.29 us
    ppermute x4, starting transfers between devices, swap(): return lax.ppermute(x, 'seq', [(i, i ^ bits) for i in range(n_seq)])  4.89 us
    unnamed x30, local copies, waits for them, and re-layouts  4.18 us
    ppermute x6, waiting for transfers between devices, shift(): lax.ppermute(x, 'seq', [(r[i], r[(i + step) % GROUP]) for r in rings for...  3.9 us
    ppermute x4, waiting for transfers between devices, swap(): return lax.ppermute(x, 'seq', [(i, i ^ bits) for i in range(n_seq)])  3.26 us
  transfers between devices with their start and end apart: 13, of which 6 were waited for; matrix products, arithmetic and copies ran while one was open for 0% of the time, Pallas kernels for 18%

profile of v4, /device:TPU:2, one launch (start us, length us, event | category | flops | bytes accessed | tf_op | source)
XLA Modules:
  0.0 81.3 jit_solution(17843471841061718794)
XLA Ops:
  0.6 2.0 %collective-permute-start = (bf16[128,384]{1,0:T(8,128)(2,1)}, bf16[128,384]{1,0:T(8,128)(2,1)S(1)}, u32[]{:S(2)}, u32[]{:S(2)}) collective-permute-start(bf16[128,384]{1,0:T(8,128)(2,1)} %k.3), channel_id=1, source_target_pairs={{0,4},{4,0},{8,12},{12,8},{16,20},{20,16},{24,28},{28,24},{32,36},... | collective-permute-start | bytes 294920 | tf_op jit(solution)/shard_map/ppermute | solution.py:515
  2.6 0.1 collective-permute-start.1
  2.7 0.0 copy-start.1
  2.7 0.9 %copy-done.1 = bf16[128,384]{1,0:T(8,128)(2,1)S(1)} copy-done((bf16[128,384]{1,0:T(8,128)(2,1)S(1)}, bf16[128,384]{1,0:T(8,128)(2,1)}, u32[]{:S(2)}) %copy-start.1) | copy-done | bytes 98328
  3.6 0.0 copy-start.3
  3.6 0.9 %copy-done.3 = bf16[128,384]{1,0:T(8,128)(2,1)S(1)} copy-done((bf16[128,384]{1,0:T(8,128)(2,1)S(1)}, bf16[128,384]{1,0:T(8,128)(2,1)}, u32[]{:S(2)}) %copy-start.3) | copy-done | bytes 98328
  4.5 0.0 copy-start.9
  4.5 0.7 copy-done.9
  5.2 1.9 %shard_map.95 = (bf16[80,384]{1,0:T(8,128)(2,1)S(1)}, bf16[8,80,384]{2,1,0:T(8,128)(2,1)}) custom-call(s32[2,16]{1,0:T(2,128)S(1)} %copy-done.9, bf16[128,384]{1,0:T(8,128)(2,1)S(1)} %copy-done.1, bf16[128,384]{1,0:T(8,128)(2,1)S(1)} %copy-done.3), custom_call_target="tpu_custom_call" | custom-call | tf_op jit(solution)/shard_map/pallas_call | solution.py:499
  7.1 0.0 copy-start.6
  7.1 0.0 collective-permute-done.k_next
  7.1 0.6 collective-permute-done.1.v_next
  7.7 0.0 copy-start.12
  7.8 0.0 copy-done.6
  7.8 8.5 %all-to-all-start = ((bf16[8,80,384]{2,1,0:T(8,128)(2,1)}), bf16[8,80,384]{2,1,0:T(8,128)(2,1)S(1)}, u32[]{:S(2)}, u32[]{:S(2)}) async-start(bf16[8,80,384]{2,1,0:T(8,128)(2,1)} %get-tuple-element.27), calls=%async_computation | async-start | bytes 983040 | tf_op jit(solution)/shard_map/all_to_all | solution.py:521
  16.2 0.0 copy-done.12
  16.2 0.0 copy-start.5
  16.2 0.0 copy-start.8
  16.2 8.3 %all-gather = bf16[512,384]{1,0:T(8,128)(2,1)S(1)} all-gather(bf16[128,384]{1,0:T(8,128)(2,1)S(1)} %copy-done.12), channel_id=2, replica_groups=mesh['seq'=64,'head'=4] {'head'}, dimensions={0}, use_global_device_ids=true | all-gather | bytes 491520 | tf_op jit(solution)/shard_map/all_gather | solution.py:535
  24.5 0.0 copy-start.10
  24.5 0.0 copy-start.11
  24.5 0.0 copy-done.5
  24.5 0.0 copy-done.8
  24.6 0.7 copy-done.10
  25.2 0.0 copy-done.11
  25.2 0.0 copy-start.2
  25.2 0.0 copy-start.4
  25.2 1.4 %shard_map.94 = (bf16[320,384]{1,0:T(8,128)(2,1)S(1)}, bf16[16,384]{1,0:T(8,128)(2,1)S(1)}) custom-call(s32[2,16]{1,0:T(2,128)S(1)} %copy-done.10, s32[64]{0:T(128)S(1)} %copy-done.11, bf16[4,128,384]{2,1,0:T(8,128)(2,1)S(1)} %bitcast.1, bf16[192,768]{1,0:T(8,128)(2,1)S(1)} %copy-done.5, bf16[128,384]{1,0:T(8,128)(2,1)S(1)} %copy-done.8), custom_call_target="tpu_custom_call" | custom-call | tf_op jit(solution)/shard_map/pallas_call | solution.py:499
  26.6 2.1 %collective-permute-start.3 = (bf16[320,384]{1,0:T(8,128)(2,1)S(1)}, bf16[320,384]{1,0:T(8,128)(2,1)S(1)}, u32[]{:S(2)}, u32[]{:S(2)}) collective-permute-start(bf16[320,384]{1,0:T(8,128)(2,1)S(1)} %get-tuple-element.24.qg), channel_id=1, source_target_pairs={{0,4},{4,0},{8,12},{12,8},{16,20},{20,16},{24,28},{28,24},{32,36},... | collective-permute-start | bytes 737288 | tf_op jit(solution)/shard_map/ppermute | solution.py:515
  28.7 0.0 copy-done.2
  28.7 0.0 copy-done.4
  28.7 0.4 shard_map.96
  29.1 1.5 %shard_map.97.stats = f32[16,256]{1,0:T(8,128)S(1)} custom-call(s32[64]{0:T(128)S(1)} %copy-done.11, bf16[320,384]{1,0:T(8,128)(2,1)S(1)} %get-tuple-element.24.qg, bf16[256,384]{1,0:T(8,128)(2,1)S(1)} %get-tuple-element.30.kv, bf16[256,384]{1,0:T(8,128)(2,1)S(1)} %get-tuple-element.31.kvp), custom_call_target="tpu_custom_call" | custom-call | tf_op jit(solution)/shard_map/pallas_call | solution.py:499
  30.6 1.8 %all-to-all-done.rows.rows1 = bf16[8,80,384]{2,1,0:T(8,128)(2,1)S(1)} async-done(((bf16[8,80,384]{2,1,0:T(8,128)(2,1)}), bf16[8,80,384]{2,1,0:T(8,128)(2,1)S(1)}, u32[]{:S(2)}, u32[]{:S(2)}) %all-to-all-start) | async-done | bytes 491552 | tf_op jit(solution)/shard_map/all_to_all | solution.py:521
  32.5 1.6 %shard_map.98 = bf16[80,384]{1,0:T(8,128)(2,1)S(1)} custom-call(s32[2,16]{1,0:T(2,128)S(1)} %copy-done.10, s32[64]{0:T(128)S(1)} %copy-done.11, bf16[320,384]{1,0:T(8,128)(2,1)S(1)} %get-tuple-element.24.qg, bf16[16,384]{1,0:T(8,128)(2,1)S(1)} %get-tuple-element.25.qg_top, bf16[8,80,384]{2,1,0:T(8,128)(2,1)S(1)} %all-to-all-done.rows.rows1, ...), custom_call_target="tpu_custom_call" | custom-call | tf_op jit(solution)/shard_map/pallas_call | solution.py:499
  34.1 0.7 collective-permute-start.2
  34.8 1.0 %shard_map.99 = bf16[8,128,384]{2,1,0:T(8,128)(2,1)} custom-call(bf16[8,80,384]{2,1,0:T(8,128)(2,1)S(1)} %all-to-all-done.rows.rows1), custom_call_target="tpu_custom_call" | custom-call | tf_op jit(solution)/shard_map/pallas_call | solution.py:499
  35.8 0.0 collective-permute-done.3.qgp
  35.8 2.6 %collective-permute-done.2 = bf16[80,384]{1,0:T(8,128)(2,1)S(1)} collective-permute-done((bf16[80,384]{1,0:T(8,128)(2,1)S(1)}, bf16[80,384]{1,0:T(8,128)(2,1)S(1)}, u32[]{:S(2)}, u32[]{:S(2)}) %collective-permute-start.2) | collective-permute-done | bytes 61472 | tf_op jit(solution)/shard_map/ppermute | solution.py:515
  38.4 5.9 %all-to-all-start.1 = ((bf16[8,128,384]{2,1,0:T(8,128)(2,1)}), bf16[8,128,384]{2,1,0:T(8,128)(2,1)S(1)}, u32[]{:S(2)}, u32[]{:S(2)}) async-start(bf16[8,128,384]{2,1,0:T(8,128)(2,1)} %shard_map.99), calls=%async_computation.1 | async-start | bytes 1572864 | tf_op jit(solution)/shard_map/all_to_all | solution.py:521
  44.4 0.9 %collective-permute-start.4 = (bf16[64,384]{1,0:T(8,128)(2,1)S(1)}, bf16[64,384]{1,0:T(8,128)(2,1)S(1)}, u32[]{:S(2)}, u32[]{:S(2)}) collective-permute-start(bf16[64,384]{1,0:T(8,128)(2,1)S(1)} %pad_maximum_fusion.1), channel_id=1, source_target_pairs={{0,8},{4,12},{8,16},{12,20},{16,24},{20,28},{24,0},{28,4},{32,40},... | collective-permute-start | bytes 147464 | tf_op jit(solution)/shard_map/ppermute | solution.py:518
  45.2 2.9 %collective-permute-start.5 = (bf16[64,384]{1,0:T(8,128)(2,1)S(1)}, bf16[64,384]{1,0:T(8,128)(2,1)S(1)}, u32[]{:S(2)}, u32[]{:S(2)}) collective-permute-start(bf16[64,384]{1,0:T(8,128)(2,1)S(1)} %pad_maximum_fusion.1), channel_id=1, source_target_pairs={{0,16},{4,20},{8,24},{12,28},{16,0},{20,4},{24,8},{28,12},{32,48},... | collective-permute-start | bytes 147464 | tf_op jit(solution)/shard_map/ppermute | solution.py:518
  48.2 3.6 %collective-permute-start.6 = (bf16[64,384]{1,0:T(8,128)(2,1)S(1)}, bf16[64,384]{1,0:T(8,128)(2,1)S(1)}, u32[]{:S(2)}, u32[]{:S(2)}) collective-permute-start(bf16[64,384]{1,0:T(8,128)(2,1)S(1)} %pad_maximum_fusion.1), channel_id=1, source_target_pairs={{0,24},{4,28},{8,0},{12,4},{16,8},{20,12},{24,16},{28,20},{32,56},... | collective-permute-start | bytes 147464 | tf_op jit(solution)/shard_map/ppermute | solution.py:518
  51.8 0.0 collective-permute-done.4
  51.8 1.5 %collective-permute-done.5 = bf16[64,384]{1,0:T(8,128)(2,1)S(1)} collective-permute-done((bf16[64,384]{1,0:T(8,128)(2,1)S(1)}, bf16[64,384]{1,0:T(8,128)(2,1)S(1)}, u32[]{:S(2)}, u32[]{:S(2)}) %collective-permute-start.5) | collective-permute-done | bytes 49184 | tf_op jit(solution)/shard_map/ppermute | solution.py:518
  53.3 1.5 %collective-permute-done.6 = bf16[64,384]{1,0:T(8,128)(2,1)S(1)} collective-permute-done((bf16[64,384]{1,0:T(8,128)(2,1)S(1)}, bf16[64,384]{1,0:T(8,128)(2,1)S(1)}, u32[]{:S(2)}, u32[]{:S(2)}) %collective-permute-start.6) | collective-permute-done | bytes 49184 | tf_op jit(solution)/shard_map/ppermute | solution.py:518
  54.7 0.0 all-to-all-done.1.rows.rows2
  54.7 2.7 %shard_map.100 = (bf16[512,128]{1,0:T(8,128)(2,1)S(1)}, bf16[640,128]{1,0:T(8,128)(2,1)S(1)}, bf16[8,128,512]{2,1,0:T(8,128)(2,1)S(1)}) custom-call(s32[2,16]{1,0:T(2,128)S(1)} %copy-done.10, s32[64]{0:T(128)S(1)} %copy-done.11, bf16[352,384]{1,0:T(8,128)(2,1)S(1)} %constant_dynamic-update-slice_fusion.tails, bf16[8,128,384]{2,1,0:T(8,128)(2,1)S(1)} %all-to-all-done.1.rows.rows2), custom_call_target="tpu_custom_call" | custom-call | tf_op jit(solution)/shard_map/pallas_call | solution.py:499
  57.5 0.0 copy-start
  57.5 1.0 %copy-done = bf16[8,128,512]{2,1,0:T(8,128)(2,1)} copy-done((bf16[8,128,512]{2,1,0:T(8,128)(2,1)}, bf16[8,128,512]{2,1,0:T(8,128)(2,1)S(1)}, u32[]{:S(2)}) %copy-start) | copy-done | bytes 1048600
  58.4 5.7 %all-to-all-start.2 = ((bf16[8,128,512]{2,1,0:T(8,128)(2,1)}), bf16[8,128,512]{2,1,0:T(8,128)(2,1)S(1)}, u32[]{:S(2)}, u32[]{:S(2)}) async-start(bf16[8,128,512]{2,1,0:T(8,128)(2,1)} %copy-done), calls=%async_computation.2 | async-start | bytes 2097152 | tf_op jit(solution)/shard_map/all_to_all | solution.py:521
  64.2 3.2 %collective-permute-start.7 = (bf16[128,384]{1,0:T(8,128)(2,1)S(1)}, bf16[128,384]{1,0:T(8,128)(2,1)S(1)}, u32[]{:S(2)}, u32[]{:S(2)}) collective-permute-start(bf16[128,384]{1,0:T(8,128)(2,1)S(1)} %pad_maximum_fusion.near), channel_id=1, source_target_pairs={{0,8},{4,12},{8,16},{12,20},{16,24},{20,28},{24,0},{28,4},{32,40},... | collective-permute-start | bytes 294920 | tf_op jit(solution)/shard_map/ppermute | solution.py:518
  67.4 3.0 %collective-permute-start.8 = (bf16[128,384]{1,0:T(8,128)(2,1)S(1)}, bf16[128,384]{1,0:T(8,128)(2,1)S(1)}, u32[]{:S(2)}, u32[]{:S(2)}) collective-permute-start(bf16[128,384]{1,0:T(8,128)(2,1)S(1)} %pad_maximum_fusion.near), channel_id=1, source_target_pairs={{0,16},{4,20},{8,24},{12,28},{16,0},{20,4},{24,8},{28,12},{32,48},... | collective-permute-start | bytes 294920 | tf_op jit(solution)/shard_map/ppermute | solution.py:518
  70.4 1.1 %collective-permute-start.9 = (bf16[128,384]{1,0:T(8,128)(2,1)S(1)}, bf16[128,384]{1,0:T(8,128)(2,1)S(1)}, u32[]{:S(2)}, u32[]{:S(2)}) collective-permute-start(bf16[128,384]{1,0:T(8,128)(2,1)S(1)} %pad_maximum_fusion.near), channel_id=1, source_target_pairs={{0,24},{4,28},{8,0},{12,4},{16,8},{20,12},{24,16},{28,20},{32,56},... | collective-permute-start | bytes 294920 | tf_op jit(solution)/shard_map/ppermute | solution.py:518
  71.5 1.8 %shard_map.102.level0 = f32[256,384]{1,0:T(8,128)S(1)} custom-call(s32[64]{0:T(128)S(1)} %copy-done.11, bf16[256,384]{1,0:T(8,128)(2,1)S(1)} %get-tuple-element.30.kv, bf16[320,384]{1,0:T(8,128)(2,1)S(1)} %get-tuple-element.24.qg, bf16[640,128]{1,0:T(8,128)(2,1)S(1)} %get-tuple-element.39.st, bf16[320,384]{1,0:T(8,128)(2,1)S(1)} %collective-permute-done.3.qgp), custom_call_target="tpu_custom_call" | custom-call | tf_op jit(solution)/shard_map/pallas_call | solution.py:499
  73.4 0.0 copy-start.7
  73.4 3.3 %shard_map.101 = bf16[128,384]{1,0:T(8,128)(2,1)} custom-call(s32[2,16]{1,0:T(2,128)S(1)} %copy-done.10, s32[64]{0:T(128)S(1)} %copy-done.11, bf16[320,384]{1,0:T(8,128)(2,1)S(1)} %get-tuple-element.24.qg, bf16[16,384]{1,0:T(8,128)(2,1)S(1)} %get-tuple-element.25.qg_top, bf16[512,128]{1,0:T(8,128)(2,1)S(1)} %get-tuple-element.38.st1, ...), custom_call_target="tpu_custom_call" | custom-call | tf_op jit(solution)/shard_map/pallas_call | solution.py:499
  76.7 0.0 collective-permute-done.7.far2
  76.7 0.0 collective-permute-done.8.far4
  76.7 1.0 %collective-permute-done.9.far6 = bf16[128,384]{1,0:T(8,128)(2,1)S(1)} collective-permute-done((bf16[128,384]{1,0:T(8,128)(2,1)S(1)}, bf16[128,384]{1,0:T(8,128)(2,1)S(1)}, u32[]{:S(2)}, u32[]{:S(2)}) %collective-permute-start.9) | collective-permute-done | bytes 98336 | tf_op jit(solution)/shard_map/ppermute | solution.py:518
  77.7 0.0 copy-done.7
  77.7 1.4 %shard_map.103.early = f32[256,384]{1,0:T(8,128)S(1)} custom-call(s32[2,16]{1,0:T(2,128)S(1)} %copy-done.10, s32[64]{0:T(128)S(1)} %copy-done.11, bf16[80,384]{1,0:T(8,128)(2,1)S(1)} %copy-done.7, bf16[128,384]{1,0:T(8,128)(2,1)S(1)} %pad_maximum_fusion.near, bf16[128,384]{1,0:T(8,128)(2,1)S(1)} %collective-permute-done.7.far2, ...), custom_call_target="tpu_custom_call" | custom-call | tf_op jit(solution)/shard_map/pallas_call | solution.py:499
  79.1 0.0 all-to-all-done.2.all_qg
  79.1 2.2 %shard_map.104 = (bf16[128,384]{1,0:T(8,128)(2,1)}, bf16[128,384]{1,0:T(8,128)(2,1)}) custom-call(s32[2,16]{1,0:T(2,128)S(1)} %copy-done.10, s32[64]{0:T(128)S(1)} %copy-done.11, bf16[80,384]{1,0:T(8,128)(2,1)S(1)} %copy-done.7, bf16[8,128,512]{2,1,0:T(8,128)(2,1)S(1)} %all-to-all-done.2.all_qg, f32[256,384]{1,0:T(8,128)S(1)} %shard_map.103.early), custom_call_target="tpu_custom_call" | custom-call | tf_op jit(solution)/shard_map/pallas_call | solution.py:499
  (11 shorter events, 0.1 us)
Async XLA Ops:
  0.6 6.5 %collective-permute-start = (bf16[128,384]{1,0:T(8,128)(2,1)}, bf16[128,384]{1,0:T(8,128)(2,1)S(1)}, u32[]{:S(2)}, u32[]{:S(2)}) collective-permute-start(bf16[128,384]{1,0:T(8,128)(2,1)} %k.3), channel_id=1, source_target_pairs={{0,4},{4,0},{8,12},{12,8},{16,20},{20,16},{24,28},{28,24},{32,36},... | collective-permute-start | bytes 294920 | tf_op jit(solution)/shard_map/ppermute | solution.py:515
  2.6 5.1 %collective-permute-start.1 = (bf16[128,384]{1,0:T(8,128)(2,1)}, bf16[128,384]{1,0:T(8,128)(2,1)S(1)}, u32[]{:S(2)}, u32[]{:S(2)}) collective-permute-start(bf16[128,384]{1,0:T(8,128)(2,1)} %v.3), channel_id=1, source_target_pairs={{0,4},{4,0},{8,12},{12,8},{16,20},{20,16},{24,28},{28,24},{32,36},... | collective-permute-start | bytes 294920 | tf_op jit(solution)/shard_map/ppermute | solution.py:515
  2.7 0.9 %copy-start.1 = (bf16[128,384]{1,0:T(8,128)(2,1)S(1)}, bf16[128,384]{1,0:T(8,128)(2,1)}, u32[]{:S(2)}) copy-start(bf16[128,384]{1,0:T(8,128)(2,1)} %k.3) | copy-start | bytes 294916
  3.6 0.9 %copy-start.3 = (bf16[128,384]{1,0:T(8,128)(2,1)S(1)}, bf16[128,384]{1,0:T(8,128)(2,1)}, u32[]{:S(2)}) copy-start(bf16[128,384]{1,0:T(8,128)(2,1)} %v.3) | copy-start | bytes 294916
  4.5 0.7 copy-start.9
  7.1 0.6 copy-start.6
  7.7 8.5 %copy-start.12 = (bf16[128,384]{1,0:T(8,128)(2,1)S(1)}, bf16[128,384]{1,0:T(8,128)(2,1)}, u32[]{:S(2)}) copy-start(bf16[128,384]{1,0:T(8,128)(2,1)} %param.10) | copy-start | bytes 294916
  7.8 24.7 %all-to-all-start = ((bf16[8,80,384]{2,1,0:T(8,128)(2,1)}), bf16[8,80,384]{2,1,0:T(8,128)(2,1)S(1)}, u32[]{:S(2)}, u32[]{:S(2)}) async-start(bf16[8,80,384]{2,1,0:T(8,128)(2,1)} %get-tuple-element.27), calls=%async_computation | async-start | bytes 983040 | tf_op jit(solution)/shard_map/all_to_all | solution.py:521
  16.2 8.3 %copy-start.5 = (bf16[192,768]{1,0:T(8,128)(2,1)S(1)}, bf16[192,768]{1,0:T(8,128)(2,1)}, u32[]{:S(2)}) copy-start(bf16[192,768]{1,0:T(8,128)(2,1)} %w.1) | copy-start | bytes 884740
  16.2 8.3 %copy-start.8 = (bf16[128,384]{1,0:T(8,128)(2,1)S(1)}, bf16[128,384]{1,0:T(8,128)(2,1)}, u32[]{:S(2)}) copy-start(bf16[128,384]{1,0:T(8,128)(2,1)} %q.1) | copy-start | bytes 294916
  24.5 0.7 copy-start.10
  24.5 0.7 copy-start.11
  25.2 3.5 %copy-start.2 = (bf16[128,384]{1,0:T(8,128)(2,1)S(1)}, bf16[128,384]{1,0:T(8,128)(2,1)}, u32[]{:S(2)}) copy-start(bf16[128,384]{1,0:T(8,128)(2,1)} %k.3) | copy-start | bytes 294916
  25.2 3.5 %copy-start.4 = (bf16[128,384]{1,0:T(8,128)(2,1)S(1)}, bf16[128,384]{1,0:T(8,128)(2,1)}, u32[]{:S(2)}) copy-start(bf16[128,384]{1,0:T(8,128)(2,1)} %v.3) | copy-start | bytes 294916
  26.6 9.1 %collective-permute-start.3 = (bf16[320,384]{1,0:T(8,128)(2,1)S(1)}, bf16[320,384]{1,0:T(8,128)(2,1)S(1)}, u32[]{:S(2)}, u32[]{:S(2)}) collective-permute-start(bf16[320,384]{1,0:T(8,128)(2,1)S(1)} %get-tuple-element.24.qg), channel_id=1, source_target_pairs={{0,4},{4,0},{8,12},{12,8},{16,20},{20,16},{24,28},{28,24},{32,36},... | collective-permute-start | bytes 737288 | tf_op jit(solution)/shard_map/ppermute | solution.py:515
  34.1 4.3 %collective-permute-start.2 = (bf16[80,384]{1,0:T(8,128)(2,1)S(1)}, bf16[80,384]{1,0:T(8,128)(2,1)S(1)}, u32[]{:S(2)}, u32[]{:S(2)}) collective-permute-start(bf16[80,384]{1,0:T(8,128)(2,1)S(1)} %shard_map.98), channel_id=1, source_target_pairs={{0,4},{4,0},{8,12},{12,8},{16,20},{20,16},{24,28},{28,24},{32,36},... | collective-permute-start | bytes 184328 | tf_op jit(solution)/shard_map/ppermute | solution.py:515
  38.4 16.3 %all-to-all-start.1 = ((bf16[8,128,384]{2,1,0:T(8,128)(2,1)}), bf16[8,128,384]{2,1,0:T(8,128)(2,1)S(1)}, u32[]{:S(2)}, u32[]{:S(2)}) async-start(bf16[8,128,384]{2,1,0:T(8,128)(2,1)} %shard_map.99), calls=%async_computation.1 | async-start | bytes 1572864 | tf_op jit(solution)/shard_map/all_to_all | solution.py:521
  44.4 7.4 %collective-permute-start.4 = (bf16[64,384]{1,0:T(8,128)(2,1)S(1)}, bf16[64,384]{1,0:T(8,128)(2,1)S(1)}, u32[]{:S(2)}, u32[]{:S(2)}) collective-permute-start(bf16[64,384]{1,0:T(8,128)(2,1)S(1)} %pad_maximum_fusion.1), channel_id=1, source_target_pairs={{0,8},{4,12},{8,16},{12,20},{16,24},{20,28},{24,0},{28,4},{32,40},... | collective-permute-start | bytes 147464 | tf_op jit(solution)/shard_map/ppermute | solution.py:518
  45.2 8.0 %collective-permute-start.5 = (bf16[64,384]{1,0:T(8,128)(2,1)S(1)}, bf16[64,384]{1,0:T(8,128)(2,1)S(1)}, u32[]{:S(2)}, u32[]{:S(2)}) collective-permute-start(bf16[64,384]{1,0:T(8,128)(2,1)S(1)} %pad_maximum_fusion.1), channel_id=1, source_target_pairs={{0,16},{4,20},{8,24},{12,28},{16,0},{20,4},{24,8},{28,12},{32,48},... | collective-permute-start | bytes 147464 | tf_op jit(solution)/shard_map/ppermute | solution.py:518
  48.2 6.5 %collective-permute-start.6 = (bf16[64,384]{1,0:T(8,128)(2,1)S(1)}, bf16[64,384]{1,0:T(8,128)(2,1)S(1)}, u32[]{:S(2)}, u32[]{:S(2)}) collective-permute-start(bf16[64,384]{1,0:T(8,128)(2,1)S(1)} %pad_maximum_fusion.1), channel_id=1, source_target_pairs={{0,24},{4,28},{8,0},{12,4},{16,8},{20,12},{24,16},{28,20},{32,56},... | collective-permute-start | bytes 147464 | tf_op jit(solution)/shard_map/ppermute | solution.py:518
  57.5 1.0 %copy-start = (bf16[8,128,512]{2,1,0:T(8,128)(2,1)}, bf16[8,128,512]{2,1,0:T(8,128)(2,1)S(1)}, u32[]{:S(2)}) copy-start(bf16[8,128,512]{2,1,0:T(8,128)(2,1)S(1)} %get-tuple-element.41) | copy-start | bytes 3145732
  58.4 20.6 %all-to-all-start.2 = ((bf16[8,128,512]{2,1,0:T(8,128)(2,1)}), bf16[8,128,512]{2,1,0:T(8,128)(2,1)S(1)}, u32[]{:S(2)}, u32[]{:S(2)}) async-start(bf16[8,128,512]{2,1,0:T(8,128)(2,1)} %copy-done), calls=%async_computation.2 | async-start | bytes 2097152 | tf_op jit(solution)/shard_map/all_to_all | solution.py:521
  64.2 12.5 %collective-permute-start.7 = (bf16[128,384]{1,0:T(8,128)(2,1)S(1)}, bf16[128,384]{1,0:T(8,128)(2,1)S(1)}, u32[]{:S(2)}, u32[]{:S(2)}) collective-permute-start(bf16[128,384]{1,0:T(8,128)(2,1)S(1)} %pad_maximum_fusion.near), channel_id=1, source_target_pairs={{0,8},{4,12},{8,16},{12,20},{16,24},{20,28},{24,0},{28,4},{32,40},... | collective-permute-start | bytes 294920 | tf_op jit(solution)/shard_map/ppermute | solution.py:518
  67.4 9.3 %collective-permute-start.8 = (bf16[128,384]{1,0:T(8,128)(2,1)S(1)}, bf16[128,384]{1,0:T(8,128)(2,1)S(1)}, u32[]{:S(2)}, u32[]{:S(2)}) collective-permute-start(bf16[128,384]{1,0:T(8,128)(2,1)S(1)} %pad_maximum_fusion.near), channel_id=1, source_target_pairs={{0,16},{4,20},{8,24},{12,28},{16,0},{20,4},{24,8},{28,12},{32,48},... | collective-permute-start | bytes 294920 | tf_op jit(solution)/shard_map/ppermute | solution.py:518
  70.4 7.3 %collective-permute-start.9 = (bf16[128,384]{1,0:T(8,128)(2,1)S(1)}, bf16[128,384]{1,0:T(8,128)(2,1)S(1)}, u32[]{:S(2)}, u32[]{:S(2)}) collective-permute-start(bf16[128,384]{1,0:T(8,128)(2,1)S(1)} %pad_maximum_fusion.near), channel_id=1, source_target_pairs={{0,24},{4,28},{8,0},{12,4},{16,8},{20,12},{24,16},{28,20},{32,56},... | collective-permute-start | bytes 294920 | tf_op jit(solution)/shard_map/ppermute | solution.py:518
  73.4 4.3 %copy-start.7 = (bf16[80,384]{1,0:T(8,128)(2,1)S(1)}, bf16[80,384]{1,0:T(8,128)(2,1)}, u32[]{:S(2)}) copy-start(bf16[80,384]{1,0:T(8,128)(2,1)} %copy-done.6) | copy-start | bytes 184324

commit v5 on v4

--- a/solution.py
+++ b/solution.py
@@ -184,7 +184,14 @@
     return jnp.concatenate(parts, axis=0)
 
 
-def rows_kernel(offsets, k, v, own, copies):
+def rows_kernel(offsets_far, k_far, v_far, own, copies, offsets, k, v, *semaphores):
+    moves = [
+        pltpu.make_async_copy(*x) for x in zip((offsets_far, k_far, v_far), (offsets, k, v), semaphores)
+    ]
+    for m in moves:
+        m.start()
+    for m in moves:
+        m.wait()
     both = jnp.concatenate([paired_rows(offsets, k), paired_rows(offsets, v)], axis=1).astype(BF)
     own[...] = both
     for i in range(GROUP):
@@ -506,6 +513,18 @@
     )(*args)
 
 
+def first_call(offsets, keys, values):
+    return pl.pallas_call(
+        rows_kernel,
+        out_shape=[jax.ShapeDtypeStruct(s, BF) for s in ((ROWS, PAIR), (GROUP, ROWS, PAIR))],
+        in_specs=[pl.BlockSpec(memory_space=pl.ANY)] * 3,
+        out_specs=[VMEM] * 2,
+        scratch_shapes=[pltpu.SMEM(offsets.shape, offsets.dtype), pltpu.VMEM(keys.shape, BF), pltpu.VMEM(values.shape, BF)]
+        + [pltpu.SemaphoreType.DMA(())] * 3,
+        compiler_params=pltpu.CompilerParams(vmem_limit_bytes=60 * 1024 * 1024),
+    )(offsets, keys, values)
+
+
 def per_device(queries, keys, values, grad_y, out_weight, counts, offsets):
     n_seq = lax.axis_size("seq")
     rings = [[GROUP * b + i for i in range(GROUP)] for b in range(n_seq // GROUP)]
@@ -525,9 +544,7 @@
         return tuple(shift(both, step) for step in (2, 4, 6))
 
     k_next, v_next = swap(keys, 1), swap(values, 1)
-    own, copies = call(
-        rows_kernel, [((ROWS, PAIR), BF), ((GROUP, ROWS, PAIR), BF)], 1, offsets, keys, values
-    )
+    own, copies = first_call(offsets, keys, values)
     copies, k_next, v_next = lax.optimization_barrier((copies, k_next, v_next))
     ring_kv = exchange(copies, rings)
     flat = (TOKENS, PAIR)

time: 81.7 us -> 82.7 us (1.012)
  local copies, waits for them, and re-layouts: 4.21 us -> 1.76 us
  waiting for transfers between devices: 9.01 us -> 10.6 us
    unnamed x30 -> x22, local copies, waits for them, and re-layouts: 4.18 us -> 1.73 us
    pallas_call x0 -> x1, Pallas kernels: none -> 2.38 us  [first_call(): pl.pallas_call(rows_kernel, out_shape=[jax.ShapeDtypeStruct(s, BF) for s...]
    ppermute x4, waiting for transfers between devices: 3.26 us -> 5.31 us  [swap(): return lax.ppermute(x, 'seq', [(i, i ^ bits) for i in range(n_seq)])]
    pallas_call x11 -> x10, Pallas kernels: 19.3 us -> 17.5 us  [call(): pl.pallas_call(kernel, out_shape=[jax.ShapeDtypeStruct(s, d) for s, d in...]
  transfers between devices with their start and end apart: 13 -> 13, of which waited for: 6 -> 8; matrix products, arithmetic and copies ran while one was open for 0% -> 0% of each run, Pallas kernels for 18% -> 18%
where the time goes in v5:
time: 82.7 us; the launch traced here: 81.7 us
  starting transfers between devices  40.3 us (49%)
  Pallas kernels  19.9 us (24%)
  waiting for transfers between devices  10.6 us (13%)
  blocking collectives  8.29 us (10%)
  local copies, waits for them, and re-layouts  1.76 us (2%)
    all_to_all x3, starting transfers between devices, exchange(): return lax.all_to_all(copies, 'seq', 0, 0, axis_index_groups=groups)  20.1 us
    pallas_call x10, Pallas kernels, call(): pl.pallas_call(kernel, out_shape=[jax.ShapeDtypeStruct(s, d) for s, d in...  17.5 us
    ppermute x6, starting transfers between devices, shift(): lax.ppermute(x, 'seq', [(r[i], r[(i + step) % GROUP]) for r in rings for...  15.4 us
    all_gather x1, blocking collectives, per_device(): gy = lax.all_gather(grad_y, 'head', axis=0)  8.29 us
    ppermute x4, waiting for transfers between devices, swap(): return lax.ppermute(x, 'seq', [(i, i ^ bits) for i in range(n_seq)])  5.31 us
    ppermute x4, starting transfers between devices, swap(): return lax.ppermute(x, 'seq', [(i, i ^ bits) for i in range(n_seq)])  4.86 us
    ppermute x6, waiting for transfers between devices, shift(): lax.ppermute(x, 'seq', [(r[i], r[(i + step) % GROUP]) for r in rings for...  3.77 us
    pallas_call x1, Pallas kernels, first_call(): pl.pallas_call(rows_kernel, out_shape=[jax.ShapeDtypeStruct(s, BF) for s...  2.38 us
  transfers between devices with their start and end apart: 13, of which 8 were waited for; matrix products, arithmetic and copies ran while one was open for 0% of the time, Pallas kernels for 18%

profile of v5, /device:TPU:2, one launch (start us, length us, event | category | flops | bytes accessed | tf_op | source)
XLA Modules:
  0.0 81.7 jit_solution(1633560848393679667)
XLA Ops:
  0.6 2.0 %collective-permute-start = (bf16[128,384]{1,0:T(8,128)(2,1)}, bf16[128,384]{1,0:T(8,128)(2,1)S(1)}, u32[]{:S(2)}, u32[]{:S(2)}) collective-permute-start(bf16[128,384]{1,0:T(8,128)(2,1)} %k.1), channel_id=1, source_target_pairs={{0,4},{4,0},{8,12},{12,8},{16,20},{20,16},{24,28},{28,24},{32,36},... | collective-permute-start | bytes 294920 | tf_op jit(solution)/shard_map/ppermute | solution.py:534
  2.6 0.1 collective-permute-start.1
  2.7 2.4 %shard_map.95 = (bf16[80,384]{1,0:T(8,128)(2,1)}, bf16[8,80,384]{2,1,0:T(8,128)(2,1)}) custom-call(s32[2,16]{1,0:T(2,128)} %offsets.11, bf16[128,384]{1,0:T(8,128)(2,1)} %k.1, bf16[128,384]{1,0:T(8,128)(2,1)} %v.1), custom_call_target="tpu_custom_call" | custom-call | tf_op jit(solution)/shard_map/pallas_call | solution.py:517
  5.1 1.2 %collective-permute-done.k_next = bf16[128,384]{1,0:T(8,128)(2,1)S(1)} collective-permute-done((bf16[128,384]{1,0:T(8,128)(2,1)}, bf16[128,384]{1,0:T(8,128)(2,1)S(1)}, u32[]{:S(2)}, u32[]{:S(2)}) %collective-permute-start) | collective-permute-done | bytes 98336 | tf_op jit(solution)/shard_map/ppermute | solution.py:534
  6.4 1.4 %collective-permute-done.1.v_next = bf16[128,384]{1,0:T(8,128)(2,1)S(1)} collective-permute-done((bf16[128,384]{1,0:T(8,128)(2,1)}, bf16[128,384]{1,0:T(8,128)(2,1)S(1)}, u32[]{:S(2)}, u32[]{:S(2)}) %collective-permute-start.1) | collective-permute-done | bytes 98336 | tf_op jit(solution)/shard_map/ppermute | solution.py:534
  7.7 0.0 copy-start.8
  7.8 8.4 %all-to-all-start = ((bf16[8,80,384]{2,1,0:T(8,128)(2,1)}), bf16[8,80,384]{2,1,0:T(8,128)(2,1)S(1)}, u32[]{:S(2)}, u32[]{:S(2)}) async-start(bf16[8,80,384]{2,1,0:T(8,128)(2,1)} %get-tuple-element.27), calls=%async_computation | async-start | bytes 983040 | tf_op jit(solution)/shard_map/all_to_all | solution.py:540
  16.2 0.0 copy-done.8
  16.2 0.0 copy-start.3
  16.2 0.0 copy-start.5
  16.2 8.3 %all-gather = bf16[512,384]{1,0:T(8,128)(2,1)S(1)} all-gather(bf16[128,384]{1,0:T(8,128)(2,1)S(1)} %copy-done.8), channel_id=2, replica_groups=mesh['seq'=64,'head'=4] {'head'}, dimensions={0}, use_global_device_ids=true | all-gather | bytes 491520 | tf_op jit(solution)/shard_map/all_gather | solution.py:552
  24.5 0.0 copy-start.6
  24.5 0.0 copy-start.7
  24.5 0.0 copy-done.3
  24.5 0.0 copy-done.5
  24.5 0.7 copy-done.6
  25.2 0.0 copy-done.7
  25.2 0.0 copy-start.1
  25.2 0.0 copy-start.2
  25.2 1.4 %shard_map.94 = (bf16[320,384]{1,0:T(8,128)(2,1)S(1)}, bf16[16,384]{1,0:T(8,128)(2,1)S(1)}) custom-call(s32[2,16]{1,0:T(2,128)S(1)} %copy-done.6, s32[64]{0:T(128)S(1)} %copy-done.7, bf16[4,128,384]{2,1,0:T(8,128)(2,1)S(1)} %bitcast.1, bf16[192,768]{1,0:T(8,128)(2,1)S(1)} %copy-done.3, bf16[128,384]{1,0:T(8,128)(2,1)S(1)} %copy-done.5), custom_call_target="tpu_custom_call" | custom-call | tf_op jit(solution)/shard_map/pallas_call | solution.py:506
  26.6 2.1 %collective-permute-start.3 = (bf16[320,384]{1,0:T(8,128)(2,1)S(1)}, bf16[320,384]{1,0:T(8,128)(2,1)S(1)}, u32[]{:S(2)}, u32[]{:S(2)}) collective-permute-start(bf16[320,384]{1,0:T(8,128)(2,1)S(1)} %get-tuple-element.24.qg), channel_id=1, source_target_pairs={{0,4},{4,0},{8,12},{12,8},{16,20},{20,16},{24,28},{28,24},{32,36},... | collective-permute-start | bytes 737288 | tf_op jit(solution)/shard_map/ppermute | solution.py:534
  28.7 0.0 copy-done.1
  28.7 0.0 copy-done.2
  28.7 0.4 shard_map.96
  29.1 1.5 %shard_map.97.stats = f32[16,256]{1,0:T(8,128)S(1)} custom-call(s32[64]{0:T(128)S(1)} %copy-done.7, bf16[320,384]{1,0:T(8,128)(2,1)S(1)} %get-tuple-element.24.qg, bf16[256,384]{1,0:T(8,128)(2,1)S(1)} %get-tuple-element.30.kv, bf16[256,384]{1,0:T(8,128)(2,1)S(1)} %get-tuple-element.31.kvp), custom_call_target="tpu_custom_call" | custom-call | tf_op jit(solution)/shard_map/pallas_call | solution.py:506
  30.6 1.5 %all-to-all-done.rows.rows1 = bf16[8,80,384]{2,1,0:T(8,128)(2,1)S(1)} async-done(((bf16[8,80,384]{2,1,0:T(8,128)(2,1)}), bf16[8,80,384]{2,1,0:T(8,128)(2,1)S(1)}, u32[]{:S(2)}, u32[]{:S(2)}) %all-to-all-start) | async-done | bytes 491552 | tf_op jit(solution)/shard_map/all_to_all | solution.py:540
  32.1 1.7 %shard_map.98 = bf16[80,384]{1,0:T(8,128)(2,1)S(1)} custom-call(s32[2,16]{1,0:T(2,128)S(1)} %copy-done.6, s32[64]{0:T(128)S(1)} %copy-done.7, bf16[320,384]{1,0:T(8,128)(2,1)S(1)} %get-tuple-element.24.qg, bf16[16,384]{1,0:T(8,128)(2,1)S(1)} %get-tuple-element.25.qg_top, bf16[8,80,384]{2,1,0:T(8,128)(2,1)S(1)} %all-to-all-done.rows.rows1, ...), custom_call_target="tpu_custom_call" | custom-call | tf_op jit(solution)/shard_map/pallas_call | solution.py:506
  33.7 0.7 collective-permute-start.2
  34.4 1.0 %shard_map.99 = bf16[8,128,384]{2,1,0:T(8,128)(2,1)} custom-call(bf16[8,80,384]{2,1,0:T(8,128)(2,1)S(1)} %all-to-all-done.rows.rows1), custom_call_target="tpu_custom_call" | custom-call | tf_op jit(solution)/shard_map/pallas_call | solution.py:506
  35.4 0.0 collective-permute-done.3.qgp
  35.4 2.7 %collective-permute-done.2 = bf16[80,384]{1,0:T(8,128)(2,1)S(1)} collective-permute-done((bf16[80,384]{1,0:T(8,128)(2,1)S(1)}, bf16[80,384]{1,0:T(8,128)(2,1)S(1)}, u32[]{:S(2)}, u32[]{:S(2)}) %collective-permute-start.2) | collective-permute-done | bytes 61472 | tf_op jit(solution)/shard_map/ppermute | solution.py:534
  38.0 5.9 %all-to-all-start.1 = ((bf16[8,128,384]{2,1,0:T(8,128)(2,1)}), bf16[8,128,384]{2,1,0:T(8,128)(2,1)S(1)}, u32[]{:S(2)}, u32[]{:S(2)}) async-start(bf16[8,128,384]{2,1,0:T(8,128)(2,1)} %shard_map.99), calls=%async_computation.1 | async-start | bytes 1572864 | tf_op jit(solution)/shard_map/all_to_all | solution.py:540
  44.0 1.2 %collective-permute-start.4 = (bf16[64,384]{1,0:T(8,128)(2,1)S(1)}, bf16[64,384]{1,0:T(8,128)(2,1)S(1)}, u32[]{:S(2)}, u32[]{:S(2)}) collective-permute-start(bf16[64,384]{1,0:T(8,128)(2,1)S(1)} %pad_maximum_fusion.1), channel_id=1, source_target_pairs={{0,8},{4,12},{8,16},{12,20},{16,24},{20,28},{24,0},{28,4},{32,40},... | collective-permute-start | bytes 147464 | tf_op jit(solution)/shard_map/ppermute | solution.py:537
  45.2 2.9 %collective-permute-start.5 = (bf16[64,384]{1,0:T(8,128)(2,1)S(1)}, bf16[64,384]{1,0:T(8,128)(2,1)S(1)}, u32[]{:S(2)}, u32[]{:S(2)}) collective-permute-start(bf16[64,384]{1,0:T(8,128)(2,1)S(1)} %pad_maximum_fusion.1), channel_id=1, source_target_pairs={{0,16},{4,20},{8,24},{12,28},{16,0},{20,4},{24,8},{28,12},{32,48},... | collective-permute-start | bytes 147464 | tf_op jit(solution)/shard_map/ppermute | solution.py:537
  48.1 3.6 %collective-permute-start.6 = (bf16[64,384]{1,0:T(8,128)(2,1)S(1)}, bf16[64,384]{1,0:T(8,128)(2,1)S(1)}, u32[]{:S(2)}, u32[]{:S(2)}) collective-permute-start(bf16[64,384]{1,0:T(8,128)(2,1)S(1)} %pad_maximum_fusion.1), channel_id=1, source_target_pairs={{0,24},{4,28},{8,0},{12,4},{16,8},{20,12},{24,16},{28,20},{32,56},... | collective-permute-start | bytes 147464 | tf_op jit(solution)/shard_map/ppermute | solution.py:537
  51.7 0.0 collective-permute-done.4
  51.7 1.5 %collective-permute-done.5 = bf16[64,384]{1,0:T(8,128)(2,1)S(1)} collective-permute-done((bf16[64,384]{1,0:T(8,128)(2,1)S(1)}, bf16[64,384]{1,0:T(8,128)(2,1)S(1)}, u32[]{:S(2)}, u32[]{:S(2)}) %collective-permute-start.5) | collective-permute-done | bytes 49184 | tf_op jit(solution)/shard_map/ppermute | solution.py:537
  53.2 1.0 %collective-permute-done.6 = bf16[64,384]{1,0:T(8,128)(2,1)S(1)} collective-permute-done((bf16[64,384]{1,0:T(8,128)(2,1)S(1)}, bf16[64,384]{1,0:T(8,128)(2,1)S(1)}, u32[]{:S(2)}, u32[]{:S(2)}) %collective-permute-start.6) | collective-permute-done | bytes 49184 | tf_op jit(solution)/shard_map/ppermute | solution.py:537
  54.3 0.0 all-to-all-done.1.rows.rows2
  54.3 2.8 %shard_map.100 = (bf16[512,128]{1,0:T(8,128)(2,1)S(1)}, bf16[640,128]{1,0:T(8,128)(2,1)S(1)}, bf16[8,128,512]{2,1,0:T(8,128)(2,1)S(1)}) custom-call(s32[2,16]{1,0:T(2,128)S(1)} %copy-done.6, s32[64]{0:T(128)S(1)} %copy-done.7, bf16[352,384]{1,0:T(8,128)(2,1)S(1)} %constant_dynamic-update-slice_fusion.tails, bf16[8,128,384]{2,1,0:T(8,128)(2,1)S(1)} %all-to-all-done.1.rows.rows2), custom_call_target="tpu_custom_call" | custom-call | tf_op jit(solution)/shard_map/pallas_call | solution.py:506
  57.0 0.0 copy-start
  57.0 1.0 %copy-done = bf16[8,128,512]{2,1,0:T(8,128)(2,1)} copy-done((bf16[8,128,512]{2,1,0:T(8,128)(2,1)}, bf16[8,128,512]{2,1,0:T(8,128)(2,1)S(1)}, u32[]{:S(2)}) %copy-start) | copy-done | bytes 1048600
  58.0 5.7 %all-to-all-start.2 = ((bf16[8,128,512]{2,1,0:T(8,128)(2,1)}), bf16[8,128,512]{2,1,0:T(8,128)(2,1)S(1)}, u32[]{:S(2)}, u32[]{:S(2)}) async-start(bf16[8,128,512]{2,1,0:T(8,128)(2,1)} %copy-done), calls=%async_computation.2 | async-start | bytes 2097152 | tf_op jit(solution)/shard_map/all_to_all | solution.py:540
  63.8 3.3 %collective-permute-start.7 = (bf16[128,384]{1,0:T(8,128)(2,1)S(1)}, bf16[128,384]{1,0:T(8,128)(2,1)S(1)}, u32[]{:S(2)}, u32[]{:S(2)}) collective-permute-start(bf16[128,384]{1,0:T(8,128)(2,1)S(1)} %pad_maximum_fusion.near), channel_id=1, source_target_pairs={{0,8},{4,12},{8,16},{12,20},{16,24},{20,28},{24,0},{28,4},{32,40},... | collective-permute-start | bytes 294920 | tf_op jit(solution)/shard_map/ppermute | solution.py:537
  67.1 3.3 %collective-permute-start.8 = (bf16[128,384]{1,0:T(8,128)(2,1)S(1)}, bf16[128,384]{1,0:T(8,128)(2,1)S(1)}, u32[]{:S(2)}, u32[]{:S(2)}) collective-permute-start(bf16[128,384]{1,0:T(8,128)(2,1)S(1)} %pad_maximum_fusion.near), channel_id=1, source_target_pairs={{0,16},{4,20},{8,24},{12,28},{16,0},{20,4},{24,8},{28,12},{32,48},... | collective-permute-start | bytes 294920 | tf_op jit(solution)/shard_map/ppermute | solution.py:537
  70.4 1.1 %collective-permute-start.9 = (bf16[128,384]{1,0:T(8,128)(2,1)S(1)}, bf16[128,384]{1,0:T(8,128)(2,1)S(1)}, u32[]{:S(2)}, u32[]{:S(2)}) collective-permute-start(bf16[128,384]{1,0:T(8,128)(2,1)S(1)} %pad_maximum_fusion.near), channel_id=1, source_target_pairs={{0,24},{4,28},{8,0},{12,4},{16,8},{20,12},{24,16},{28,20},{32,56},... | collective-permute-start | bytes 294920 | tf_op jit(solution)/shard_map/ppermute | solution.py:537
  71.5 1.8 %shard_map.102.level0 = f32[256,384]{1,0:T(8,128)S(1)} custom-call(s32[64]{0:T(128)S(1)} %copy-done.7, bf16[256,384]{1,0:T(8,128)(2,1)S(1)} %get-tuple-element.30.kv, bf16[320,384]{1,0:T(8,128)(2,1)S(1)} %get-tuple-element.24.qg, bf16[640,128]{1,0:T(8,128)(2,1)S(1)} %get-tuple-element.39.st, bf16[320,384]{1,0:T(8,128)(2,1)S(1)} %collective-permute-done.3.qgp), custom_call_target="tpu_custom_call" | custom-call | tf_op jit(solution)/shard_map/pallas_call | solution.py:506
  73.4 0.0 copy-start.4
  73.4 3.4 %shard_map.101 = bf16[128,384]{1,0:T(8,128)(2,1)} custom-call(s32[2,16]{1,0:T(2,128)S(1)} %copy-done.6, s32[64]{0:T(128)S(1)} %copy-done.7, bf16[320,384]{1,0:T(8,128)(2,1)S(1)} %get-tuple-element.24.qg, bf16[16,384]{1,0:T(8,128)(2,1)S(1)} %get-tuple-element.25.qg_top, bf16[512,128]{1,0:T(8,128)(2,1)S(1)} %get-tuple-element.38.st1, ...), custom_call_target="tpu_custom_call" | custom-call | tf_op jit(solution)/shard_map/pallas_call | solution.py:506
  76.8 0.0 collective-permute-done.7.far2
  76.8 0.8 collective-permute-done.8.far4
  77.6 0.5 collective-permute-done.9.far6
  78.1 0.0 copy-done.4
  78.1 1.4 %shard_map.103.early = f32[256,384]{1,0:T(8,128)S(1)} custom-call(s32[2,16]{1,0:T(2,128)S(1)} %copy-done.6, s32[64]{0:T(128)S(1)} %copy-done.7, bf16[80,384]{1,0:T(8,128)(2,1)S(1)} %copy-done.4, bf16[128,384]{1,0:T(8,128)(2,1)S(1)} %pad_maximum_fusion.near, bf16[128,384]{1,0:T(8,128)(2,1)S(1)} %collective-permute-done.7.far2, ...), custom_call_target="tpu_custom_call" | custom-call | tf_op jit(solution)/shard_map/pallas_call | solution.py:506
  79.4 0.0 all-to-all-done.2.all_qg
  79.5 2.3 %shard_map.104 = (bf16[128,384]{1,0:T(8,128)(2,1)}, bf16[128,384]{1,0:T(8,128)(2,1)}) custom-call(s32[2,16]{1,0:T(2,128)S(1)} %copy-done.6, s32[64]{0:T(128)S(1)} %copy-done.7, bf16[80,384]{1,0:T(8,128)(2,1)S(1)} %copy-done.4, bf16[8,128,512]{2,1,0:T(8,128)(2,1)S(1)} %all-to-all-done.2.all_qg, f32[256,384]{1,0:T(8,128)S(1)} %shard_map.103.early), custom_call_target="tpu_custom_call" | custom-call | tf_op jit(solution)/shard_map/pallas_call | solution.py:506
  (11 shorter events, 0.1 us)
Async XLA Ops:
  0.6 5.7 %collective-permute-start = (bf16[128,384]{1,0:T(8,128)(2,1)}, bf16[128,384]{1,0:T(8,128)(2,1)S(1)}, u32[]{:S(2)}, u32[]{:S(2)}) collective-permute-start(bf16[128,384]{1,0:T(8,128)(2,1)} %k.1), channel_id=1, source_target_pairs={{0,4},{4,0},{8,12},{12,8},{16,20},{20,16},{24,28},{28,24},{32,36},... | collective-permute-start | bytes 294920 | tf_op jit(solution)/shard_map/ppermute | solution.py:534
  2.6 5.1 %collective-permute-start.1 = (bf16[128,384]{1,0:T(8,128)(2,1)}, bf16[128,384]{1,0:T(8,128)(2,1)S(1)}, u32[]{:S(2)}, u32[]{:S(2)}) collective-permute-start(bf16[128,384]{1,0:T(8,128)(2,1)} %v.1), channel_id=1, source_target_pairs={{0,4},{4,0},{8,12},{12,8},{16,20},{20,16},{24,28},{28,24},{32,36},... | collective-permute-start | bytes 294920 | tf_op jit(solution)/shard_map/ppermute | solution.py:534
  7.7 8.4 %copy-start.8 = (bf16[128,384]{1,0:T(8,128)(2,1)S(1)}, bf16[128,384]{1,0:T(8,128)(2,1)}, u32[]{:S(2)}) copy-start(bf16[128,384]{1,0:T(8,128)(2,1)} %param.10) | copy-start | bytes 294916
  7.8 24.3 %all-to-all-start = ((bf16[8,80,384]{2,1,0:T(8,128)(2,1)}), bf16[8,80,384]{2,1,0:T(8,128)(2,1)S(1)}, u32[]{:S(2)}, u32[]{:S(2)}) async-start(bf16[8,80,384]{2,1,0:T(8,128)(2,1)} %get-tuple-element.27), calls=%async_computation | async-start | bytes 983040 | tf_op jit(solution)/shard_map/all_to_all | solution.py:540
  16.2 8.3 %copy-start.3 = (bf16[192,768]{1,0:T(8,128)(2,1)S(1)}, bf16[192,768]{1,0:T(8,128)(2,1)}, u32[]{:S(2)}) copy-start(bf16[192,768]{1,0:T(8,128)(2,1)} %w.1) | copy-start | bytes 884740
  16.2 8.3 %copy-start.5 = (bf16[128,384]{1,0:T(8,128)(2,1)S(1)}, bf16[128,384]{1,0:T(8,128)(2,1)}, u32[]{:S(2)}) copy-start(bf16[128,384]{1,0:T(8,128)(2,1)} %q.1) | copy-start | bytes 294916
  24.5 0.7 copy-start.6
  24.5 0.7 copy-start.7
  25.2 3.5 %copy-start.1 = (bf16[128,384]{1,0:T(8,128)(2,1)S(1)}, bf16[128,384]{1,0:T(8,128)(2,1)}, u32[]{:S(2)}) copy-start(bf16[128,384]{1,0:T(8,128)(2,1)} %k.1) | copy-start | bytes 294916
  25.2 3.5 %copy-start.2 = (bf16[128,384]{1,0:T(8,128)(2,1)S(1)}, bf16[128,384]{1,0:T(8,128)(2,1)}, u32[]{:S(2)}) copy-start(bf16[128,384]{1,0:T(8,128)(2,1)} %v.1) | copy-start | bytes 294916
  26.6 8.8 %collective-permute-start.3 = (bf16[320,384]{1,0:T(8,128)(2,1)S(1)}, bf16[320,384]{1,0:T(8,128)(2,1)S(1)}, u32[]{:S(2)}, u32[]{:S(2)}) collective-permute-start(bf16[320,384]{1,0:T(8,128)(2,1)S(1)} %get-tuple-element.24.qg), channel_id=1, source_target_pairs={{0,4},{4,0},{8,12},{12,8},{16,20},{20,16},{24,28},{28,24},{32,36},... | collective-permute-start | bytes 737288 | tf_op jit(solution)/shard_map/ppermute | solution.py:534
  33.7 4.3 %collective-permute-start.2 = (bf16[80,384]{1,0:T(8,128)(2,1)S(1)}, bf16[80,384]{1,0:T(8,128)(2,1)S(1)}, u32[]{:S(2)}, u32[]{:S(2)}) collective-permute-start(bf16[80,384]{1,0:T(8,128)(2,1)S(1)} %shard_map.98), channel_id=1, source_target_pairs={{0,4},{4,0},{8,12},{12,8},{16,20},{20,16},{24,28},{28,24},{32,36},... | collective-permute-start | bytes 184328 | tf_op jit(solution)/shard_map/ppermute | solution.py:534
  38.0 16.2 %all-to-all-start.1 = ((bf16[8,128,384]{2,1,0:T(8,128)(2,1)}), bf16[8,128,384]{2,1,0:T(8,128)(2,1)S(1)}, u32[]{:S(2)}, u32[]{:S(2)}) async-start(bf16[8,128,384]{2,1,0:T(8,128)(2,1)} %shard_map.99), calls=%async_computation.1 | async-start | bytes 1572864 | tf_op jit(solution)/shard_map/all_to_all | solution.py:540
  44.0 7.7 %collective-permute-start.4 = (bf16[64,384]{1,0:T(8,128)(2,1)S(1)}, bf16[64,384]{1,0:T(8,128)(2,1)S(1)}, u32[]{:S(2)}, u32[]{:S(2)}) collective-permute-start(bf16[64,384]{1,0:T(8,128)(2,1)S(1)} %pad_maximum_fusion.1), channel_id=1, source_target_pairs={{0,8},{4,12},{8,16},{12,20},{16,24},{20,28},{24,0},{28,4},{32,40},... | collective-permute-start | bytes 147464 | tf_op jit(solution)/shard_map/ppermute | solution.py:537
  45.2 8.0 %collective-permute-start.5 = (bf16[64,384]{1,0:T(8,128)(2,1)S(1)}, bf16[64,384]{1,0:T(8,128)(2,1)S(1)}, u32[]{:S(2)}, u32[]{:S(2)}) collective-permute-start(bf16[64,384]{1,0:T(8,128)(2,1)S(1)} %pad_maximum_fusion.1), channel_id=1, source_target_pairs={{0,16},{4,20},{8,24},{12,28},{16,0},{20,4},{24,8},{28,12},{32,48},... | collective-permute-start | bytes 147464 | tf_op jit(solution)/shard_map/ppermute | solution.py:537
  48.1 6.1 %collective-permute-start.6 = (bf16[64,384]{1,0:T(8,128)(2,1)S(1)}, bf16[64,384]{1,0:T(8,128)(2,1)S(1)}, u32[]{:S(2)}, u32[]{:S(2)}) collective-permute-start(bf16[64,384]{1,0:T(8,128)(2,1)S(1)} %pad_maximum_fusion.1), channel_id=1, source_target_pairs={{0,24},{4,28},{8,0},{12,4},{16,8},{20,12},{24,16},{28,20},{32,56},... | collective-permute-start | bytes 147464 | tf_op jit(solution)/shard_map/ppermute | solution.py:537
  57.0 1.0 %copy-start = (bf16[8,128,512]{2,1,0:T(8,128)(2,1)}, bf16[8,128,512]{2,1,0:T(8,128)(2,1)S(1)}, u32[]{:S(2)}) copy-start(bf16[8,128,512]{2,1,0:T(8,128)(2,1)S(1)} %get-tuple-element.41) | copy-start | bytes 3145732
  58.0 21.4 %all-to-all-start.2 = ((bf16[8,128,512]{2,1,0:T(8,128)(2,1)}), bf16[8,128,512]{2,1,0:T(8,128)(2,1)S(1)}, u32[]{:S(2)}, u32[]{:S(2)}) async-start(bf16[8,128,512]{2,1,0:T(8,128)(2,1)} %copy-done), calls=%async_computation.2 | async-start | bytes 2097152 | tf_op jit(solution)/shard_map/all_to_all | solution.py:540
  63.8 13.0 %collective-permute-start.7 = (bf16[128,384]{1,0:T(8,128)(2,1)S(1)}, bf16[128,384]{1,0:T(8,128)(2,1)S(1)}, u32[]{:S(2)}, u32[]{:S(2)}) collective-permute-start(bf16[128,384]{1,0:T(8,128)(2,1)S(1)} %pad_maximum_fusion.near), channel_id=1, source_target_pairs={{0,8},{4,12},{8,16},{12,20},{16,24},{20,28},{24,0},{28,4},{32,40},... | collective-permute-start | bytes 294920 | tf_op jit(solution)/shard_map/ppermute | solution.py:537
  67.1 10.5 %collective-permute-start.8 = (bf16[128,384]{1,0:T(8,128)(2,1)S(1)}, bf16[128,384]{1,0:T(8,128)(2,1)S(1)}, u32[]{:S(2)}, u32[]{:S(2)}) collective-permute-start(bf16[128,384]{1,0:T(8,128)(2,1)S(1)} %pad_maximum_fusion.near), channel_id=1, source_target_pairs={{0,16},{4,20},{8,24},{12,28},{16,0},{20,4},{24,8},{28,12},{32,48},... | collective-permute-start | bytes 294920 | tf_op jit(solution)/shard_map/ppermute | solution.py:537
  70.4 7.7 %collective-permute-start.9 = (bf16[128,384]{1,0:T(8,128)(2,1)S(1)}, bf16[128,384]{1,0:T(8,128)(2,1)S(1)}, u32[]{:S(2)}, u32[]{:S(2)}) collective-permute-start(bf16[128,384]{1,0:T(8,128)(2,1)S(1)} %pad_maximum_fusion.near), channel_id=1, source_target_pairs={{0,24},{4,28},{8,0},{12,4},{16,8},{20,12},{24,16},{28,20},{32,56},... | collective-permute-start | bytes 294920 | tf_op jit(solution)/shard_map/ppermute | solution.py:537
  73.4 4.7 %copy-start.4 = (bf16[80,384]{1,0:T(8,128)(2,1)S(1)}, bf16[80,384]{1,0:T(8,128)(2,1)}, u32[]{:S(2)}) copy-start(bf16[80,384]{1,0:T(8,128)(2,1)} %get-tuple-element.40.own) | copy-start | bytes 184324
